TPU v7x, 32 devices: a whole 2x2x4 slice. The times are simulated.
32 devices in a mesh: ctx: 8 (over z, x), tp: 2 (over y), pp: 2 (over core).
Axes of the slice: x: 2, y: 2, z: 4, core: 2. Of those that a mesh axis runs over, the one named last changes fastest.
Arguments:
- features: bfloat16 [2, 2048, 3, 8192], P('pp', 'ctx', None, 'tp'), may hold values from -6 to 6
- short_taps: float32 [2, 3, 3, 8192], P('pp', None, None, 'tp'), may hold values from -3 to 3
- long_filters: bfloat16 [2, 128, 512], P('pp', None, 'tp'), may hold values from -0.5 to 0.5
- out_weight: bfloat16 [2, 8192, 4096], P('pp', 'tp', 'ctx'), may hold values from -0.09375 to 0.09375
- out_grad: bfloat16 [2, 2048, 4096], P('pp', 'ctx', 'tp'), may hold values from -6 to 6
Outputs:
- received_adjoint: bfloat16 [2, 2048, 3, 8192], P('pp', 'ctx', None, 'tp')
All inputs are finite; a program needn't handle non-finite values.
Results may differ from a plain program's by a relative error of at most 0.013.
Values may be sent and summed in bfloat16 or wider, within the bound.
A program may use at most 192 MiB of HBM per device.

v0:
```python
import jax
import jax.numpy as jnp
from jax import lax
from jax.sharding import PartitionSpec as P


def from_behind(block, axis, distance):
    devices = range(lax.axis_size(axis))
    route = [(i - distance, i) for i in devices if i - distance in devices]
    return lax.ppermute(block, axis, route)


def from_behind_2(shard, axis, by):
    peers = lax.axis_size(axis)
    return lax.ppermute(shard, axis, [(i, (i + by) % peers) for i in range(peers)])


def short_conv(extended, short_taps):
    ext_f = extended.astype(jnp.float32)
    return short_taps[0] * ext_f[2:] + short_taps[1] * ext_f[1:-1] + short_taps[2] * ext_f[:-2]


def bands(filters):
    filter_len = filters.shape[0]
    by_group = jnp.transpose(filters)
    zero_band = jnp.zeros((), filters.dtype)
    rows_f = lax.broadcasted_iota(jnp.int32, (filter_len, 2 * filter_len), 0)
    cols_f = lax.broadcasted_iota(jnp.int32, (filter_len, 2 * filter_len), 1)
    lag_f = rows_f - cols_f + filter_len
    valid_f = (lag_f >= 0) & (lag_f < filter_len)
    forward_band = jnp.where(
        valid_f[None], jnp.take(by_group, jnp.clip(lag_f, 0, filter_len - 1), axis=1), zero_band
    )
    rows_b = lax.broadcasted_iota(jnp.int32, (2 * filter_len, filter_len), 0)
    cols_b = lax.broadcasted_iota(jnp.int32, (2 * filter_len, filter_len), 1)
    lag_b = rows_b - cols_b
    valid_b = (lag_b >= 0) & (lag_b < filter_len)
    backward_band = jnp.where(
        valid_b[None], jnp.take(by_group, jnp.clip(lag_b, 0, filter_len - 1), axis=1), zero_band
    )
    return (forward_band, backward_band)


def local(features, short_taps, long_filters, out_weight, out_grad):
    feats = features[0]
    taps_local = short_taps[0]
    filters = long_filters[0]
    weight = out_weight[0]
    cotangent = out_grad[0]
    row_count = feats.shape[0]
    channels = feats.shape[2]
    filter_len = filters.shape[0]
    groups = filters.shape[1]
    group_width = channels // groups
    blocks = row_count // filter_len
    forward_band, backward_band = bands(filters)
    rim_rows = from_behind(feats[row_count - filter_len - 1 :], "ctx", 1)
    mixed = short_conv(jnp.concatenate([rim_rows, feats], axis=0), taps_local)
    products = (mixed[:, 1] * mixed[:, 2]).astype(jnp.bfloat16)
    own_mix = mixed[filter_len - 1 :]
    gate_part = own_mix[:, 0]
    key_part = own_mix[:, 1]
    value_part = own_mix[:, 2]
    prod_ext = jnp.concatenate([jnp.zeros((1, channels), jnp.bfloat16), products], axis=0)
    prod_blocks = prod_ext.reshape(blocks + 1, filter_len, groups, group_width)
    prod_window = jnp.concatenate([prod_blocks[:-1], prod_blocks[1:]], axis=1)
    conv_out = jnp.einsum(
        "bugw,gtu->bgwt", prod_window, forward_band, preferred_element_type=jnp.float32
    )
    conv_out = jnp.transpose(conv_out, (0, 3, 1, 2)).reshape(row_count, channels)
    cot_full = lax.all_gather(cotangent, "tp", axis=1, tiled=True)
    weight_full = lax.all_gather(weight, "ctx", axis=1, tiled=True)
    grad_y = jnp.einsum(
        "tn,cn->tc", cot_full, weight_full, preferred_element_type=jnp.float32
    ).astype(jnp.bfloat16)
    grad_yf = grad_y.astype(jnp.float32)
    grad_gate = grad_yf * conv_out
    grad_conv = (grad_yf * gate_part).astype(jnp.bfloat16)
    conv_window = (
        grad_conv[: filter_len + 1].astype(jnp.float32).reshape(filter_len + 1, groups, group_width)
    )
    filt_f = filters.astype(jnp.float32)
    head_first = jnp.einsum("jg,jgw->gw", filt_f, conv_window[:filter_len]).reshape(1, channels)
    head_second = jnp.einsum("jg,jgw->gw", filt_f, conv_window[1:]).reshape(1, channels)
    head_prod_grad = jnp.concatenate([head_first, head_second], axis=0)
    head_grad = jnp.stack(
        [grad_gate[:2], head_prod_grad * value_part[:2], head_prod_grad * key_part[:2]], axis=1
    ).astype(jnp.bfloat16)
    conv_next, mix_next = from_behind((grad_conv[: filter_len - 1], head_grad), "ctx", -1)
    conv_ext = jnp.concatenate(
        [grad_conv, conv_next, jnp.zeros((1, channels), jnp.bfloat16)], axis=0
    )
    conv_blocks = conv_ext.reshape(blocks + 1, filter_len, groups, group_width)
    conv_pair = jnp.concatenate([conv_blocks[:-1], conv_blocks[1:]], axis=1)
    grad_prod = jnp.einsum(
        "bugw,gut->bgwt", conv_pair, backward_band, preferred_element_type=jnp.float32
    )
    grad_prod = jnp.transpose(grad_prod, (0, 3, 1, 2)).reshape(row_count, channels)
    grad_mix = jnp.stack([grad_gate, grad_prod * value_part, grad_prod * key_part], axis=1).astype(
        jnp.bfloat16
    )
    mix_ext = jnp.concatenate([grad_mix, mix_next], axis=0).astype(jnp.float32)
    grad_feat = (
        taps_local[0] * mix_ext[:row_count]
        + taps_local[1] * mix_ext[1 : row_count + 1]
        + taps_local[2] * mix_ext[2:]
    )
    grad_feat = grad_feat.astype(jnp.bfloat16)
    passed = from_behind_2(grad_feat, "pp", -1)
    return passed[None]


def solution(mesh):
    in_specs = (
        P("pp", "ctx", None, "tp"),
        P("pp", None, None, "tp"),
        P("pp", None, "tp"),
        P("pp", "tp", "ctx"),
        P("pp", "ctx", "tp"),
    )
    out_specs = P("pp", "ctx", None, "tp")
    return jax.shard_map(local, mesh=mesh, in_specs=in_specs, out_specs=out_specs, check_vma=False)
```

profile of v0, /device:TPU:0, one launch (start us, length us, event | category | flops | bytes accessed | tf_op | source)
XLA Modules:
  0.0 840.3 jit_solution(135080060727757560)
XLA Ops:
  6.5 0.7 all-gather.5.cloned.1.call-update
  7.3 0.7 all-gather.7.cloned.1.call-update
  8.0 4.6 slice_bitcast_fusion.1
  12.6 5.0 collective-permute-start
  17.7 0.6 fusion.55
  18.5 0.7 broadcast_clamp_fusion
  19.1 139.1 %gather_fusion = bf16[32768,256]{1,0:T(8,128)(2,1)} fusion(bf16[256,128]{0,1:T(8,128)(2,1)S(1)} %bitcast.96, s32[32768]{0:T(1024)} %broadcast_clamp_fusion), kind=kCustom, calls=%fused_computation | custom fusion | bytes 33685504 | tf_op jit(solution)/shard_map/jit(_take)/gather | solution.py:32
  158.2 23.2 %copy.14 = bf16[128,256,256]{1,0,2:T(8,128)(2,1)} copy(bf16[128,256,256]{2,1,0:T(8,128)(2,1)} %bitcast.99) | data formatting | bytes 33554432 | tf_op jit(solution)/shard_map/jit(_take)/gather | solution.py:32
  181.5 0.6 slice.157
  182.1 0.7 fusion.35
  182.8 139.1 %gather_fusion.1 = bf16[32768,256]{1,0:T(8,128)(2,1)} fusion(bf16[256,128]{0,1:T(8,128)(2,1)S(1)} %bitcast.97, s32[32768]{0:T(1024)} %fusion.35), kind=kCustom, calls=%fused_computation.1 | custom fusion | bytes 33685504 | tf_op jit(solution)/shard_map/jit(_take)/gather | solution.py:39
  321.8 22.2 %copy.21 = bf16[256,128,256]{1,0,2:T(8,128)(2,1)} copy(bf16[256,128,256]{2,1,0:T(8,128)(2,1)} %bitcast.100) | data formatting | bytes 33554432 | tf_op jit(solution)/shard_map/jit(_take)/gather | solution.py:39
  344.1 0.8 copy.33
  344.8 0.7 fusion.44
  345.6 0.7 fusion.45
  346.3 0.9 copy_bitcast_fusion.1
  347.2 5.1 maximum_convert_fusion
  352.3 9.0 %fusion.2 = f32[383,3,4096]{2,0,1:T(8,128)} fusion(f32[385,3,4096]{2,0,1:T(8,128)S(1)} %maximum_convert_fusion, f32[3,4096]{1,0:T(4,128)S(1)} %get-tuple-element.16, f32[3,4096]{1,0:T(4,128)S(1)} %get-tuple-element.17, f32[3,4096]{1,0:T(4,128)S(1)} %bitcast.112), kind=kLoop, calls=%fused_computation.5 | loop fusion | flops 23531520 | bytes 75448320 | tf_op jit(solution)/shard_map/add | solution.py:20
  361.3 5.4 fusion.64
  366.8 0.5 pad_slice_fusion
  367.3 2.5 copy.15
  369.7 2.5 slice.125
  372.3 1.6 copy.17
  373.9 5.4 fusion.23
  379.3 0.5 slice.154
  379.8 2.5 copy.16
  382.3 2.5 slice.127
  384.8 0.3 copy.18
  385.1 2.2 pad_maximum_fusion
  387.4 9.5 %fusion.6 = f32[256,128,32]{1,2,0:S(1)} fusion(bf16[256,256,32]{1,2,0:T(8,128)(2,1)S(1)} %bitcast.105, bf16[128,256,256]{1,0,2:T(8,128)(2,1)} %copy.14, pred[128,256]{1,0:T(8,128)(4,1)S(1)} %copy-done.9, pred[128,256]{1,0:T(8,128)(4,1)S(1)} %copy-done.8), kind=kOutput, calls=%fused_computation.11 | convolution fusion | flops 553648128 | bytes 25231360
  396.9 2.2 copy.19
  399.1 2.3 copy.45
  401.4 5.7 copy.20
  407.0 311.5 %all-gather.7.cloned.1.call-done = bf16[1,4096,4096]{2,1,0:T(8,128)(2,1)} async-done(((bf16[1,4096,512]{2,1,0:T(8,128)(2,1)}), bf16[1,4096,4096]{2,1,0:T(8,128)(2,1)}) %all-gather.7.cloned.1.call-update) | async-done | bytes 33554448 | tf_op jit(solution)/shard_map/all_gather | solution.py:72
  718.5 18.7 %fusion.27 = (bf16[256,4096]{1,0:T(8,128)(2,1)}, bf16[256,4096]{1,0:T(8,128)(2,1)S(1)}) fusion(f32[256,4096]{1,0:T(8,128)} %copy.20, f32[383,3,4096]{2,0,1:T(8,128)} %fusion.2, bf16[1,4096,4096]{2,1,0:T(8,128)(2,1)} %all-gather.7.cloned.1.call-done, bf16[1,256,4096]{2,1,0:T(8,128)(2,1)} %all-gather.5.cloned.1.call-done), kind=kOutput, calls=%fused_computation.38 | convolution fusion | flops 8596226048 | bytes 48234496 | tf_op jit(solution)/shard_map/tn,cn->tc/dot_general | solution.py:73
  737.3 1.1 slice.156
  738.4 2.4 copy.22
  740.8 1.2 fusion.54
  742.0 1.4 collective-permute-start.1
  743.5 4.0 slice.129
  747.4 3.2 copy.24
  750.6 2.3 copy.29
  752.9 1.9 fusion.56
  754.7 0.1 concatenate.32
  754.9 1.3 copy.30
  756.2 1.9 fusion.57
  758.2 1.1 fusion.49
  759.3 0.9 slice_bitcast_fusion.2
  760.2 1.3 collective-permute-start.2
  761.5 9.7 %collective-permute-done.1 = bf16[127,4096]{1,0:T(8,128)(2,1)} collective-permute-done((bf16[127,4096]{1,0:T(8,128)(2,1)}, bf16[127,4096]{1,0:T(8,128)(2,1)}, u32[]{:S(2)}, u32[]{:S(2)}) %collective-permute-start.1) | collective-permute-done | bytes 1040416 | tf_op jit(solution)/shard_map/ppermute | solution.py:10
  771.2 3.1 fusion.31
  774.3 3.3 copy.23
  777.6 2.0 slice.132
  779.6 1.9 copy.25
  781.5 2.2 pad_maximum_fusion.1
  783.8 8.5 %fusion.4 = f32[256,128,32]{1,2,0:S(1)} fusion(bf16[256,256,32]{1,2,0:T(8,128)(2,1)S(1)} %bitcast.106, bf16[256,128,256]{1,0,2:T(8,128)(2,1)} %copy.21, pred[256,128]{1,0:T(8,128)(4,1)S(1)} %copy-done.7, pred[256,128]{1,0:T(8,128)(4,1)S(1)} %copy-done.6), kind=kOutput, calls=%fused_computation.9 | convolution fusion | flops 553648128 | bytes 25231360
  792.3 4.2 copy.26
  796.5 6.4 reshape.123
  802.9 5.6 copy.27
  808.5 6.4 fusion.30
  814.9 1.6 maximum_convert_fusion.1
  816.6 3.9 fusion.17
  820.6 10.1 %collective-permute-done.3 = bf16[256,3,4096]{2,0,1:T(8,128)(2,1)S(1)} collective-permute-done((bf16[256,3,4096]{2,0,1:T(8,128)(2,1)S(1)}, bf16[256,3,4096]{2,0,1:T(8,128)(2,1)S(1)}, u32[]{:S(2)}, u32[]{:S(2)}) %collective-permute-start.3) | collective-permute-done | bytes 6291488 | tf_op jit(solution)/shard_map/ppermute | solution.py:15
  830.7 2.7 copy.48
  (32 shorter events, 0.6 us)
Async XLA Ops:
  6.5 11.1 %copy-start.4 = (f32[1,3,3,4096]{3,0,2,1:T(1,128)S(1)}, f32[1,3,3,4096]{3,0,2,1:T(1,128)}, u32[]{:S(2)}) copy-start(f32[1,3,3,4096]{3,0,2,1:T(1,128)} %param.6) | copy-start | bytes 442372
  6.5 12.6 %copy-start = (bf16[1,128,256]{2,1,0:T(8,128)(2,1)S(1)}, bf16[1,128,256]{2,1,0:T(8,128)(2,1)}, u32[]{:S(2)}) copy-start(bf16[1,128,256]{2,1,0:T(8,128)(2,1)} %param.7) | copy-start | bytes 196612
  6.5 400.5 %all-gather.5.cloned.1.call-start = ((), (), s32[]{:S(2)}) async-start(), calls=%async_computation | async-start | bytes 3145728 | tf_op jit(solution)/shard_map/all_gather | solution.py:71
  7.3 711.3 %all-gather.7.cloned.1.call-start = ((), (), s32[]{:S(2)}) async-start(), calls=%async_computation.1 | async-start | bytes 37748736 | tf_op jit(solution)/shard_map/all_gather | solution.py:72
  12.6 334.6 %collective-permute-start = (bf16[129,3,4096]{2,0,1:T(8,128)(2,1)}, bf16[129,3,4096]{2,0,1:T(8,128)(2,1)S(1)}, u32[]{:S(2)}, u32[]{:S(2)}) collective-permute-start(bf16[129,3,4096]{2,0,1:T(8,128)(2,1)} %slice_bitcast_fusion.1), channel_id=1, source_target_pairs={{0,4},{4,8},{8,12},{12,16},{16,20},{20,24},{24,28},{1,5},{5,9},{9,... | collective-permute-start | bytes 9510920 | tf_op jit(solution)/shard_map/ppermute | solution.py:10
  347.2 5.1 copy-start.2
  384.8 2.5 copy-start.8
  384.8 2.5 copy-start.9
  742.0 10.8 %copy-start.5 = (bf16[128,256,1]{0,2,1:T(2,128)(2,1)S(1)}, bf16[128,256,1]{0,2,1:T(2,128)(2,1)}, u32[]{:S(2)}) copy-start(bf16[128,256,1]{0,2,1:T(2,128)(2,1)} %copy.33) | copy-start | bytes 196612
  742.0 29.2 %collective-permute-start.1 = (bf16[127,4096]{1,0:T(8,128)(2,1)}, bf16[127,4096]{1,0:T(8,128)(2,1)}, u32[]{:S(2)}, u32[]{:S(2)}) collective-permute-start(bf16[127,4096]{1,0:T(8,128)(2,1)} %slice.156), channel_id=1, source_target_pairs={{4,0},{8,4},{12,8},{16,12},{20,16},{24,20},{28,24},{5,1},{9,5},{13... | collective-permute-start | bytes 3121160 | tf_op jit(solution)/shard_map/ppermute | solution.py:10
  760.2 54.7 %collective-permute-start.2 = (bf16[2,3,4096]{2,0,1:T(2,128)(2,1)S(1)}, bf16[2,3,4096]{2,0,1:T(2,128)(2,1)S(1)}, u32[]{:S(2)}, u32[]{:S(2)}) collective-permute-start(bf16[2,3,4096]{2,0,1:T(2,128)(2,1)S(1)} %pad_maximum_fusion.3), channel_id=1, source_target_pairs={{4,0},{8,4},{12,8},{16,12},{20,16},{24,20},{28,24},{5,1},{9,5},{13... | collective-permute-start | bytes 147464 | tf_op jit(solution)/shard_map/ppermute | solution.py:10
  779.6 4.1 copy-start.6
  779.6 4.1 copy-start.7
  808.5 6.4 copy-start.1
  814.9 1.7 copy-start.3
  820.5 10.2 %collective-permute-start.3 = (bf16[256,3,4096]{2,0,1:T(8,128)(2,1)S(1)}, bf16[256,3,4096]{2,0,1:T(8,128)(2,1)S(1)}, u32[]{:S(2)}, u32[]{:S(2)}) collective-permute-start(bf16[256,3,4096]{2,0,1:T(8,128)(2,1)S(1)} %fusion.17), channel_id=1, source_target_pairs={{0,1},{1,0},{2,3},{3,2},{4,5},{5,4},{6,7},{7,6},{8,9},{9,8},{10,11... | collective-permute-start | bytes 18874376 | tf_op jit(solution)/shard_map/ppermute | solution.py:15
Sparse Core Ops, SparseCore 0:
  8.9 35.8 all-gather.4
  46.3 672.2 all-gather.6
where the time goes:
time: 848 us; the launch traced here: 840 us
  local copies, waits for them, and re-layouts  397 us (47%)
  waiting for transfers between devices  333 us (39%)
  other arithmetic  48.6 us (6%)
  matrix products  40.5 us (5%)
  between operations  13.8 us (2%)
    all_gather x1, waiting for transfers between devices, local(): weight_full = lax.all_gather(weight, 'ctx', axis=1, tiled=True)  312 us
    gather x2, local copies, waits for them, and re-layouts, bands(): jnp.take(by_group, jnp.clip(lag_f, 0, filter_len - 1), axis=1)  162 us
    gather x2, local copies, waits for them, and re-layouts, bands(): jnp.take(by_group, jnp.clip(lag_b, 0, filter_len - 1), axis=1)  161 us
    dot_general x1, matrix products, local(): jnp.einsum('tn,cn->tc', cot_full, weight_full, preferred_element_type=jnp...  18.7 us
    unnamed x2, matrix products  18.1 us
  transfers between devices with their start and end apart: 6, of which 3 were waited for; matrix products, arithmetic and copies ran while one was open for 54% of the time, Pallas kernels for 0%

commit v1 on v0

v1 whole, which is shorter than its diff:
```python
import functools

import jax
import jax.numpy as jnp
from jax import lax
from jax.experimental import pallas as pl
from jax.experimental.pallas import tpu as pltpu
from jax.sharding import PartitionSpec as P

LANES = 128
TAIL = 8
CHUNKS = 4
F32 = jnp.float32
BF16 = jnp.bfloat16


def split_of(count):
    inner = 1
    while inner * inner * 4 <= count:
        inner *= 2
    return count // inner, inner


def ahead(block, axis, distance):
    devices = range(lax.axis_size(axis))
    return lax.ppermute(block, axis, [(i - distance, i) for i in devices if i - distance in devices])


def toeplitz(row, rows, shift):
    wide = jnp.broadcast_to(row, (rows, row.shape[1]))
    return pltpu.roll(wide, shift, 1, stride=1, stride_axis=0).astype(BF16)


def group_conv(filter_rows, windows, shift, group_width, tail=None):
    taps = windows.shape[0] // 2
    lane = lax.broadcasted_iota(jnp.int32, (1, 2 * LANES), 1) % LANES // group_width
    total = jnp.zeros((taps, 2 * LANES), F32)
    end = None if tail is None else jnp.zeros((TAIL, LANES), F32)
    for g in range(LANES // group_width):
        band = toeplitz(filter_rows[g : g + 1, :], taps, shift)
        part = jnp.dot(band, windows, preferred_element_type=F32)
        total = jnp.where(lane == g, part, total)
        if tail is not None:
            part = jnp.dot(band[:16], tail, preferred_element_type=F32)[:TAIL]
            end = jnp.where(lane[:, :LANES] == g, part, end)
    joined = jnp.concatenate([total[:, :LANES], total[:, LANES:]], axis=0)
    return joined if tail is None else (joined, end)


def forward_kernel(group_width, feat_ref, taps_ref, filt_ref, halo_ref, conv_ref, mix_ref):
    rows = conv_ref.shape[0]
    taps = halo_ref.shape[0]
    pad = feat_ref.shape[1] - rows
    per = LANES // group_width
    for tile in range(conv_ref.shape[1] // LANES):
        cols = slice(tile * LANES, (tile + 1) * LANES)
        mixed = []
        for i in range(3):
            ext = feat_ref[i, :, cols].astype(F32)
            mixed.append(
                taps_ref[0, i : i + 1, cols] * ext[pad:]
                + taps_ref[1, i : i + 1, cols] * pltpu.roll(ext, 1, 0)[pad:]
                + taps_ref[2, i : i + 1, cols] * pltpu.roll(ext, 2, 0)[pad:]
            )
            mix_ref[i, :, cols] = mixed[i]
        products = (mixed[1] * mixed[2]).astype(BF16)
        whole = jnp.concatenate([halo_ref[:, cols], products], axis=0)
        windows = jnp.concatenate([whole[: 2 * taps], whole[taps : 3 * taps]], axis=1)
        conv_ref[:, cols] = group_conv(filt_ref[tile * per : (tile + 1) * per, :], windows, 1, group_width)


def backward_kernel(group_width, gc_ref, halo_ref, gg_ref, mix_ref, next_ref, taps_ref, filt_ref, out_ref):
    rows = gc_ref.shape[0]
    taps = filt_ref.shape[1] // 2
    held = halo_ref.shape[0]
    per = LANES // group_width
    for tile in range(gc_ref.shape[1] // LANES):
        cols = slice(tile * LANES, (tile + 1) * LANES)
        halo = halo_ref[:, cols]
        own = gc_ref[:, cols]
        last = jnp.concatenate([halo, jnp.zeros((2 * taps - held, LANES), BF16)], axis=0)
        windows = jnp.concatenate(
            [own, jnp.concatenate([own[taps:], halo[:taps]], axis=0)], axis=1
        )
        prod, prod_end = group_conv(filt_ref[tile * per : (tile + 1) * per, :], windows, 0, group_width, last)
        ends = (
            halo.astype(F32)[held - TAIL :],
            prod_end * next_ref[1, :, cols],
            prod_end * next_ref[0, :, cols],
        )
        bodies = (gg_ref[:, cols].astype(F32), prod * mix_ref[2, :, cols], prod * mix_ref[1, :, cols])
        for i in range(3):
            ext = jnp.concatenate([bodies[i], ends[i]], axis=0).astype(BF16).astype(F32)
            size = rows + TAIL
            out_ref[i, :, cols] = (
                taps_ref[0, i : i + 1, cols] * ext[:rows]
                + taps_ref[1, i : i + 1, cols] * pltpu.roll(ext, size - 1, 0)[:rows]
                + taps_ref[2, i : i + 1, cols] * pltpu.roll(ext, size - 2, 0)[:rows]
            ).astype(BF16)


def tiled(kernel, operands, outs, channels, group_width, flops, wide=512):
    wide = min(wide, channels)

    def spec(shape, by_group):
        if by_group:
            return pl.BlockSpec((wide // group_width,) + shape[1:], lambda c: (c, 0))
        lead = len(shape) - 1
        return pl.BlockSpec(shape[:-1] + (wide,), lambda c: (0,) * lead + (c,))

    moved = sum(a.size * a.dtype.itemsize for a, _ in operands) + sum(4 * o.size for o in outs)
    return pl.pallas_call(
        functools.partial(kernel, group_width),
        grid=(channels // wide,),
        in_specs=[spec(a.shape, by_group) for a, by_group in operands],
        out_specs=[spec(o.shape, False) for o in outs],
        out_shape=outs,
        compiler_params=pltpu.CompilerParams(vmem_limit_bytes=48 * 1024 * 1024),
        cost_estimate=pl.CostEstimate(flops=flops, bytes_accessed=moved, transcendentals=0),
    )(*[a for a, _ in operands])


def local(features, short_taps, long_filters, out_weight, out_grad):
    feats, taps, filters = features[0], short_taps[0], long_filters[0]
    weight, cotangent = out_weight[0], out_grad[0]
    rows, _, channels = feats.shape
    reach, groups = filters.shape
    width = channels // groups
    outer, inner = split_of(lax.axis_size("ctx"))
    place = lax.axis_index("ctx")
    z, x = place // inner, place % inner
    tp_count, tp_place = lax.axis_size("tp"), lax.axis_index("tp")
    chunks = max(1, min(CHUNKS, channels // 512))
    piece = channels // chunks
    own_depth = weight.shape[1]
    depth = inner * own_depth

    full = jnp.zeros((rows, tp_count * cotangent.shape[1]), cotangent.dtype)
    full = lax.dynamic_update_slice(full, cotangent, (0, tp_place * cotangent.shape[1]))
    for s in range(1, tp_count):
        got = lax.ppermute(cotangent, "tp", [(i, (i + s) % tp_count) for i in range(tp_count)])
        full = lax.dynamic_update_slice(full, got, (0, (tp_place - s) % tp_count * cotangent.shape[1]))
    tokens = jnp.zeros((outer, rows, depth), cotangent.dtype)
    for s in range(outer):
        block = lax.dynamic_slice(full, (0, (z + s) % outer * depth), (rows, depth))
        if s:
            route = [
                (zz * inner + xx, (zz + s) % outer * inner + xx) for zz in range(outer) for xx in range(inner)
            ]
            block = lax.ppermute(block, "ctx", route)
        tokens = lax.dynamic_update_slice(tokens, block[None], ((z - s) % outer, 0, 0))
    tokens = tokens.reshape(outer * rows, inner, own_depth)
    order = [(x - s) % inner for s in range(inner)]
    tokens = jnp.concatenate(
        [lax.dynamic_slice_in_dim(tokens, o, 1, 1)[:, 0] for o in order], axis=1
    )

    tail_f = feats[rows - reach - 2 :].astype(F32)
    tail_mix = taps[0] * tail_f[2:] + taps[1] * tail_f[1:-1] + taps[2] * tail_f[:-2]
    prod_halo = ahead((tail_mix[:, 1] * tail_mix[:, 2]).astype(BF16), "ctx", 1)
    feat_halo = ahead(feats[rows - 2 :], "ctx", 1)
    ext = jnp.concatenate([jnp.zeros((14, 3, channels), BF16), feat_halo, feats], axis=0)
    ext = jnp.transpose(ext, (1, 0, 2))
    by_group = jnp.transpose(filters).astype(F32)
    blank = jnp.zeros((groups, reach), F32)
    backward_rows = jnp.concatenate([by_group, blank], axis=1)
    forward_rows = jnp.concatenate([by_group[:, ::-1], blank], axis=1)
    flops = 2 * groups * reach * 4 * reach * LANES
    conv, mix = tiled(
        forward_kernel,
        [(ext, False), (taps, False), (forward_rows, True), (prod_halo, False)],
        [jax.ShapeDtypeStruct((rows, channels), F32), jax.ShapeDtypeStruct((3, rows, channels), F32)],
        channels,
        width,
        flops,
    )
    next_mix = ahead(mix[1:, :TAIL], "ctx", -1)

    results = []
    for k in range(chunks):
        lo, hi = k * piece, (k + 1) * piece
        mine = weight[lo:hi]
        held = [mine]
        for s in range(1, inner):
            route = [
                (zz * inner + xx, zz * inner + (xx + s) % inner) for zz in range(outer) for xx in range(inner)
            ]
            held.append(lax.ppermute(mine, "ctx", route))
        joined = jnp.concatenate(held, axis=1)
        partial = jnp.einsum("tn,cn->tc", tokens, joined, preferred_element_type=F32).astype(BF16)
        partial = partial.reshape(outer, rows, piece)

        def part_for(d):
            return lax.dynamic_index_in_dim(partial, jnp.clip(d, 0, outer - 1), 0, False).astype(F32)

        grad_y = part_for(z)
        for sign in (1, -1):
            got = None
            for j in range(outer - 1):
                send = part_for(z + sign * (outer - 1 - j))
                if got is not None:
                    send = send + got.astype(F32)
                sources = range(j + 1) if sign == 1 else range(outer - 1 - j, outer)
                route = [(zz * inner + xx, (zz + sign) * inner + xx) for zz in sources for xx in range(inner)]
                got = lax.ppermute(send.astype(BF16), "ctx", route)
            grad_y = grad_y + got.astype(F32)
        grad_y = grad_y.astype(BF16).astype(F32)
        grad_gate = (grad_y * conv[:, lo:hi]).astype(BF16)
        grad_conv = (grad_y * mix[0, :, lo:hi]).astype(BF16)
        halo = ahead(jnp.concatenate([grad_conv[: reach + 8], grad_gate[:TAIL]], axis=0), "ctx", -1)
        (out,) = tiled(
            backward_kernel,
            [
                (grad_conv, False),
                (halo, False),
                (grad_gate, False),
                (mix[:, :, lo:hi], False),
                (next_mix[:, :, lo:hi], False),
                (taps[:, :, lo:hi], False),
                (backward_rows[lo // width : hi // width], True),
            ],
            [jax.ShapeDtypeStruct((3, rows, piece), BF16)],
            piece,
            width,
            flops // chunks,
        )
        count = lax.axis_size("pp")
        results.append(lax.ppermute(out, "pp", [(i, (i - 1) % count) for i in range(count)]))
    return jnp.transpose(jnp.concatenate(results, axis=2), (1, 0, 2))[None]


def solution(mesh):
    in_specs = (
        P("pp", "ctx", None, "tp"),
        P("pp", None, None, "tp"),
        P("pp", None, "tp"),
        P("pp", "tp", "ctx"),
        P("pp", "ctx", "tp"),
    )
    out_specs = P("pp", "ctx", None, "tp")
    return jax.shard_map(local, mesh=mesh, in_specs=in_specs, out_specs=out_specs, check_vma=False)
```

time: 848 us -> 339 us (0.40)
  local copies, waits for them, and re-layouts: 397 us -> 41.7 us
  waiting for transfers between devices: 333 us -> 91.2 us
  starting transfers between devices: 7.86 us -> 115 us
  Pallas kernels: 0 us -> 36.7 us
  matrix products: 40.5 us -> 15.3 us
  other arithmetic: 48.6 us -> 30.7 us
  between operations: 13.8 us -> 1.7 us
    gather x4 -> x0, local copies, waits for them, and re-layouts: 324 us -> none  [the longest x2 162 us: bands(): jnp.take(by_group, jnp.clip(lag_f, 0, filter_len - 1), axis=1)]
    all_gather x2 -> x0, waiting for transfers between devices: 312 us -> none  [the longest x1 312 us: local(): weight_full = lax.all_gather(weight, 'ctx', axis=1, tiled=True)]
    ppermute x4 -> x43, starting transfers between devices: 7.82 us -> 115 us  [the longest x24 81.9 us: local(): got = lax.ppermute(send.astype(BF16), 'ctx', route)]
    ppermute x4 -> x43, waiting for transfers between devices: 19.8 us -> 91.2 us  [the longest x24 65.8 us: local(): got = lax.ppermute(send.astype(BF16), 'ctx', route)]
    pallas_call x0 -> x5, Pallas kernels: none -> 36.7 us  [tiled(): pl.pallas_call(functools.partial(kernel, group_width), grid=(channels //...]
    slice x20 -> x16, local copies, waits for them, and re-layouts: 38.9 us -> 15.1 us  [the longest x1 10.9 us: local(): mix[:, :, lo:hi]]
    unnamed x2 -> x0, matrix products: 18.1 us -> none
    reshape x3 -> x1, local copies, waits for them, and re-layouts: 17.6 us -> 4.51 us  [local(): tokens = tokens.reshape(outer * rows, inner, own_depth)]
  transfers between devices with their start and end apart: 6 -> 43, of which waited for: 3 -> 17; matrix products, arithmetic and copies ran while one was open for 54% -> 23% of each run, Pallas kernels for 0% -> 11%
where the time goes in v1:
time: 339 us; the launch traced here: 332 us
  starting transfers between devices  115 us (34%)
  waiting for transfers between devices  91.2 us (27%)
  local copies, waits for them, and re-layouts  41.7 us (12%)
  Pallas kernels  36.7 us (11%)
  other arithmetic  30.7 us (9%)
  matrix products  15.3 us (5%)
    ppermute x24, starting transfers between devices, local(): got = lax.ppermute(send.astype(BF16), 'ctx', route)  81.9 us
    ppermute x24, waiting for transfers between devices, local(): got = lax.ppermute(send.astype(BF16), 'ctx', route)  65.8 us
    pallas_call x5, Pallas kernels, tiled(): pl.pallas_call(functools.partial(kernel, group_width), grid=(channels //...  36.7 us
    dot_general x4, matrix products, local(): jnp.einsum('tn,cn->tc', tokens, joined, preferred_element_type=F32)  15.3 us
    ppermute x7, starting transfers between devices, ahead(): lax.ppermute(block, axis, [(i - distance, i) for i in devices if i - dist...  15.2 us
    ppermute x3, starting transfers between devices, local(): block = lax.ppermute(block, 'ctx', route)  10.9 us
    slice x1, local copies, waits for them, and re-layouts, local(): mix[:, :, lo:hi]  10.9 us
    ppermute x1, waiting for transfers between devices, local(): lax.ppermute(cotangent, 'tp', [(i, (i + s) % tp_count) for i in range(tp_...  9.65 us
  transfers between devices with their start and end apart: 43, of which 17 were waited for; matrix products, arithmetic and copies ran while one was open for 23% of the time, Pallas kernels for 11%

profile of v1, /device:TPU:0, one launch (start us, length us, event | category | flops | bytes accessed | tf_op | source)
XLA Modules:
  0.0 332.2 jit_solution(14033807660844162436)
XLA Ops:
  1.0 5.0 %collective-permute-start.11 = (bf16[2,3,4096]{2,0,1:T(2,128)(2,1)S(1)}, bf16[2,3,4096]{2,0,1:T(2,128)(2,1)S(1)}, u32[]{:S(2)}, u32[]{:S(2)}) collective-permute-start(bf16[2,3,4096]{2,0,1:T(2,128)(2,1)S(1)} %slice_bitcast_fusion.7), channel_id=1, source_target_pairs={{0,4},{4,8},{8,12},{12,16},{16,20},{20,24},{24,28},{1,5},{5,9},{9,... | collective-permute-start | bytes 147464 | tf_op jit(solution)/shard_map/ppermute | solution.py:26
  6.0 2.9 slice_convert_fusion
  9.0 1.9 fusion.1
  11.2 3.8 %collective-permute-start.12 = (bf16[128,4096]{1,0:T(8,128)(2,1)S(1)}, bf16[128,4096]{1,0:T(8,128)(2,1)S(1)}, u32[]{:S(2)}, u32[]{:S(2)}) collective-permute-start(bf16[128,4096]{1,0:T(8,128)(2,1)S(1)} %fusion.42), channel_id=1, source_target_pairs={{0,4},{4,8},{8,12},{12,16},{16,20},{20,24},{24,28},{1,5},{5,9},{9,... | collective-permute-start | bytes 3145736 | tf_op jit(solution)/shard_map/ppermute | solution.py:26
  15.0 2.1 slice_bitcast_fusion.6
  17.1 1.4 collective-permute-start.4
  18.5 1.5 collective-permute-start
  20.9 1.6 broadcast_in_dim.26
  22.5 2.3 constant_dynamic-update-slice_fusion.1
  25.4 7.8 %maximum_bitcast_fusion.feat_ref = bf16[3,272,4096]{2,1,0:T(8,128)(2,1)} fusion(bf16[256,3,4096]{2,0,1:T(8,128)(2,1)} %bitcast.162, bf16[2,3,4096]{2,0,1:T(2,128)(2,1)S(1)} %collective-permute-done.11, bf16[272]{0:T(512)(128)(2,1)S(1)} %pad.20.clone), kind=kLoop, calls=%fused_computation | loop fusion | flops 20054016 | bytes 13025824 | tf_op jit(solution)/shard_map/transpose | solution.py:163
  33.2 9.7 %collective-permute-done = bf16[256,2048]{1,0:T(8,128)(2,1)} collective-permute-done((bf16[256,2048]{1,0:T(8,128)(2,1)}, bf16[256,2048]{1,0:T(8,128)(2,1)}, u32[]{:S(2)}, u32[]{:S(2)}) %collective-permute-start) | collective-permute-done | bytes 1048608 | tf_op jit(solution)/shard_map/ppermute | solution.py:141
  42.9 2.3 constant_dynamic-update-slice_fusion
  45.2 1.5 constant_dynamic-slice_fusion.2
  46.7 1.6 collective-permute-start.1
  48.3 3.4 %collective-permute-start.2 = (bf16[256,1024]{1,0:T(8,128)(2,1)S(1)}, bf16[256,1024]{1,0:T(8,128)(2,1)S(1)}, u32[]{:S(2)}, u32[]{:S(2)}) collective-permute-start(bf16[256,1024]{1,0:T(8,128)(2,1)S(1)} %get-tuple-element.54), channel_id=1, source_target_pairs={{0,16},{4,20},{8,24},{12,28},{16,0},{20,4},{24,8},{28,12},{1,17},{... | collective-permute-start | bytes 1572872 | tf_op jit(solution)/shard_map/ppermute | solution.py:150
  51.7 5.9 %collective-permute-start.3 = (bf16[256,1024]{1,0:T(8,128)(2,1)S(1)}, bf16[256,1024]{1,0:T(8,128)(2,1)S(1)}, u32[]{:S(2)}, u32[]{:S(2)}) collective-permute-start(bf16[256,1024]{1,0:T(8,128)(2,1)S(1)} %get-tuple-element.53), channel_id=1, source_target_pairs={{0,24},{4,28},{8,0},{12,4},{16,8},{20,12},{24,16},{28,20},{1,25},{... | collective-permute-start | bytes 1572872 | tf_op jit(solution)/shard_map/ppermute | solution.py:150
  57.6 15.6 %shard_map.55 = (f32[256,4096]{1,0:T(8,128)S(1)}, f32[3,256,4096]{2,1,0:T(8,128)}) custom-call(bf16[3,272,4096]{2,1,0:T(8,128)(2,1)} %maximum_bitcast_fusion.feat_ref, f32[3,3,4096]{2,1,0:T(4,128)S(1)} %bitcast.161, f32[256,256]{1,0:T(8,128)S(1)} %concatenate.42.filt_ref, bf16[128,4096]{1,0:T(8,128)(2,1)S(1)} %collective-permute-done.12.halo_ref), custom_call_target="tpu_custom_call" | custom-call | flops 4294967296 | bytes 24920064 | tf_op jit(solution)/shard_map/pallas_call | solution.py:112
  73.2 1.6 broadcast_in_dim.25
  74.7 2.3 bitcast_dynamic-update-slice_fusion.3
  78.0 1.9 collective-permute-start.25
  80.8 2.2 collective-permute-done.2
  85.2 4.5 %reshape.75 = bf16[1024,2,512]{2,1,0:T(2,128)(2,1)} reshape(bf16[4,256,1024]{2,1,0:T(8,128)(2,1)} %bitcast_dynamic-update-slice_fusion) | data formatting | bytes 4194304 | tf_op jit(solution)/shard_map/reshape | solution.py:152
  89.8 6.5 %constant_dynamic-slice_fusion.1 = (bf16[1024,1,512]{2,1,0:T(2,128)(2,1)S(1)}, bf16[1024,1,512]{2,1,0:T(2,128)(2,1)S(1)}) fusion(bf16[1024,2,512]{2,1,0:T(2,128)(2,1)} %reshape.75, s32[]{:T(128)S(6)} %select_n.139, s32[]{:T(128)S(6)} %select_n.141), kind=kLoop, calls=%fused_computation.128 | loop fusion | bytes 4194312 | tf_op jit(solution)/shard_map/dynamic_slice | solution.py:155
  96.9 3.9 %fusion.31 = bf16[1024,1024]{1,0:T(8,128)(2,1)S(1)} fusion(bf16[1024,512]{1,0:T(8,128)(2,1)} %collective-permute-done.4, bf16[1024,512]{1,0:T(8,128)(2,1)} %get-tuple-element.31, bf16[1024,512]{1,0:T(8,128)(2,1)S(1)} %get-tuple-element.73, bf16[1024,512]{1,0:T(8,128)(2,1)S(1)} %get-tuple-element.74), kind=kOutput, calls=%fused_computation.33 | convolution fusion | flops 2156920832 | bytes 6291456 | tf_op jit(solution)/shard_map/tn,cn->tc/dot_general | solution.py:190
  100.9 12.3 %collective-permute-start.5 = (bf16[256,1024]{1,0:T(8,128)(2,1)S(1)}, bf16[256,1024]{1,0:T(8,128)(2,1)S(1)}, u32[]{:S(2)}, u32[]{:S(2)}) collective-permute-start(bf16[256,1024]{1,0:T(8,128)(2,1)S(1)} %get-tuple-element.37), channel_id=1, source_target_pairs={{0,8},{4,12},{1,9},{5,13},{2,10},{6,14},{3,11},{7,15}} | collective-permute-start | bytes 1572872 | tf_op jit(solution)/shard_map/ppermute | solution.py:205
  113.9 3.9 %fusion.22 = bf16[1024,1024]{1,0:T(8,128)(2,1)S(1)} fusion(bf16[1024,512]{1,0:T(8,128)(2,1)} %collective-permute-done.34, bf16[1024,512]{1,0:T(8,128)(2,1)} %get-tuple-element.33, bf16[1024,512]{1,0:T(8,128)(2,1)S(1)} %get-tuple-element.73, bf16[1024,512]{1,0:T(8,128)(2,1)S(1)} %get-tuple-element.74), kind=kOutput, calls=%fused_computation.30 | convolution fusion | flops 2156920832 | bytes 6291456 | tf_op jit(solution)/shard_map/tn,cn->tc/dot_general | solution.py:190
  117.9 1.3 collective-permute-start.35
  120.1 3.9 %fusion.25 = bf16[1024,1024]{1,0:T(8,128)(2,1)S(1)} fusion(bf16[1024,512]{1,0:T(8,128)(2,1)} %collective-permute-done.25, bf16[1024,512]{1,0:T(8,128)(2,1)} %get-tuple-element.34, bf16[1024,512]{1,0:T(8,128)(2,1)S(1)} %get-tuple-element.73, bf16[1024,512]{1,0:T(8,128)(2,1)S(1)} %get-tuple-element.74), kind=kOutput, calls=%fused_computation.31 | convolution fusion | flops 2156920832 | bytes 6291456 | tf_op jit(solution)/shard_map/tn,cn->tc/dot_general | solution.py:190
  124.2 2.8 collective-permute-done.16
  126.9 5.4 %collective-permute-start.26 = (bf16[256,1024]{1,0:T(8,128)(2,1)S(1)}, bf16[256,1024]{1,0:T(8,128)(2,1)S(1)}, u32[]{:S(2)}, u32[]{:S(2)}) collective-permute-start(bf16[256,1024]{1,0:T(8,128)(2,1)S(1)} %get-tuple-element.45), channel_id=1, source_target_pairs={{0,8},{4,12},{1,9},{5,13},{2,10},{6,14},{3,11},{7,15}} | collective-permute-start | bytes 1572872 | tf_op jit(solution)/shard_map/ppermute | solution.py:205
  132.4 3.6 %fusion.28 = bf16[1024,1024]{1,0:T(8,128)(2,1)S(1)} fusion(bf16[1024,512]{1,0:T(8,128)(2,1)} %collective-permute-done.16, bf16[1024,512]{1,0:T(8,128)(2,1)S(1)} %copy-done.7, bf16[1024,512]{1,0:T(8,128)(2,1)S(1)} %get-tuple-element.73, bf16[1024,512]{1,0:T(8,128)(2,1)S(1)} %get-tuple-element.74), kind=kOutput, calls=%fused_computation.32 | convolution fusion | flops 2156920832 | bytes 6291456 | tf_op jit(solution)/shard_map/tn,cn->tc/dot_general | solution.py:190
  136.1 1.3 collective-permute-start.17
  137.6 3.5 %collective-permute-start.6 = (bf16[256,1024]{1,0:T(8,128)(2,1)S(1)}, bf16[256,1024]{1,0:T(8,128)(2,1)S(1)}, u32[]{:S(2)}, u32[]{:S(2)}) collective-permute-start(bf16[256,1024]{1,0:T(8,128)(2,1)S(1)} %fusion.63), channel_id=1, source_target_pairs={{0,8},{4,12},{8,16},{12,20},{1,9},{5,13},{9,17},{13,21},{2,10},{6,... | collective-permute-start | bytes 1572872 | tf_op jit(solution)/shard_map/ppermute | solution.py:205
  141.3 6.6 %collective-permute-done.26 = bf16[256,1024]{1,0:T(8,128)(2,1)S(1)} collective-permute-done((bf16[256,1024]{1,0:T(8,128)(2,1)S(1)}, bf16[256,1024]{1,0:T(8,128)(2,1)S(1)}, u32[]{:S(2)}, u32[]{:S(2)}) %collective-permute-start.26) | collective-permute-done | bytes 524320 | tf_op jit(solution)/shard_map/ppermute | solution.py:205
  148.8 10.3 %collective-permute-done.17 = bf16[256,1024]{1,0:T(8,128)(2,1)S(1)} collective-permute-done((bf16[256,1024]{1,0:T(8,128)(2,1)S(1)}, bf16[256,1024]{1,0:T(8,128)(2,1)S(1)}, u32[]{:S(2)}, u32[]{:S(2)}) %collective-permute-start.17) | collective-permute-done | bytes 524320 | tf_op jit(solution)/shard_map/ppermute | solution.py:205
  159.1 4.4 %collective-permute-start.36 = (bf16[256,1024]{1,0:T(8,128)(2,1)S(1)}, bf16[256,1024]{1,0:T(8,128)(2,1)S(1)}, u32[]{:S(2)}, u32[]{:S(2)}) collective-permute-start(bf16[256,1024]{1,0:T(8,128)(2,1)S(1)} %fusion.45), channel_id=1, source_target_pairs={{0,8},{4,12},{8,16},{12,20},{1,9},{5,13},{9,17},{13,21},{2,10},{6,... | collective-permute-start | bytes 1572872 | tf_op jit(solution)/shard_map/ppermute | solution.py:205
  164.5 5.9 %collective-permute-done.6 = bf16[256,1024]{1,0:T(8,128)(2,1)S(1)} collective-permute-done((bf16[256,1024]{1,0:T(8,128)(2,1)S(1)}, bf16[256,1024]{1,0:T(8,128)(2,1)S(1)}, u32[]{:S(2)}, u32[]{:S(2)}) %collective-permute-start.6) | collective-permute-done | bytes 524320 | tf_op jit(solution)/shard_map/ppermute | solution.py:205
  170.4 4.4 %collective-permute-start.27 = (bf16[256,1024]{1,0:T(8,128)(2,1)S(1)}, bf16[256,1024]{1,0:T(8,128)(2,1)S(1)}, u32[]{:S(2)}, u32[]{:S(2)}) collective-permute-start(bf16[256,1024]{1,0:T(8,128)(2,1)S(1)} %fusion.51), channel_id=1, source_target_pairs={{0,8},{4,12},{8,16},{12,20},{1,9},{5,13},{9,17},{13,21},{2,10},{6,... | collective-permute-start | bytes 1572872 | tf_op jit(solution)/shard_map/ppermute | solution.py:205
  175.2 1.9 collective-permute-start.18
  177.1 4.5 %collective-permute-done.36 = bf16[256,1024]{1,0:T(8,128)(2,1)S(1)} collective-permute-done((bf16[256,1024]{1,0:T(8,128)(2,1)S(1)}, bf16[256,1024]{1,0:T(8,128)(2,1)S(1)}, u32[]{:S(2)}, u32[]{:S(2)}) %collective-permute-start.36) | collective-permute-done | bytes 524320 | tf_op jit(solution)/shard_map/ppermute | solution.py:205
  182.7 5.0 %collective-permute-start.7 = (bf16[256,1024]{1,0:T(8,128)(2,1)S(1)}, bf16[256,1024]{1,0:T(8,128)(2,1)S(1)}, u32[]{:S(2)}, u32[]{:S(2)}) collective-permute-start(bf16[256,1024]{1,0:T(8,128)(2,1)S(1)} %get-tuple-element.35), channel_id=1, source_target_pairs={{0,8},{4,12},{8,16},{12,20},{16,24},{20,28},{1,9},{5,13},{9,17},{1... | collective-permute-start | bytes 1572872 | tf_op jit(solution)/shard_map/ppermute | solution.py:205
  187.7 5.1 %collective-permute-done.27 = bf16[256,1024]{1,0:T(8,128)(2,1)S(1)} collective-permute-done((bf16[256,1024]{1,0:T(8,128)(2,1)S(1)}, bf16[256,1024]{1,0:T(8,128)(2,1)S(1)}, u32[]{:S(2)}, u32[]{:S(2)}) %collective-permute-start.27) | collective-permute-done | bytes 524320 | tf_op jit(solution)/shard_map/ppermute | solution.py:205
  193.9 5.0 %collective-permute-start.37 = (bf16[256,1024]{1,0:T(8,128)(2,1)S(1)}, bf16[256,1024]{1,0:T(8,128)(2,1)S(1)}, u32[]{:S(2)}, u32[]{:S(2)}) collective-permute-start(bf16[256,1024]{1,0:T(8,128)(2,1)S(1)} %get-tuple-element.47), channel_id=1, source_target_pairs={{0,8},{4,12},{8,16},{12,20},{16,24},{20,28},{1,9},{5,13},{9,17},{1... | collective-permute-start | bytes 1572872 | tf_op jit(solution)/shard_map/ppermute | solution.py:205
  199.0 5.1 %collective-permute-done.18 = bf16[256,1024]{1,0:T(8,128)(2,1)S(1)} collective-permute-done((bf16[256,1024]{1,0:T(8,128)(2,1)S(1)}, bf16[256,1024]{1,0:T(8,128)(2,1)S(1)}, u32[]{:S(2)}, u32[]{:S(2)}) %collective-permute-start.18) | collective-permute-done | bytes 524320 | tf_op jit(solution)/shard_map/ppermute | solution.py:205
  207.8 5.6 %collective-permute-start.28 = (bf16[256,1024]{1,0:T(8,128)(2,1)S(1)}, bf16[256,1024]{1,0:T(8,128)(2,1)S(1)}, u32[]{:S(2)}, u32[]{:S(2)}) collective-permute-start(bf16[256,1024]{1,0:T(8,128)(2,1)S(1)} %get-tuple-element.43), channel_id=1, source_target_pairs={{0,8},{4,12},{8,16},{12,20},{16,24},{20,28},{1,9},{5,13},{9,17},{1... | collective-permute-start | bytes 1572872 | tf_op jit(solution)/shard_map/ppermute | solution.py:205
  216.7 20.6 %collective-permute-start.19 = (bf16[256,1024]{1,0:T(8,128)(2,1)}, bf16[256,1024]{1,0:T(8,128)(2,1)}, u32[]{:S(2)}, u32[]{:S(2)}) collective-permute-start(bf16[256,1024]{1,0:T(8,128)(2,1)} %get-tuple-element.39), channel_id=1, source_target_pairs={{0,8},{4,12},{8,16},{12,20},{16,24},{20,28},{1,9},{5,13},{9,17},{1... | collective-permute-start | bytes 1572872 | tf_op jit(solution)/shard_map/ppermute | solution.py:205
  239.5 1.3 collective-permute-start.40
  240.9 1.3 collective-permute-start.31
  242.2 1.5 collective-permute-start.22
  243.8 10.9 %fusion.75 = (f32[3,256,1024]{2,1,0:T(8,128)}, f32[3,256,1024]{2,1,0:T(8,128)}, f32[3,256,1024]{2,1,0:T(8,128)}, f32[3,256,1024]{2,1,0:T(8,128)}) fusion(f32[3,256,4096]{2,1,0:T(8,128)} %get-tuple-element.7), kind=kLoop, calls=%fused_computation.138 | loop fusion | bytes 25165824 | tf_op jit(solution)/shard_map/slice | solution.py:217
  255.3 11.2 %collective-permute-done.40 = bf16[256,1024]{1,0:T(8,128)(2,1)} collective-permute-done((bf16[256,1024]{1,0:T(8,128)(2,1)}, bf16[256,1024]{1,0:T(8,128)(2,1)}, u32[]{:S(2)}, u32[]{:S(2)}) %collective-permute-start.40) | collective-permute-done | bytes 524320 | tf_op jit(solution)/shard_map/ppermute | solution.py:205
  266.5 10.7 %collective-permute-done.31 = bf16[256,1024]{1,0:T(8,128)(2,1)} collective-permute-done((bf16[256,1024]{1,0:T(8,128)(2,1)}, bf16[256,1024]{1,0:T(8,128)(2,1)}, u32[]{:S(2)}, u32[]{:S(2)}) %collective-permute-start.31) | collective-permute-done | bytes 524320 | tf_op jit(solution)/shard_map/ppermute | solution.py:205
  277.2 5.6 %collective-permute-done.22 = bf16[256,1024]{1,0:T(8,128)(2,1)} collective-permute-done((bf16[256,1024]{1,0:T(8,128)(2,1)}, bf16[256,1024]{1,0:T(8,128)(2,1)}, u32[]{:S(2)}, u32[]{:S(2)}) %collective-permute-start.22) | collective-permute-done | bytes 524320 | tf_op jit(solution)/shard_map/ppermute | solution.py:205
  282.9 4.7 %fusion.35 = (bf16[256,1024]{1,0:T(8,128)(2,1)S(1)}, bf16[256,1024]{1,0:T(8,128)(2,1)S(1)}, bf16[256,1024]{1,0:T(8,128)(2,1)S(1)}, bf16[256,1024]{1,0:T(8,128)(2...) fusion(f32[256,4096]{1,0:T(8,128)S(1)} %copy-done.1, ...), kind=kLoop, calls=%fused_computation.43 | loop fusion | flops 9437184 | bytes 14680068 | tf_op jit(solution)/shard_map/convert_element_type | solution.py:208
  287.5 3.0 fusion.34
  290.6 1.3 collective-permute-start.41
  291.9 1.3 collective-permute-start.32
  296.0 6.4 %collective-permute-done.41.halo_ref = bf16[144,1024]{1,0:T(8,128)(2,1)S(1)} collective-permute-done((bf16[144,1024]{1,0:T(8,128)(2,1)S(1)}, bf16[144,1024]{1,0:T(8,128)(2,1)S(1)}, u32[]{:S(2)}, u32[]{:S(2)}) %collective-permute-start.41) | collective-permute-done | bytes 294944 | tf_op jit(solution)/shard_map/ppermute | solution.py:26
  302.4 5.3 %shard_map.59 = bf16[3,256,1024]{2,1,0:T(8,128)(2,1)S(1)} custom-call(bf16[256,1024]{1,0:T(8,128)(2,1)S(1)} %get-tuple-element.22.gc_ref, bf16[144,1024]{1,0:T(8,128)(2,1)S(1)} %collective-permute-done.41.halo_ref, bf16[256,1024]{1,0:T(8,128)(2,1)S(1)} %get-tuple-element.25.gg_ref, f32[3,256,1024]{2,1,0:T(8,128)} %get-tuple-element.18.mix_ref, ...), custom_call_target="tpu_custom_call" | custom-call | flops 1073741824 | bytes 7802880 | tf_op jit(solution)/shard_map/pallas_call | solution.py:112
  308.7 5.3 %shard_map.58 = bf16[3,256,1024]{2,1,0:T(8,128)(2,1)S(1)} custom-call(bf16[256,1024]{1,0:T(8,128)(2,1)S(1)} %get-tuple-element.23.gc_ref, bf16[144,1024]{1,0:T(8,128)(2,1)S(1)} %collective-permute-done.32.halo_ref, bf16[256,1024]{1,0:T(8,128)(2,1)S(1)} %get-tuple-element.27.gg_ref, f32[3,256,1024]{2,1,0:T(8,128)} %get-tuple-element.19.mix_ref, ...), custom_call_target="tpu_custom_call" | custom-call | flops 1073741824 | bytes 7802880 | tf_op jit(solution)/shard_map/pallas_call | solution.py:112
  314.4 5.3 %shard_map.57 = bf16[3,256,1024]{2,1,0:T(8,128)(2,1)S(1)} custom-call(bf16[256,1024]{1,0:T(8,128)(2,1)S(1)} %get-tuple-element.24.gc_ref, bf16[144,1024]{1,0:T(8,128)(2,1)S(1)} %collective-permute-done.23.halo_ref, bf16[256,1024]{1,0:T(8,128)(2,1)S(1)} %get-tuple-element.29.gg_ref, f32[3,256,1024]{2,1,0:T(8,128)} %get-tuple-element.20.mix_ref, ...), custom_call_target="tpu_custom_call" | custom-call | flops 1073741824 | bytes 7802880 | tf_op jit(solution)/shard_map/pallas_call | solution.py:112
  320.0 5.3 %shard_map.56 = bf16[3,256,1024]{2,1,0:T(8,128)(2,1)S(1)} custom-call(bf16[256,1024]{1,0:T(8,128)(2,1)S(1)} %get-tuple-element.21.gc_ref, bf16[144,1024]{1,0:T(8,128)(2,1)S(1)} %collective-permute-done.13.halo_ref, bf16[256,1024]{1,0:T(8,128)(2,1)S(1)} %get-tuple-element.9.gg_ref, f32[3,256,1024]{2,1,0:T(8,128)} %get-tuple-element.17.mix_ref, ...), custom_call_target="tpu_custom_call" | custom-call | flops 1073741824 | bytes 7802880 | tf_op jit(solution)/shard_map/pallas_call | solution.py:112
  325.6 3.1 collective-permute-done.15
  328.7 3.0 maximum_bitcast_fusion.1
  (123 shorter events, 28.4 us)
Async XLA Ops:
  1.0 7.9 %copy-start.8 = (f32[1,3,3,4096]{3,0,2,1:T(1,128)S(1)}, f32[1,3,3,4096]{3,0,2,1:T(1,128)}, u32[]{:S(2)}) copy-start(f32[1,3,3,4096]{3,0,2,1:T(1,128)} %param.6) | copy-start | bytes 442372
  1.0 24.4 %collective-permute-start.11 = (bf16[2,3,4096]{2,0,1:T(2,128)(2,1)S(1)}, bf16[2,3,4096]{2,0,1:T(2,128)(2,1)S(1)}, u32[]{:S(2)}, u32[]{:S(2)}) collective-permute-start(bf16[2,3,4096]{2,0,1:T(2,128)(2,1)S(1)} %slice_bitcast_fusion.7), channel_id=1, source_target_pairs={{0,4},{4,8},{8,12},{12,16},{16,20},{20,24},{24,28},{1,5},{5,9},{9,... | collective-permute-start | bytes 147464 | tf_op jit(solution)/shard_map/ppermute | solution.py:26
  10.9 4.0 %copy-start.6 = (bf16[1,4096,512]{2,1,0:T(8,128)(2,1)S(1)}, bf16[1,4096,512]{2,1,0:T(8,128)(2,1)}, u32[]{:S(2)}) copy-start(bf16[1,4096,512]{2,1,0:T(8,128)(2,1)} %param.8) | copy-start | bytes 12582916
  11.2 9.6 %copy-start.13 = (bf16[1,128,256]{2,1,0:T(8,128)(2,1)S(1)}, bf16[1,128,256]{2,1,0:T(8,128)(2,1)}, u32[]{:S(2)}) copy-start(bf16[1,128,256]{2,1,0:T(8,128)(2,1)} %param.7) | copy-start | bytes 196612
  11.2 40.5 %collective-permute-start.12 = (bf16[128,4096]{1,0:T(8,128)(2,1)S(1)}, bf16[128,4096]{1,0:T(8,128)(2,1)S(1)}, u32[]{:S(2)}, u32[]{:S(2)}) collective-permute-start(bf16[128,4096]{1,0:T(8,128)(2,1)S(1)} %fusion.42), channel_id=1, source_target_pairs={{0,4},{4,8},{8,12},{12,16},{16,20},{20,24},{24,28},{1,5},{5,9},{9,... | collective-permute-start | bytes 3145736 | tf_op jit(solution)/shard_map/ppermute | solution.py:26
  17.1 79.8 %collective-permute-start.4 = (bf16[1024,512]{1,0:T(8,128)(2,1)}, bf16[1024,512]{1,0:T(8,128)(2,1)}, u32[]{:S(2)}, u32[]{:S(2)}) collective-permute-start(bf16[1024,512]{1,0:T(8,128)(2,1)} %get-tuple-element.31), channel_id=1, source_target_pairs={{0,4},{4,0},{8,12},{12,8},{16,20},{20,16},{24,28},{28,24},{1,5},{5... | collective-permute-start | bytes 3145736 | tf_op jit(solution)/shard_map/ppermute | solution.py:188
  18.5 24.4 %collective-permute-start = (bf16[256,2048]{1,0:T(8,128)(2,1)}, bf16[256,2048]{1,0:T(8,128)(2,1)}, u32[]{:S(2)}, u32[]{:S(2)}) collective-permute-start(bf16[256,2048]{1,0:T(8,128)(2,1)} %bitcast), channel_id=1, source_target_pairs={{0,2},{2,0},{1,3},{3,1},{4,6},{6,4},{5,7},{7,5},{8,10},{10,8},{9,1... | collective-permute-start | bytes 3145736 | tf_op jit(solution)/shard_map/ppermute | solution.py:141
  20.0 93.9 %collective-permute-start.34 = (bf16[1024,512]{1,0:T(8,128)(2,1)}, bf16[1024,512]{1,0:T(8,128)(2,1)}, u32[]{:S(2)}, u32[]{:S(2)}) collective-permute-start(bf16[1024,512]{1,0:T(8,128)(2,1)} %get-tuple-element.33), channel_id=1, source_target_pairs={{0,4},{4,0},{8,12},{12,8},{16,20},{20,16},{24,28},{28,24},{1,5},{5... | collective-permute-start | bytes 3145736 | tf_op jit(solution)/shard_map/ppermute | solution.py:188
  46.7 31.3 %collective-permute-start.1 = (bf16[256,1024]{1,0:T(8,128)(2,1)S(1)}, bf16[256,1024]{1,0:T(8,128)(2,1)S(1)}, u32[]{:S(2)}, u32[]{:S(2)}) collective-permute-start(bf16[256,1024]{1,0:T(8,128)(2,1)S(1)} %get-tuple-element.55), channel_id=1, source_target_pairs={{0,8},{4,12},{8,16},{12,20},{16,24},{20,28},{24,0},{28,4},{1,9},{5... | collective-permute-start | bytes 1572872 | tf_op jit(solution)/shard_map/ppermute | solution.py:150
  48.3 34.7 %collective-permute-start.2 = (bf16[256,1024]{1,0:T(8,128)(2,1)S(1)}, bf16[256,1024]{1,0:T(8,128)(2,1)S(1)}, u32[]{:S(2)}, u32[]{:S(2)}) collective-permute-start(bf16[256,1024]{1,0:T(8,128)(2,1)S(1)} %get-tuple-element.54), channel_id=1, source_target_pairs={{0,16},{4,20},{8,24},{12,28},{16,0},{20,4},{24,8},{28,12},{1,17},{... | collective-permute-start | bytes 1572872 | tf_op jit(solution)/shard_map/ppermute | solution.py:150
  51.7 32.7 %collective-permute-start.3 = (bf16[256,1024]{1,0:T(8,128)(2,1)S(1)}, bf16[256,1024]{1,0:T(8,128)(2,1)S(1)}, u32[]{:S(2)}, u32[]{:S(2)}) collective-permute-start(bf16[256,1024]{1,0:T(8,128)(2,1)S(1)} %get-tuple-element.53), channel_id=1, source_target_pairs={{0,24},{4,28},{8,0},{12,4},{16,8},{20,12},{24,16},{28,20},{1,25},{... | collective-permute-start | bytes 1572872 | tf_op jit(solution)/shard_map/ppermute | solution.py:150
  73.2 7.6 %copy-start = (f32[256,4096]{1,0:T(8,128)}, f32[256,4096]{1,0:T(8,128)S(1)}, u32[]{:S(2)}) copy-start(f32[256,4096]{1,0:T(8,128)S(1)} %get-tuple-element.8) | copy-start | bytes 12582916
  73.2 9.8 %copy-start.7 = (bf16[1024,512]{1,0:T(8,128)(2,1)S(1)}, bf16[1024,512]{1,0:T(8,128)(2,1)}, u32[]{:S(2)}) copy-start(bf16[1024,512]{1,0:T(8,128)(2,1)} %get-tuple-element.32) | copy-start | bytes 3145732
  78.0 41.2 %collective-permute-start.25 = (bf16[1024,512]{1,0:T(8,128)(2,1)}, bf16[1024,512]{1,0:T(8,128)(2,1)}, u32[]{:S(2)}, u32[]{:S(2)}) collective-permute-start(bf16[1024,512]{1,0:T(8,128)(2,1)} %get-tuple-element.34), channel_id=1, source_target_pairs={{0,4},{4,0},{8,12},{12,8},{16,20},{20,16},{24,28},{28,24},{1,5},{5... | collective-permute-start | bytes 3145736 | tf_op jit(solution)/shard_map/ppermute | solution.py:188
  83.0 43.9 %collective-permute-start.16 = (bf16[1024,512]{1,0:T(8,128)(2,1)S(1)}, bf16[1024,512]{1,0:T(8,128)(2,1)}, u32[]{:S(2)}, u32[]{:S(2)}) collective-permute-start(bf16[1024,512]{1,0:T(8,128)(2,1)S(1)} %copy-done.7), channel_id=1, source_target_pairs={{0,4},{4,0},{8,12},{12,8},{16,20},{20,16},{24,28},{28,24},{1,5},{5... | collective-permute-start | bytes 3145736 | tf_op jit(solution)/shard_map/ppermute | solution.py:188
  100.8 105.9 %copy-start.2 = (bf16[1024,1024]{1,0:T(8,128)(2,1)}, bf16[1024,1024]{1,0:T(8,128)(2,1)S(1)}, u32[]{:S(2)}) copy-start(bf16[1024,1024]{1,0:T(8,128)(2,1)S(1)} %fusion.31) | copy-start | bytes 6291460
  100.9 35.1 %collective-permute-start.5 = (bf16[256,1024]{1,0:T(8,128)(2,1)S(1)}, bf16[256,1024]{1,0:T(8,128)(2,1)S(1)}, u32[]{:S(2)}, u32[]{:S(2)}) collective-permute-start(bf16[256,1024]{1,0:T(8,128)(2,1)S(1)} %get-tuple-element.37), channel_id=1, source_target_pairs={{0,8},{4,12},{1,9},{5,13},{2,10},{6,14},{3,11},{7,15}} | collective-permute-start | bytes 1572872 | tf_op jit(solution)/shard_map/ppermute | solution.py:205
  113.2 50.6 %collective-permute-start.8 = (bf16[256,1024]{1,0:T(8,128)(2,1)S(1)}, bf16[256,1024]{1,0:T(8,128)(2,1)S(1)}, u32[]{:S(2)}, u32[]{:S(2)}) collective-permute-start(bf16[256,1024]{1,0:T(8,128)(2,1)S(1)} %get-tuple-element.38), channel_id=1, source_target_pairs={{24,16},{28,20},{25,17},{29,21},{26,18},{30,22},{27,19},{31,23}} | collective-permute-start | bytes 1572872 | tf_op jit(solution)/shard_map/ppermute | solution.py:205
  117.8 95.6 %copy-start.3 = (bf16[1024,1024]{1,0:T(8,128)(2,1)}, bf16[1024,1024]{1,0:T(8,128)(2,1)S(1)}, u32[]{:S(2)}) copy-start(bf16[1024,1024]{1,0:T(8,128)(2,1)S(1)} %fusion.22) | copy-start | bytes 6291460
  117.9 19.7 %collective-permute-start.35 = (bf16[256,1024]{1,0:T(8,128)(2,1)S(1)}, bf16[256,1024]{1,0:T(8,128)(2,1)S(1)}, u32[]{:S(2)}, u32[]{:S(2)}) collective-permute-start(bf16[256,1024]{1,0:T(8,128)(2,1)S(1)} %get-tuple-element.49), channel_id=1, source_target_pairs={{0,8},{4,12},{1,9},{5,13},{2,10},{6,14},{3,11},{7,15}} | collective-permute-start | bytes 1572872 | tf_op jit(solution)/shard_map/ppermute | solution.py:205
  119.2 55.9 %collective-permute-start.38 = (bf16[256,1024]{1,0:T(8,128)(2,1)S(1)}, bf16[256,1024]{1,0:T(8,128)(2,1)S(1)}, u32[]{:S(2)}, u32[]{:S(2)}) collective-permute-start(bf16[256,1024]{1,0:T(8,128)(2,1)S(1)} %get-tuple-element.50), channel_id=1, source_target_pairs={{24,16},{28,20},{25,17},{29,21},{26,18},{30,22},{27,19},{31,23}} | collective-permute-start | bytes 1572872 | tf_op jit(solution)/shard_map/ppermute | solution.py:205
  124.1 91.6 %copy-start.4 = (bf16[1024,1024]{1,0:T(8,128)(2,1)}, bf16[1024,1024]{1,0:T(8,128)(2,1)S(1)}, u32[]{:S(2)}) copy-start(bf16[1024,1024]{1,0:T(8,128)(2,1)S(1)} %fusion.25) | copy-start | bytes 6291460
  126.9 21.0 %collective-permute-start.26 = (bf16[256,1024]{1,0:T(8,128)(2,1)S(1)}, bf16[256,1024]{1,0:T(8,128)(2,1)S(1)}, u32[]{:S(2)}, u32[]{:S(2)}) collective-permute-start(bf16[256,1024]{1,0:T(8,128)(2,1)S(1)} %get-tuple-element.45), channel_id=1, source_target_pairs={{0,8},{4,12},{1,9},{5,13},{2,10},{6,14},{3,11},{7,15}} | collective-permute-start | bytes 1572872 | tf_op jit(solution)/shard_map/ppermute | solution.py:205
  135.9 101.3 %copy-start.5 = (bf16[1024,1024]{1,0:T(8,128)(2,1)}, bf16[1024,1024]{1,0:T(8,128)(2,1)S(1)}, u32[]{:S(2)}) copy-start(bf16[1024,1024]{1,0:T(8,128)(2,1)S(1)} %fusion.28) | copy-start | bytes 6291460
  136.1 23.1 %collective-permute-start.17 = (bf16[256,1024]{1,0:T(8,128)(2,1)S(1)}, bf16[256,1024]{1,0:T(8,128)(2,1)S(1)}, u32[]{:S(2)}, u32[]{:S(2)}) collective-permute-start(bf16[256,1024]{1,0:T(8,128)(2,1)S(1)} %get-tuple-element.41), channel_id=1, source_target_pairs={{0,8},{4,12},{1,9},{5,13},{2,10},{6,14},{3,11},{7,15}} | collective-permute-start | bytes 1572872 | tf_op jit(solution)/shard_map/ppermute | solution.py:205
  137.6 32.8 %collective-permute-start.6 = (bf16[256,1024]{1,0:T(8,128)(2,1)S(1)}, bf16[256,1024]{1,0:T(8,128)(2,1)S(1)}, u32[]{:S(2)}, u32[]{:S(2)}) collective-permute-start(bf16[256,1024]{1,0:T(8,128)(2,1)S(1)} %fusion.63), channel_id=1, source_target_pairs={{0,8},{4,12},{8,16},{12,20},{1,9},{5,13},{9,17},{13,21},{2,10},{6,... | collective-permute-start | bytes 1572872 | tf_op jit(solution)/shard_map/ppermute | solution.py:205
  147.9 34.8 %collective-permute-start.29 = (bf16[256,1024]{1,0:T(8,128)(2,1)S(1)}, bf16[256,1024]{1,0:T(8,128)(2,1)S(1)}, u32[]{:S(2)}, u32[]{:S(2)}) collective-permute-start(bf16[256,1024]{1,0:T(8,128)(2,1)S(1)} %get-tuple-element.46), channel_id=1, source_target_pairs={{24,16},{28,20},{25,17},{29,21},{26,18},{30,22},{27,19},{31,23}} | collective-permute-start | bytes 1572872 | tf_op jit(solution)/shard_map/ppermute | solution.py:205
  159.1 22.5 %collective-permute-start.36 = (bf16[256,1024]{1,0:T(8,128)(2,1)S(1)}, bf16[256,1024]{1,0:T(8,128)(2,1)S(1)}, u32[]{:S(2)}, u32[]{:S(2)}) collective-permute-start(bf16[256,1024]{1,0:T(8,128)(2,1)S(1)} %fusion.45), channel_id=1, source_target_pairs={{0,8},{4,12},{8,16},{12,20},{1,9},{5,13},{9,17},{13,21},{2,10},{6,... | collective-permute-start | bytes 1572872 | tf_op jit(solution)/shard_map/ppermute | solution.py:205
  163.8 30.2 %collective-permute-start.20 = (bf16[256,1024]{1,0:T(8,128)(2,1)S(1)}, bf16[256,1024]{1,0:T(8,128)(2,1)S(1)}, u32[]{:S(2)}, u32[]{:S(2)}) collective-permute-start(bf16[256,1024]{1,0:T(8,128)(2,1)S(1)} %get-tuple-element.42), channel_id=1, source_target_pairs={{24,16},{28,20},{25,17},{29,21},{26,18},{30,22},{27,19},{31,23}} | collective-permute-start | bytes 1572872 | tf_op jit(solution)/shard_map/ppermute | solution.py:205
  170.4 22.5 %collective-permute-start.27 = (bf16[256,1024]{1,0:T(8,128)(2,1)S(1)}, bf16[256,1024]{1,0:T(8,128)(2,1)S(1)}, u32[]{:S(2)}, u32[]{:S(2)}) collective-permute-start(bf16[256,1024]{1,0:T(8,128)(2,1)S(1)} %fusion.51), channel_id=1, source_target_pairs={{0,8},{4,12},{8,16},{12,20},{1,9},{5,13},{9,17},{13,21},{2,10},{6,... | collective-permute-start | bytes 1572872 | tf_op jit(solution)/shard_map/ppermute | solution.py:205
  175.2 28.9 %collective-permute-start.18 = (bf16[256,1024]{1,0:T(8,128)(2,1)S(1)}, bf16[256,1024]{1,0:T(8,128)(2,1)S(1)}, u32[]{:S(2)}, u32[]{:S(2)}) collective-permute-start(bf16[256,1024]{1,0:T(8,128)(2,1)S(1)} %fusion.57), channel_id=1, source_target_pairs={{0,8},{4,12},{8,16},{12,20},{1,9},{5,13},{9,17},{13,21},{2,10},{6,... | collective-permute-start | bytes 1572872 | tf_op jit(solution)/shard_map/ppermute | solution.py:205
  181.6 24.4 %collective-permute-start.9 = (bf16[256,1024]{1,0:T(8,128)(2,1)S(1)}, bf16[256,1024]{1,0:T(8,128)(2,1)S(1)}, u32[]{:S(2)}, u32[]{:S(2)}) collective-permute-start(bf16[256,1024]{1,0:T(8,128)(2,1)S(1)} %get-tuple-element.36), channel_id=1, source_target_pairs={{16,8},{20,12},{24,16},{28,20},{17,9},{21,13},{25,17},{29,21},{18,... | collective-permute-start | bytes 1572872 | tf_op jit(solution)/shard_map/ppermute | solution.py:205
  182.7 56.9 %collective-permute-start.7 = (bf16[256,1024]{1,0:T(8,128)(2,1)S(1)}, bf16[256,1024]{1,0:T(8,128)(2,1)S(1)}, u32[]{:S(2)}, u32[]{:S(2)}) collective-permute-start(bf16[256,1024]{1,0:T(8,128)(2,1)S(1)} %get-tuple-element.35), channel_id=1, source_target_pairs={{0,8},{4,12},{8,16},{12,20},{16,24},{20,28},{1,9},{5,13},{9,17},{1... | collective-permute-start | bytes 1572872 | tf_op jit(solution)/shard_map/ppermute | solution.py:205
  192.8 14.9 %collective-permute-start.39 = (bf16[256,1024]{1,0:T(8,128)(2,1)S(1)}, bf16[256,1024]{1,0:T(8,128)(2,1)S(1)}, u32[]{:S(2)}, u32[]{:S(2)}) collective-permute-start(bf16[256,1024]{1,0:T(8,128)(2,1)S(1)} %get-tuple-element.48), channel_id=1, source_target_pairs={{16,8},{20,12},{24,16},{28,20},{17,9},{21,13},{25,17},{29,21},{18,... | collective-permute-start | bytes 1572872 | tf_op jit(solution)/shard_map/ppermute | solution.py:205
  193.9 46.9 %collective-permute-start.37 = (bf16[256,1024]{1,0:T(8,128)(2,1)S(1)}, bf16[256,1024]{1,0:T(8,128)(2,1)S(1)}, u32[]{:S(2)}, u32[]{:S(2)}) collective-permute-start(bf16[256,1024]{1,0:T(8,128)(2,1)S(1)} %get-tuple-element.47), channel_id=1, source_target_pairs={{0,8},{4,12},{8,16},{12,20},{16,24},{20,28},{1,9},{5,13},{9,17},{1... | collective-permute-start | bytes 1572872 | tf_op jit(solution)/shard_map/ppermute | solution.py:205
  204.1 10.3 %collective-permute-start.30 = (bf16[256,1024]{1,0:T(8,128)(2,1)S(1)}, bf16[256,1024]{1,0:T(8,128)(2,1)S(1)}, u32[]{:S(2)}, u32[]{:S(2)}) collective-permute-start(bf16[256,1024]{1,0:T(8,128)(2,1)S(1)} %get-tuple-element.44), channel_id=1, source_target_pairs={{16,8},{20,12},{24,16},{28,20},{17,9},{21,13},{25,17},{29,21},{18,... | collective-permute-start | bytes 1572872 | tf_op jit(solution)/shard_map/ppermute | solution.py:205
  206.0 10.6 %collective-permute-start.21 = (bf16[256,1024]{1,0:T(8,128)(2,1)S(1)}, bf16[256,1024]{1,0:T(8,128)(2,1)S(1)}, u32[]{:S(2)}, u32[]{:S(2)}) collective-permute-start(bf16[256,1024]{1,0:T(8,128)(2,1)S(1)} %get-tuple-element.40), channel_id=1, source_target_pairs={{16,8},{20,12},{24,16},{28,20},{17,9},{21,13},{25,17},{29,21},{18,... | collective-permute-start | bytes 1572872 | tf_op jit(solution)/shard_map/ppermute | solution.py:205
  207.8 34.4 %collective-permute-start.28 = (bf16[256,1024]{1,0:T(8,128)(2,1)S(1)}, bf16[256,1024]{1,0:T(8,128)(2,1)S(1)}, u32[]{:S(2)}, u32[]{:S(2)}) collective-permute-start(bf16[256,1024]{1,0:T(8,128)(2,1)S(1)} %get-tuple-element.43), channel_id=1, source_target_pairs={{0,8},{4,12},{8,16},{12,20},{16,24},{20,28},{1,9},{5,13},{9,17},{1... | collective-permute-start | bytes 1572872 | tf_op jit(solution)/shard_map/ppermute | solution.py:205
  214.4 23.9 %collective-permute-start.14 = (f32[2,8,4096]{2,1,0:T(8,128)S(1)}, f32[2,8,4096]{2,1,0:T(8,128)S(1)}, u32[]{:S(2)}, u32[]{:S(2)}) collective-permute-start(f32[2,8,4096]{2,1,0:T(8,128)S(1)} %slice.190), channel_id=1, source_target_pairs={{4,0},{8,4},{12,8},{16,12},{20,16},{24,20},{28,24},{5,1},{9,5},{13... | collective-permute-start | bytes 786440 | tf_op jit(solution)/shard_map/ppermute | solution.py:26
  216.7 38.0 %collective-permute-start.19 = (bf16[256,1024]{1,0:T(8,128)(2,1)}, bf16[256,1024]{1,0:T(8,128)(2,1)}, u32[]{:S(2)}, u32[]{:S(2)}) collective-permute-start(bf16[256,1024]{1,0:T(8,128)(2,1)} %get-tuple-element.39), channel_id=1, source_target_pairs={{0,8},{4,12},{8,16},{12,20},{16,24},{20,28},{1,9},{5,13},{9,17},{1... | collective-permute-start | bytes 1572872 | tf_op jit(solution)/shard_map/ppermute | solution.py:205
  238.2 3.9 %copy-start.11 = (f32[2,8,4096]{2,1,0:T(8,128)}, f32[2,8,4096]{2,1,0:T(8,128)S(1)}, u32[]{:S(2)}) copy-start(f32[2,8,4096]{2,1,0:T(8,128)S(1)} %collective-permute-done.14) | copy-start | bytes 786436
  238.2 17.1 %collective-permute-start.10 = (bf16[256,1024]{1,0:T(8,128)(2,1)}, bf16[256,1024]{1,0:T(8,128)(2,1)}, u32[]{:S(2)}, u32[]{:S(2)}) collective-permute-start(bf16[256,1024]{1,0:T(8,128)(2,1)} %fusion.62), channel_id=1, source_target_pairs={{8,0},{12,4},{16,8},{20,12},{24,16},{28,20},{9,1},{13,5},{17,9},{2... | collective-permute-start | bytes 1572872 | tf_op jit(solution)/shard_map/ppermute | solution.py:205
  239.5 27.0 %collective-permute-start.40 = (bf16[256,1024]{1,0:T(8,128)(2,1)}, bf16[256,1024]{1,0:T(8,128)(2,1)}, u32[]{:S(2)}, u32[]{:S(2)}) collective-permute-start(bf16[256,1024]{1,0:T(8,128)(2,1)} %fusion.44), channel_id=1, source_target_pairs={{8,0},{12,4},{16,8},{20,12},{24,16},{28,20},{9,1},{13,5},{17,9},{2... | collective-permute-start | bytes 1572872 | tf_op jit(solution)/shard_map/ppermute | solution.py:205
  240.8 2.9 copy-start.9
  240.9 36.4 %collective-permute-start.31 = (bf16[256,1024]{1,0:T(8,128)(2,1)}, bf16[256,1024]{1,0:T(8,128)(2,1)}, u32[]{:S(2)}, u32[]{:S(2)}) collective-permute-start(bf16[256,1024]{1,0:T(8,128)(2,1)} %fusion.50), channel_id=1, source_target_pairs={{8,0},{12,4},{16,8},{20,12},{24,16},{28,20},{9,1},{13,5},{17,9},{2... | collective-permute-start | bytes 1572872 | tf_op jit(solution)/shard_map/ppermute | solution.py:205
  242.2 1.6 copy-start.10
  242.2 40.7 %collective-permute-start.22 = (bf16[256,1024]{1,0:T(8,128)(2,1)}, bf16[256,1024]{1,0:T(8,128)(2,1)}, u32[]{:S(2)}, u32[]{:S(2)}) collective-permute-start(bf16[256,1024]{1,0:T(8,128)(2,1)} %fusion.56), channel_id=1, source_target_pairs={{8,0},{12,4},{16,8},{20,12},{24,16},{28,20},{9,1},{13,5},{17,9},{2... | collective-permute-start | bytes 1572872 | tf_op jit(solution)/shard_map/ppermute | solution.py:205
  243.8 10.9 %copy-start.12 = (f32[2,8,4096]{2,1,0:T(8,128)S(1)}, f32[2,8,4096]{2,1,0:T(8,128)}, u32[]{:S(2)}) copy-start(f32[2,8,4096]{2,1,0:T(8,128)} %copy-done.11) | copy-start | bytes 786436
  243.8 39.1 %copy-start.1 = (f32[256,4096]{1,0:T(8,128)S(1)}, f32[256,4096]{1,0:T(8,128)}, u32[]{:S(2)}) copy-start(f32[256,4096]{1,0:T(8,128)} %copy-done) | copy-start | bytes 12582916
  290.6 11.8 %collective-permute-start.41 = (bf16[144,1024]{1,0:T(8,128)(2,1)S(1)}, bf16[144,1024]{1,0:T(8,128)(2,1)S(1)}, u32[]{:S(2)}, u32[]{:S(2)}) collective-permute-start(bf16[144,1024]{1,0:T(8,128)(2,1)S(1)} %pad_maximum_fusion.4), channel_id=1, source_target_pairs={{4,0},{8,4},{12,8},{16,12},{20,16},{24,20},{28,24},{5,1},{9,5},{13... | collective-permute-start | bytes 884744 | tf_op jit(solution)/shard_map/ppermute | solution.py:26
  291.9 16.8 %collective-permute-start.32 = (bf16[144,1024]{1,0:T(8,128)(2,1)S(1)}, bf16[144,1024]{1,0:T(8,128)(2,1)S(1)}, u32[]{:S(2)}, u32[]{:S(2)}) collective-permute-start(bf16[144,1024]{1,0:T(8,128)(2,1)S(1)} %pad_maximum_fusion.3), channel_id=1, source_target_pairs={{4,0},{8,4},{12,8},{16,12},{20,16},{24,20},{28,24},{5,1},{9,5},{13... | collective-permute-start | bytes 884744 | tf_op jit(solution)/shard_map/ppermute | solution.py:26
  293.3 21.1 %collective-permute-start.23 = (bf16[144,1024]{1,0:T(8,128)(2,1)S(1)}, bf16[144,1024]{1,0:T(8,128)(2,1)S(1)}, u32[]{:S(2)}, u32[]{:S(2)}) collective-permute-start(bf16[144,1024]{1,0:T(8,128)(2,1)S(1)} %pad_maximum_fusion.2), channel_id=1, source_target_pairs={{4,0},{8,4},{12,8},{16,12},{20,16},{24,20},{28,24},{5,1},{9,5},{13... | collective-permute-start | bytes 884744 | tf_op jit(solution)/shard_map/ppermute | solution.py:26
  294.7 25.3 %collective-permute-start.13 = (bf16[144,1024]{1,0:T(8,128)(2,1)S(1)}, bf16[144,1024]{1,0:T(8,128)(2,1)S(1)}, u32[]{:S(2)}, u32[]{:S(2)}) collective-permute-start(bf16[144,1024]{1,0:T(8,128)(2,1)S(1)} %pad_maximum_fusion.1), channel_id=1, source_target_pairs={{4,0},{8,4},{12,8},{16,12},{20,16},{24,20},{28,24},{5,1},{9,5},{13... | collective-permute-start | bytes 884744 | tf_op jit(solution)/shard_map/ppermute | solution.py:26
  307.7 17.9 %collective-permute-start.42 = (bf16[3,256,1024]{2,1,0:T(8,128)(2,1)S(1)}, bf16[3,256,1024]{2,1,0:T(8,128)(2,1)S(1)}, u32[]{:S(2)}, u32[]{:S(2)}) collective-permute-start(bf16[3,256,1024]{2,1,0:T(8,128)(2,1)S(1)} %shard_map.59), channel_id=1, source_target_pairs={{0,1},{1,0},{2,3},{3,2},{4,5},{5,4},{6,7},{7,6},{8,9},{9,8},{10,11... | collective-permute-start | bytes 4718600 | tf_op jit(solution)/shard_map/ppermute | solution.py:228
  314.0 11.6 %collective-permute-start.33 = (bf16[3,256,1024]{2,1,0:T(8,128)(2,1)S(1)}, bf16[3,256,1024]{2,1,0:T(8,128)(2,1)S(1)}, u32[]{:S(2)}, u32[]{:S(2)}) collective-permute-start(bf16[3,256,1024]{2,1,0:T(8,128)(2,1)S(1)} %shard_map.58), channel_id=1, source_target_pairs={{0,1},{1,0},{2,3},{3,2},{4,5},{5,4},{6,7},{7,6},{8,9},{9,8},{10,11... | collective-permute-start | bytes 4718600 | tf_op jit(solution)/shard_map/ppermute | solution.py:228
  319.7 5.9 %collective-permute-start.24 = (bf16[3,256,1024]{2,1,0:T(8,128)(2,1)S(1)}, bf16[3,256,1024]{2,1,0:T(8,128)(2,1)S(1)}, u32[]{:S(2)}, u32[]{:S(2)}) collective-permute-start(bf16[3,256,1024]{2,1,0:T(8,128)(2,1)S(1)} %shard_map.57), channel_id=1, source_target_pairs={{0,1},{1,0},{2,3},{3,2},{4,5},{5,4},{6,7},{7,6},{8,9},{9,8},{10,11... | collective-permute-start | bytes 4718600 | tf_op jit(solution)/shard_map/ppermute | solution.py:228
  325.3 3.5 %collective-permute-start.15 = (bf16[3,256,1024]{2,1,0:T(8,128)(2,1)S(1)}, bf16[3,256,1024]{2,1,0:T(8,128)(2,1)S(1)}, u32[]{:S(2)}, u32[]{:S(2)}) collective-permute-start(bf16[3,256,1024]{2,1,0:T(8,128)(2,1)S(1)} %shard_map.56), channel_id=1, source_target_pairs={{0,1},{1,0},{2,3},{3,2},{4,5},{5,4},{6,7},{7,6},{8,9},{9,8},{10,11... | collective-permute-start | bytes 4718600 | tf_op jit(solution)/shard_map/ppermute | solution.py:228

commit v2 on v1

v2 whole, which is shorter than its diff:
```python
import functools

import jax
import jax.numpy as jnp
from jax import lax
from jax.experimental import pallas as pl
from jax.experimental.pallas import tpu as pltpu
from jax.sharding import PartitionSpec as P

LANES = 128
TAIL = 8
CHUNKS = 4
WAVES = 2
F32 = jnp.float32
BF16 = jnp.bfloat16


def split_of(count):
    inner = 1
    while inner * inner * 4 <= count:
        inner *= 2
    return count // inner, inner


def ahead(block, axis, distance):
    devices = range(lax.axis_size(axis))
    return lax.ppermute(block, axis, [(i - distance, i) for i in devices if i - distance in devices])


def toeplitz(row, rows, shift):
    wide = jnp.broadcast_to(row, (rows, row.shape[1]))
    return pltpu.roll(wide, shift, 1, stride=1, stride_axis=0).astype(BF16)


def group_conv(filter_rows, windows, shift, group_width, tail=None):
    taps = windows.shape[0] // 2
    lane = lax.broadcasted_iota(jnp.int32, (1, 2 * LANES), 1) % LANES // group_width
    total = jnp.zeros((taps, 2 * LANES), F32)
    end = None if tail is None else jnp.zeros((TAIL, LANES), F32)
    for g in range(LANES // group_width):
        band = toeplitz(filter_rows[g : g + 1, :], taps, shift)
        part = jnp.dot(band, windows, preferred_element_type=F32)
        total = jnp.where(lane == g, part, total)
        if tail is not None:
            part = jnp.dot(band[:16], tail, preferred_element_type=F32)[:TAIL]
            end = jnp.where(lane[:, :LANES] == g, part, end)
    joined = jnp.concatenate([total[:, :LANES], total[:, LANES:]], axis=0)
    return joined if tail is None else (joined, end)


def forward_kernel(group_width, feat_ref, before_ref, after_ref, taps_ref, filt_ref, halo_ref, conv_ref, mix_ref):
    rows = conv_ref.shape[0]
    taps = halo_ref.shape[0]
    pad = before_ref.shape[1]
    per = LANES // group_width
    for tile in range(conv_ref.shape[1] // LANES):
        cols = slice(tile * LANES, (tile + 1) * LANES)
        mixed = []
        for i in range(3):
            ext = jnp.concatenate(
                [before_ref[i, :, cols], feat_ref[i, :, cols].astype(F32), after_ref[i, :, cols]], axis=0
            )
            mixed.append(
                taps_ref[0, i : i + 1, cols] * ext[pad:]
                + taps_ref[1, i : i + 1, cols] * pltpu.roll(ext, 1, 0)[pad:]
                + taps_ref[2, i : i + 1, cols] * pltpu.roll(ext, 2, 0)[pad:]
            )
            mix_ref[i, :, cols] = mixed[i]
        products = (mixed[1] * mixed[2])[:rows].astype(BF16)
        whole = jnp.concatenate([halo_ref[:, cols], products], axis=0)
        windows = jnp.concatenate([whole[: 2 * taps], whole[taps : 3 * taps]], axis=1)
        conv_ref[:, cols] = group_conv(filt_ref[tile * per : (tile + 1) * per, :], windows, 1, group_width)


def backward_kernel(group_width, grad_ref, halo_ref, conv_ref, mix_ref, taps_ref, filt_ref, out_ref):
    rows = grad_ref.shape[0]
    taps = filt_ref.shape[1] // 2
    held = halo_ref.shape[0]
    per = LANES // group_width
    for tile in range(grad_ref.shape[1] // LANES):
        cols = slice(tile * LANES, (tile + 1) * LANES)
        halo = halo_ref[:, cols]
        grad_y = grad_ref[:, cols].astype(F32)
        own = (grad_y * mix_ref[0, :rows, cols]).astype(BF16)
        last = jnp.concatenate([halo, jnp.zeros((2 * taps - held, LANES), BF16)], axis=0)
        windows = jnp.concatenate(
            [own, jnp.concatenate([own[taps:], halo[:taps]], axis=0)], axis=1
        )
        prod, prod_end = group_conv(filt_ref[tile * per : (tile + 1) * per, :], windows, 0, group_width, last)
        prod = jnp.concatenate([prod, prod_end], axis=0)
        grad_gate = jnp.concatenate([grad_y * conv_ref[:, cols], halo.astype(F32)[held - TAIL :]], axis=0)
        for i, term in enumerate((grad_gate, prod * mix_ref[2, :, cols], prod * mix_ref[1, :, cols])):
            ext = term.astype(BF16).astype(F32)
            size = rows + TAIL
            out_ref[i, :, cols] = (
                taps_ref[0, i : i + 1, cols] * ext[:rows]
                + taps_ref[1, i : i + 1, cols] * pltpu.roll(ext, size - 1, 0)[:rows]
                + taps_ref[2, i : i + 1, cols] * pltpu.roll(ext, size - 2, 0)[:rows]
            ).astype(BF16)


def tiled(kernel, operands, outs, channels, group_width, flops, wide=512):
    wide = min(wide, channels)

    def spec(shape, by_group, start):
        first = start // wide
        if by_group:
            return pl.BlockSpec((wide // group_width,) + shape[1:], lambda c: (first + c, 0))
        lead = len(shape) - 1
        return pl.BlockSpec(shape[:-1] + (wide,), lambda c: (0,) * lead + (first + c,))

    moved = sum(a.size * a.dtype.itemsize for a, _, _ in operands) + sum(4 * o.size for o in outs)
    return pl.pallas_call(
        functools.partial(kernel, group_width),
        grid=(channels // wide,),
        in_specs=[spec(a.shape, by_group, start) for a, by_group, start in operands],
        out_specs=[spec(o.shape, False, 0) for o in outs],
        out_shape=outs,
        compiler_params=pltpu.CompilerParams(vmem_limit_bytes=48 * 1024 * 1024),
        cost_estimate=pl.CostEstimate(flops=flops, bytes_accessed=moved, transcendentals=0),
    )(*[a for a, _, _ in operands])


def after(value, *others):
    return lax.optimization_barrier((value,) + others)[0]


def local(features, short_taps, long_filters, out_weight, out_grad):
    feats, taps, filters = features[0], short_taps[0], long_filters[0]
    weight, cotangent = out_weight[0], out_grad[0]
    rows, _, channels = feats.shape
    reach, groups = filters.shape
    width = channels // groups
    outer, inner = split_of(lax.axis_size("ctx"))
    place = lax.axis_index("ctx")
    z, x = place // inner, place % inner
    tp_count, tp_place = lax.axis_size("tp"), lax.axis_index("tp")
    chunks = max(1, min(CHUNKS, channels // 512))
    waves = min(WAVES, chunks)
    piece, stretch = channels // chunks, channels // waves
    own_depth = weight.shape[1]
    depth = inner * own_depth
    share = cotangent.shape[1]
    cells = [(zz, xx) for zz in range(outer) for xx in range(inner)]

    full = jnp.zeros((rows, tp_count * share), cotangent.dtype)
    full = lax.dynamic_update_slice(full, cotangent, (0, tp_place * share))
    for s in range(1, tp_count):
        got = lax.ppermute(cotangent, "tp", [(i, (i + s) % tp_count) for i in range(tp_count)])
        full = lax.dynamic_update_slice(full, got, (0, (tp_place - s) % tp_count * share))

    weights = []
    for w in range(waves):
        mine = weight[w * stretch : (w + 1) * stretch]
        held = [mine]
        for s in range(1, inner):
            route = [(zz * inner + xx, zz * inner + (xx + s) % inner) for zz, xx in cells]
            held.append(lax.ppermute(mine, "ctx", route))
        weights.append(held)

    tokens = []
    for s in range(outer):
        start = (z + s) % outer * depth
        block = jnp.concatenate(
            [
                lax.dynamic_slice(full, (0, start + (x - i) % inner * own_depth), (rows, own_depth))
                for i in range(inner)
            ],
            axis=1,
        )
        if s:
            route = [(zz * inner + xx, (zz + s) % outer * inner + xx) for zz, xx in cells]
            block = lax.ppermute(block, "ctx", route)
        tokens.append(block)

    streams = jnp.transpose(feats, (1, 0, 2))
    tail_f = streams[:, rows - reach - 2 :].astype(F32)
    by_tap = taps[:, :, None]
    tail_mix = by_tap[0] * tail_f[:, 2:] + by_tap[1] * tail_f[:, 1:-1] + by_tap[2] * tail_f[:, :-2]
    prod_tail = (tail_mix[1] * tail_mix[2]).astype(BF16)
    packed = jnp.concatenate([prod_tail] + [streams[i, rows - 2 :] for i in range(3)], axis=0)
    packed = ahead(packed, "ctx", 1)
    prod_halo = packed[:reach]
    before = jnp.pad(packed[reach:].reshape(3, 2, channels).astype(F32), ((0, 0), (TAIL - 2, 0), (0, 0)))
    behind = ahead(streams[:, :2], "ctx", -1)
    behind = jnp.pad(behind.astype(F32), ((0, 0), (0, TAIL - 2), (0, 0)))
    by_group = jnp.transpose(filters).astype(F32)
    blank = jnp.zeros((groups, reach), F32)
    backward_rows = jnp.concatenate([by_group, blank], axis=1)
    forward_rows = jnp.concatenate([by_group[:, ::-1], blank], axis=1)
    flops = 2 * groups * reach * 4 * reach * LANES
    conv, mix = tiled(
        forward_kernel,
        [
            (streams, False, 0),
            (before, False, 0),
            (behind, False, 0),
            (taps, False, 0),
            (forward_rows, True, 0),
            (prod_halo, False, 0),
        ],
        [jax.ShapeDtypeStruct((rows, channels), F32), jax.ShapeDtypeStruct((3, rows + TAIL, channels), F32)],
        channels,
        width,
        flops,
    )

    results = []
    halos = []
    gate_order = {}
    per_wave = chunks // waves
    for k in range(chunks):
        lo, hi = k * piece, (k + 1) * piece
        wave, at = k // per_wave, k % per_wave
        joined = jnp.concatenate([h[at * piece : (at + 1) * piece] for h in weights[wave]], axis=1)
        partial = [
            lax.optimization_barrier(
                jnp.einsum("tn,cn->tc", block, joined, preferred_element_type=F32).astype(BF16)
            )
            for block in tokens
        ]
        total = partial[0].astype(F32)
        for sign in (1, -1):
            got = None
            for j in range(outer - 1):
                send = partial[j + 1] if sign == 1 else partial[outer - 1 - j]
                if got is not None:
                    send = (send.astype(F32) + got.astype(F32)).astype(BF16)
                    if wave and j == outer - 2:
                        send = after(send, halos[k - per_wave])
                elif wave:
                    send = after(send, gate_order[wave - 1, at, sign])
                sources = range(j + 1) if sign == 1 else range(outer - 1 - j, outer)
                route = [(zz * inner + xx, (zz + sign) * inner + xx) for zz in sources for xx in range(inner)]
                got = lax.ppermute(send, "ctx", route)
                if j == outer - 3:
                    gate_order[wave, at, sign] = got
            total = total + got.astype(F32)
        grad_y = total.astype(BF16)
        if wave:
            grad_y = after(grad_y, results[k - per_wave])
        top = grad_y[: reach + 8].astype(F32)
        halo = jnp.concatenate(
            [
                (top * mix[0, : reach + 8, lo:hi]).astype(BF16),
                (top[:TAIL] * conv[:TAIL, lo:hi]).astype(BF16),
            ],
            axis=0,
        )
        halos.append(halo)
        halo = ahead(halo, "ctx", -1)
        (out,) = tiled(
            backward_kernel,
            [
                (grad_y, False, 0),
                (halo, False, 0),
                (conv, False, lo),
                (mix, False, lo),
                (taps, False, lo),
                (backward_rows, True, lo),
            ],
            [jax.ShapeDtypeStruct((3, rows, piece), BF16)],
            piece,
            width,
            flops // chunks,
        )
        count = lax.axis_size("pp")
        results.append(lax.ppermute(out, "pp", [(i, (i - 1) % count) for i in range(count)]))
    return jnp.transpose(jnp.concatenate(results, axis=2), (1, 0, 2))[None]


def solution(mesh):
    in_specs = (
        P("pp", "ctx", None, "tp"),
        P("pp", None, None, "tp"),
        P("pp", None, "tp"),
        P("pp", "tp", "ctx"),
        P("pp", "ctx", "tp"),
    )
    out_specs = P("pp", "ctx", None, "tp")
    return jax.shard_map(local, mesh=mesh, in_specs=in_specs, out_specs=out_specs, check_vma=False)
```

time: 339 us -> 358 us (1.056)
  waiting for transfers between devices: 91.2 us -> 160 us
  local copies, waits for them, and re-layouts: 41.7 us -> 19.1 us
  starting transfers between devices: 115 us -> 92.7 us
  other arithmetic: 30.7 us -> 20.5 us
  matrix products: 15.3 us -> 24.5 us
    ppermute x7 -> x6, waiting for transfers between devices: 7.64 us -> 104 us  [ahead(): lax.ppermute(block, axis, [(i - distance, i) for i in devices if i - dist...]
    ppermute x24, waiting for transfers between devices: 65.8 us -> 50.5 us  [local(): got = lax.ppermute(send, 'ctx', route)]
    ppermute x24, starting transfers between devices: 81.9 us -> 67 us  [local(): got = lax.ppermute(send, 'ctx', route)]
    dot_general x4 -> x16, matrix products: 15.3 us -> 24.5 us  [local(): jnp.einsum('tn,cn->tc', block, joined, preferred_element_type=F32)]
    dynamic_update_slice x6 -> x2, local copies, waits for them, and re-layouts: 9.4 us -> 1.43 us  [the longest x1 1.31 us: local(): lax.dynamic_update_slice(full, got, (0, (tp_place - s) % tp_count * share))]
    transpose x1 -> x0, other arithmetic: 7.83 us -> none  [local(): ext = jnp.transpose(ext, (1, 0, 2))]
    ppermute x1, waiting for transfers between devices: 9.65 us -> 1.99 us  [local(): lax.ppermute(cotangent, 'tp', [(i, (i + s) % tp_count) for i in range(tp_...]
    dynamic_slice x2 -> x1, local copies, waits for them, and re-layouts: 8.02 us -> 0.97 us  [local(): lax.dynamic_slice(full, (0, start + (x - i) % inner * own_depth), (rows,...]
  transfers between devices with their start and end apart: 43 -> 40, of which waited for: 17 -> 14; matrix products, arithmetic and copies ran while one was open for 23% -> 16% of each run, Pallas kernels for 11% -> 10%
where the time goes in v2:
time: 358 us; the launch traced here: 355 us
  waiting for transfers between devices  160 us (45%)
  starting transfers between devices  92.7 us (26%)
  Pallas kernels  36.8 us (10%)
  matrix products  24.5 us (7%)
  other arithmetic  20.5 us (6%)
  local copies, waits for them, and re-layouts  19.1 us (5%)
    ppermute x6, waiting for transfers between devices, ahead(): lax.ppermute(block, axis, [(i - distance, i) for i in devices if i - dist...  104 us
    ppermute x24, starting transfers between devices, local(): got = lax.ppermute(send, 'ctx', route)  67 us
    ppermute x24, waiting for transfers between devices, local(): got = lax.ppermute(send, 'ctx', route)  50.5 us
    pallas_call x5, Pallas kernels, tiled(): pl.pallas_call(functools.partial(kernel, group_width), grid=(channels //...  36.8 us
    dot_general x16, matrix products, local(): jnp.einsum('tn,cn->tc', block, joined, preferred_element_type=F32)  24.5 us
    ppermute x6, starting transfers between devices, ahead(): lax.ppermute(block, axis, [(i - distance, i) for i in devices if i - dist...  11.4 us
    ppermute x3, starting transfers between devices, local(): block = lax.ppermute(block, 'ctx', route)  7.42 us
  transfers between devices with their start and end apart: 40, of which 14 were waited for; matrix products, arithmetic and copies ran while one was open for 16% of the time, Pallas kernels for 10%

profile of v2, /device:TPU:0, one launch (start us, length us, event | category | flops | bytes accessed | tf_op | source)
XLA Modules:
  0.0 354.7 jit_solution(9046912650023786806)
XLA Ops:
  0.0 1.6 slice.207
  2.9 3.0 collective-permute-start
  5.9 4.5 %slice_bitcast_fusion.1 = (bf16[2048,512]{1,0:T(8,128)(2,1)}, bf16[2048,512]{1,0:T(8,128)(2,1)}) fusion(bf16[1,4096,512]{2,1,0:T(8,128)(2,1)} %param.8), kind=kLoop, calls=%fused_computation.14 | loop fusion | bytes 8388608 | tf_op jit(solution)/shard_map/slice | solution.py:154
  10.4 2.6 collective-permute-start.1
  14.2 1.9 fusion
  17.5 4.9 %collective-permute-start.11 = (bf16[134,4096]{1,0:T(8,128)(2,1)}, bf16[134,4096]{1,0:T(8,128)(2,1)}, u32[]{:S(2)}, u32[]{:S(2)}) collective-permute-start(bf16[134,4096]{1,0:T(8,128)(2,1)} %pad_maximum_fusion.4), channel_id=1, source_target_pairs={{0,4},{4,8},{8,12},{12,16},{16,20},{20,24},{24,28},{1,5},{5,9},{9,... | collective-permute-start | bytes 3293192 | tf_op jit(solution)/shard_map/ppermute | solution.py:27
  22.9 1.8 copy-done
  24.7 2.0 slice_bitcast_fusion.5
  27.4 2.0 collective-permute-done
  29.4 1.3 constant_dynamic-update-slice_fusion
  32.6 5.5 %collective-permute-start.2 = (bf16[256,1024]{1,0:T(8,128)(2,1)}, bf16[256,1024]{1,0:T(8,128)(2,1)}, u32[]{:S(2)}, u32[]{:S(2)}) collective-permute-start(bf16[256,1024]{1,0:T(8,128)(2,1)} %pad_maximum_fusion.6), channel_id=1, source_target_pairs={{0,24},{4,28},{8,0},{12,4},{16,8},{20,12},{24,16},{28,20},{1,25},{... | collective-permute-start | bytes 1572872 | tf_op jit(solution)/shard_map/ppermute | solution.py:173
  39.1 87.6 %collective-permute-done.11 = bf16[134,4096]{1,0:T(8,128)(2,1)} collective-permute-done((bf16[134,4096]{1,0:T(8,128)(2,1)}, bf16[134,4096]{1,0:T(8,128)(2,1)}, u32[]{:S(2)}, u32[]{:S(2)}) %collective-permute-start.11) | collective-permute-done | bytes 1097760 | tf_op jit(solution)/shard_map/ppermute | solution.py:27
  126.7 1.8 collective-permute-start.4
  129.5 1.3 slice.208.halo_ref
  130.8 15.2 %shard_map.55 = (f32[256,4096]{1,0:T(8,128)}, f32[3,264,4096]{2,1,0:T(8,128)}) custom-call(bf16[3,256,4096]{2,1,0:T(8,128)(2,1)} %bitcast.78, f32[3,8,4096]{2,1,0:T(8,128)S(1)} %pad_convert_fusion.1.before_ref, f32[3,8,4096]{2,1,0:T(8,128)S(1)} %pad_convert_fusion.after_ref, f32[3,3,4096]{2,1,0:T(4,128)S(1)} %bitcast.72, ...), custom_call_target="tpu_custom_call" | custom-call | flops 4294967296 | bytes 25706496 | tf_op jit(solution)/shard_map/pallas_call | solution.py:113
  146.0 1.8 fusion.20
  147.8 1.8 convolution_convert_fusion.14
  149.7 1.9 convolution_convert_fusion.12
  151.5 1.8 convolution_convert_fusion.10
  153.3 1.8 convolution_convert_fusion.9
  155.1 1.8 convolution_convert_fusion.8
  157.0 3.5 collective-permute-start.15
  161.2 1.3 collective-permute-start.5
  164.2 1.8 convolution_convert_fusion.13
  166.0 1.8 fusion.21
  167.8 1.8 convolution_convert_fusion.6
  169.6 1.9 convolution_convert_fusion.5
  171.5 1.8 convolution_convert_fusion.2
  173.3 1.8 convolution_convert_fusion.1
  175.1 1.8 convolution_convert_fusion.4
  176.8 4.5 %collective-permute-done.5 = bf16[256,1024]{1,0:T(8,128)(2,1)S(1)} collective-permute-done((bf16[256,1024]{1,0:T(8,128)(2,1)S(1)}, bf16[256,1024]{1,0:T(8,128)(2,1)S(1)}, u32[]{:S(2)}, u32[]{:S(2)}) %collective-permute-start.5) | collective-permute-done | bytes 524320 | tf_op jit(solution)/shard_map/ppermute | solution.py:235
  181.7 4.4 %collective-permute-start.6 = (bf16[256,1024]{1,0:T(8,128)(2,1)S(1)}, bf16[256,1024]{1,0:T(8,128)(2,1)S(1)}, u32[]{:S(2)}, u32[]{:S(2)}) collective-permute-start(bf16[256,1024]{1,0:T(8,128)(2,1)S(1)} %get-tuple-element.60), channel_id=1, source_target_pairs={{0,8},{4,12},{8,16},{12,20},{1,9},{5,13},{9,17},{13,21},{2,10},{6,... | collective-permute-start | bytes 1572872 | tf_op jit(solution)/shard_map/ppermute | solution.py:235
  186.1 1.8 convolution_convert_fusion
  189.0 4.8 %collective-permute-start.16 = (bf16[256,1024]{1,0:T(8,128)(2,1)S(1)}, bf16[256,1024]{1,0:T(8,128)(2,1)S(1)}, u32[]{:S(2)}, u32[]{:S(2)}) collective-permute-start(bf16[256,1024]{1,0:T(8,128)(2,1)S(1)} %get-tuple-element.64), channel_id=1, source_target_pairs={{0,8},{4,12},{8,16},{12,20},{1,9},{5,13},{9,17},{13,21},{2,10},{6,... | collective-permute-start | bytes 1572872 | tf_op jit(solution)/shard_map/ppermute | solution.py:235
  194.5 4.0 %collective-permute-done.6 = bf16[256,1024]{1,0:T(8,128)(2,1)S(1)} collective-permute-done((bf16[256,1024]{1,0:T(8,128)(2,1)S(1)}, bf16[256,1024]{1,0:T(8,128)(2,1)S(1)}, u32[]{:S(2)}, u32[]{:S(2)}) %collective-permute-start.6) | collective-permute-done | bytes 524320 | tf_op jit(solution)/shard_map/ppermute | solution.py:235
  198.7 4.4 %collective-permute-start.7 = (bf16[256,1024]{1,0:T(8,128)(2,1)S(1)}, bf16[256,1024]{1,0:T(8,128)(2,1)S(1)}, u32[]{:S(2)}, u32[]{:S(2)}) collective-permute-start(bf16[256,1024]{1,0:T(8,128)(2,1)S(1)} %add_convert_fusion.11), channel_id=1, source_target_pairs={{0,8},{4,12},{8,16},{12,20},{16,24},{20,28},{1,9},{5,13},{9,17},{1... | collective-permute-start | bytes 1572872 | tf_op jit(solution)/shard_map/ppermute | solution.py:235
  203.3 1.3 collective-permute-start.10
  204.6 5.1 %collective-permute-done.16 = bf16[256,1024]{1,0:T(8,128)(2,1)S(1)} collective-permute-done((bf16[256,1024]{1,0:T(8,128)(2,1)S(1)}, bf16[256,1024]{1,0:T(8,128)(2,1)S(1)}, u32[]{:S(2)}, u32[]{:S(2)}) %collective-permute-start.16) | collective-permute-done | bytes 524320 | tf_op jit(solution)/shard_map/ppermute | solution.py:235
  209.9 4.4 %collective-permute-start.17 = (bf16[256,1024]{1,0:T(8,128)(2,1)S(1)}, bf16[256,1024]{1,0:T(8,128)(2,1)S(1)}, u32[]{:S(2)}, u32[]{:S(2)}) collective-permute-start(bf16[256,1024]{1,0:T(8,128)(2,1)S(1)} %add_convert_fusion.8), channel_id=1, source_target_pairs={{0,8},{4,12},{8,16},{12,20},{16,24},{20,28},{1,9},{5,13},{9,17},{1... | collective-permute-start | bytes 1572872 | tf_op jit(solution)/shard_map/ppermute | solution.py:235
  214.5 1.3 collective-permute-start.20
  216.6 6.4 %collective-permute-start.24 = (bf16[256,1024]{1,0:T(8,128)(2,1)S(1)}, bf16[256,1024]{1,0:T(8,128)(2,1)S(1)}, u32[]{:S(2)}, u32[]{:S(2)}) collective-permute-start(bf16[256,1024]{1,0:T(8,128)(2,1)S(1)} %convolution_convert_fusion.4), channel_id=1, source_target_pairs={{0,8},{4,12},{1,9},{5,13},{2,10},{6,14},{3,11},{7,15}} | collective-permute-start | bytes 1572872 | tf_op jit(solution)/shard_map/ppermute | solution.py:235
  223.0 2.4 collective-permute-start.32
  226.4 5.8 %collective-permute-done.17 = bf16[256,1024]{1,0:T(8,128)(2,1)S(1)} collective-permute-done((bf16[256,1024]{1,0:T(8,128)(2,1)S(1)}, bf16[256,1024]{1,0:T(8,128)(2,1)S(1)}, u32[]{:S(2)}, u32[]{:S(2)}) %collective-permute-start.17) | collective-permute-done | bytes 524320 | tf_op jit(solution)/shard_map/ppermute | solution.py:235
  233.2 10.2 %collective-permute-done.24 = bf16[256,1024]{1,0:T(8,128)(2,1)S(1)} collective-permute-done((bf16[256,1024]{1,0:T(8,128)(2,1)S(1)}, bf16[256,1024]{1,0:T(8,128)(2,1)S(1)}, u32[]{:S(2)}, u32[]{:S(2)}) %collective-permute-start.24) | collective-permute-done | bytes 524320 | tf_op jit(solution)/shard_map/ppermute | solution.py:235
  245.2 1.4 fusion.15
  246.7 1.3 collective-permute-start.21
  249.3 1.8 collective-permute-done.32
  252.2 6.2 %collective-permute-start.33 = (bf16[256,1024]{1,0:T(8,128)(2,1)}, bf16[256,1024]{1,0:T(8,128)(2,1)}, u32[]{:S(2)}, u32[]{:S(2)}) collective-permute-start(bf16[256,1024]{1,0:T(8,128)(2,1)} %get-tuple-element.62), channel_id=1, source_target_pairs={{0,8},{4,12},{8,16},{12,20},{1,9},{5,13},{9,17},{13,21},{2,10},{6,... | collective-permute-start | bytes 1572872 | tf_op jit(solution)/shard_map/ppermute | solution.py:235
  258.4 9.1 %collective-permute-start.25 = (bf16[256,1024]{1,0:T(8,128)(2,1)S(1)}, bf16[256,1024]{1,0:T(8,128)(2,1)S(1)}, u32[]{:S(2)}, u32[]{:S(2)}) collective-permute-start(bf16[256,1024]{1,0:T(8,128)(2,1)S(1)} %get-tuple-element.58), channel_id=1, source_target_pairs={{0,8},{4,12},{8,16},{12,20},{1,9},{5,13},{9,17},{13,21},{2,10},{6,... | collective-permute-start | bytes 1572872 | tf_op jit(solution)/shard_map/ppermute | solution.py:235
  267.5 1.5 collective-permute-start.36
  269.0 5.4 %shard_map.57 = bf16[3,256,1024]{2,1,0:T(8,128)(2,1)S(1)} custom-call(bf16[256,1024]{1,0:T(8,128)(2,1)S(1)} %add_convert_fusion.6.grad_ref, bf16[144,1024]{1,0:T(8,128)(2,1)S(1)} %collective-permute-done.21.halo_ref, f32[256,4096]{1,0:T(8,128)} %get-tuple-element.18.conv_ref, f32[3,264,4096]{2,1,0:T(8,128)} %get-tuple-element.17.mix_ref, ...), custom_call_target="tpu_custom_call" | custom-call | flops 1073741824 | bytes 21544960 | tf_op jit(solution)/shard_map/pallas_call | solution.py:113
  274.5 5.4 %shard_map.56 = bf16[3,256,1024]{2,1,0:T(8,128)(2,1)S(1)} custom-call(bf16[256,1024]{1,0:T(8,128)(2,1)S(1)} %add_convert_fusion.9.grad_ref, bf16[144,1024]{1,0:T(8,128)(2,1)S(1)} %collective-permute-done.13.halo_ref, f32[256,4096]{1,0:T(8,128)} %get-tuple-element.18.conv_ref, f32[3,264,4096]{2,1,0:T(8,128)} %get-tuple-element.17.mix_ref, ...), custom_call_target="tpu_custom_call" | custom-call | flops 1073741824 | bytes 21544960 | tf_op jit(solution)/shard_map/pallas_call | solution.py:113
  282.0 2.0 collective-permute-start.34
  286.7 6.5 %collective-permute-start.26 = (bf16[256,1024]{1,0:T(8,128)(2,1)S(1)}, bf16[256,1024]{1,0:T(8,128)(2,1)S(1)}, u32[]{:S(2)}, u32[]{:S(2)}) collective-permute-start(bf16[256,1024]{1,0:T(8,128)(2,1)S(1)} %add_convert_fusion.5), channel_id=1, source_target_pairs={{0,8},{4,12},{8,16},{12,20},{16,24},{20,28},{1,9},{5,13},{9,17},{1... | collective-permute-start | bytes 1572872 | tf_op jit(solution)/shard_map/ppermute | solution.py:235
  293.2 3.0 collective-permute-done.34
  299.0 3.8 %collective-permute-done.37 = bf16[256,1024]{1,0:T(8,128)(2,1)S(1)} collective-permute-done((bf16[256,1024]{1,0:T(8,128)(2,1)S(1)}, bf16[256,1024]{1,0:T(8,128)(2,1)S(1)}, u32[]{:S(2)}, u32[]{:S(2)}) %collective-permute-start.37) | collective-permute-done | bytes 524320 | tf_op jit(solution)/shard_map/ppermute | solution.py:235
  303.1 3.4 collective-permute-done.26
  306.5 8.9 %collective-permute-done.29 = bf16[256,1024]{1,0:T(8,128)(2,1)S(1)} collective-permute-done((bf16[256,1024]{1,0:T(8,128)(2,1)S(1)}, bf16[256,1024]{1,0:T(8,128)(2,1)S(1)}, u32[]{:S(2)}, u32[]{:S(2)}) %collective-permute-start.29) | collective-permute-done | bytes 524320 | tf_op jit(solution)/shard_map/ppermute | solution.py:235
  315.8 1.4 fusion.13
  320.6 16.6 %collective-permute-done.38.halo_ref = bf16[144,1024]{1,0:T(8,128)(2,1)S(1)} collective-permute-done((bf16[144,1024]{1,0:T(8,128)(2,1)S(1)}, bf16[144,1024]{1,0:T(8,128)(2,1)S(1)}, u32[]{:S(2)}, u32[]{:S(2)}) %collective-permute-start.38) | collective-permute-done | bytes 294944 | tf_op jit(solution)/shard_map/ppermute | solution.py:27
  337.3 5.4 %shard_map.59 = bf16[3,256,1024]{2,1,0:T(8,128)(2,1)S(1)} custom-call(bf16[256,1024]{1,0:T(8,128)(2,1)S(1)} %add_convert_fusion.grad_ref, bf16[144,1024]{1,0:T(8,128)(2,1)S(1)} %collective-permute-done.38.halo_ref, f32[256,4096]{1,0:T(8,128)} %get-tuple-element.18.conv_ref, f32[3,264,4096]{2,1,0:T(8,128)} %get-tuple-element.17.mix_ref, ...), custom_call_target="tpu_custom_call" | custom-call | flops 1073741824 | bytes 21544960 | tf_op jit(solution)/shard_map/pallas_call | solution.py:113
  342.8 5.4 %shard_map.58 = bf16[3,256,1024]{2,1,0:T(8,128)(2,1)S(1)} custom-call(bf16[256,1024]{1,0:T(8,128)(2,1)S(1)} %add_convert_fusion.3.grad_ref, bf16[144,1024]{1,0:T(8,128)(2,1)S(1)} %collective-permute-done.30.halo_ref, f32[256,4096]{1,0:T(8,128)} %get-tuple-element.18.conv_ref, f32[3,264,4096]{2,1,0:T(8,128)} %get-tuple-element.17.mix_ref, ...), custom_call_target="tpu_custom_call" | custom-call | flops 1073741824 | bytes 21544960 | tf_op jit(solution)/shard_map/pallas_call | solution.py:113
  348.7 3.0 collective-permute-done.31
  351.8 3.0 maximum_bitcast_fusion
  (125 shorter events, 33.0 us)
Async XLA Ops:
  1.6 25.8 %collective-permute-start.12 = (bf16[3,2,4096]{2,1,0:T(2,128)(2,1)}, bf16[3,2,4096]{2,1,0:T(2,128)(2,1)S(1)}, u32[]{:S(2)}, u32[]{:S(2)}) collective-permute-start(bf16[3,2,4096]{2,1,0:T(2,128)(2,1)} %slice.207), channel_id=1, source_target_pairs={{4,0},{8,4},{12,8},{16,12},{20,16},{24,20},{28,24},{5,1},{9,5},{13... | collective-permute-start | bytes 147464 | tf_op jit(solution)/shard_map/ppermute | solution.py:27
  2.9 10.2 %copy-start.1 = (bf16[1,256,3,4096]{3,1,2,0:T(8,128)(2,1)S(1)}, bf16[1,256,3,4096]{3,1,2,0:T(8,128)(2,1)}, u32[]{:S(2)}) copy-start(bf16[1,256,3,4096]{3,1,2,0:T(8,128)(2,1)} %param.5) | copy-start | bytes 18874372
  2.9 26.5 %collective-permute-start = (bf16[256,2048]{1,0:T(8,128)(2,1)}, bf16[256,2048]{1,0:T(8,128)(2,1)}, u32[]{:S(2)}, u32[]{:S(2)}) collective-permute-start(bf16[256,2048]{1,0:T(8,128)(2,1)} %bitcast.81), channel_id=1, source_target_pairs={{0,2},{2,0},{1,3},{3,1},{4,6},{6,4},{5,7},{7,5},{8,10},{10,8},{9,1... | collective-permute-start | bytes 3145736 | tf_op jit(solution)/shard_map/ppermute | solution.py:149
  10.4 135.6 %collective-permute-start.1 = (bf16[2048,512]{1,0:T(8,128)(2,1)}, bf16[2048,512]{1,0:T(8,128)(2,1)}, u32[]{:S(2)}, u32[]{:S(2)}) collective-permute-start(bf16[2048,512]{1,0:T(8,128)(2,1)} %get-tuple-element.44), channel_id=1, source_target_pairs={{0,4},{4,0},{8,12},{12,8},{16,20},{20,16},{24,28},{28,24},{1,5},{5... | collective-permute-start | bytes 6291464 | tf_op jit(solution)/shard_map/ppermute | solution.py:158
  13.0 152.9 %collective-permute-start.23 = (bf16[2048,512]{1,0:T(8,128)(2,1)}, bf16[2048,512]{1,0:T(8,128)(2,1)}, u32[]{:S(2)}, u32[]{:S(2)}) collective-permute-start(bf16[2048,512]{1,0:T(8,128)(2,1)} %get-tuple-element.45), channel_id=1, source_target_pairs={{0,4},{4,0},{8,12},{12,8},{16,20},{20,16},{24,28},{28,24},{1,5},{5... | collective-permute-start | bytes 6291464 | tf_op jit(solution)/shard_map/ppermute | solution.py:158
  13.1 1.0 copy-start.7
  16.4 6.1 %copy-start.13 = (bf16[1,128,256]{2,1,0:T(8,128)(2,1)S(1)}, bf16[1,128,256]{2,1,0:T(8,128)(2,1)}, u32[]{:S(2)}) copy-start(bf16[1,128,256]{2,1,0:T(8,128)(2,1)} %param.7) | copy-start | bytes 196612
  16.4 6.4 %copy-start.2 = (bf16[1,256,2048]{2,1,0:T(8,128)(2,1)S(1)}, bf16[1,256,2048]{2,1,0:T(8,128)(2,1)}, u32[]{:S(2)}) copy-start(bf16[1,256,2048]{2,1,0:T(8,128)(2,1)} %param.9) | copy-start | bytes 3145732
  17.5 109.3 %collective-permute-start.11 = (bf16[134,4096]{1,0:T(8,128)(2,1)}, bf16[134,4096]{1,0:T(8,128)(2,1)}, u32[]{:S(2)}, u32[]{:S(2)}) collective-permute-start(bf16[134,4096]{1,0:T(8,128)(2,1)} %pad_maximum_fusion.4), channel_id=1, source_target_pairs={{0,4},{4,8},{8,12},{12,16},{16,20},{20,24},{24,28},{1,5},{5,9},{9,... | collective-permute-start | bytes 3293192 | tf_op jit(solution)/shard_map/ppermute | solution.py:27
  22.5 2.2 copy-start
  24.7 2.2 copy-start.8
  31.7 184.2 %copy-start.9 = (bf16[256,512]{1,0:T(8,128)(2,1)}, bf16[256,512]{1,0:T(8,128)(2,1)S(1)}, u32[]{:S(2)}) copy-start(bf16[256,512]{1,0:T(8,128)(2,1)S(1)} %get-tuple-element.50) | copy-start | bytes 786436
  32.6 115.2 %collective-permute-start.2 = (bf16[256,1024]{1,0:T(8,128)(2,1)}, bf16[256,1024]{1,0:T(8,128)(2,1)}, u32[]{:S(2)}, u32[]{:S(2)}) collective-permute-start(bf16[256,1024]{1,0:T(8,128)(2,1)} %pad_maximum_fusion.6), channel_id=1, source_target_pairs={{0,24},{4,28},{8,0},{12,4},{16,8},{20,12},{24,16},{28,20},{1,25},{... | collective-permute-start | bytes 1572872 | tf_op jit(solution)/shard_map/ppermute | solution.py:173
  38.2 115.2 %collective-permute-start.3 = (bf16[256,1024]{1,0:T(8,128)(2,1)S(1)}, bf16[256,1024]{1,0:T(8,128)(2,1)}, u32[]{:S(2)}, u32[]{:S(2)}) collective-permute-start(bf16[256,1024]{1,0:T(8,128)(2,1)S(1)} %pad_maximum_fusion.7), channel_id=1, source_target_pairs={{0,16},{4,20},{8,24},{12,28},{16,0},{20,4},{24,8},{28,12},{1,17},{... | collective-permute-start | bytes 1572872 | tf_op jit(solution)/shard_map/ppermute | solution.py:173
  126.7 22.9 %collective-permute-start.4 = (bf16[256,1024]{1,0:T(8,128)(2,1)}, bf16[256,1024]{1,0:T(8,128)(2,1)}, u32[]{:S(2)}, u32[]{:S(2)}) collective-permute-start(bf16[256,1024]{1,0:T(8,128)(2,1)} %pad_maximum_fusion.8), channel_id=1, source_target_pairs={{0,8},{4,12},{8,16},{12,20},{16,24},{20,28},{24,0},{28,4},{1,9},{5... | collective-permute-start | bytes 1572872 | tf_op jit(solution)/shard_map/ppermute | solution.py:173
  146.0 1.9 copy-start.6
  149.6 1.9 copy-start.5
  155.1 8.3 %copy-start.11 = (bf16[256,512]{1,0:T(8,128)(2,1)S(1)}, bf16[256,512]{1,0:T(8,128)(2,1)}, u32[]{:S(2)}) copy-start(bf16[256,512]{1,0:T(8,128)(2,1)} %get-tuple-element.57) | copy-start | bytes 786436
  157.0 31.7 %collective-permute-start.15 = (bf16[256,1024]{1,0:T(8,128)(2,1)S(1)}, bf16[256,1024]{1,0:T(8,128)(2,1)S(1)}, u32[]{:S(2)}, u32[]{:S(2)}) collective-permute-start(bf16[256,1024]{1,0:T(8,128)(2,1)S(1)} %convolution_convert_fusion.8), channel_id=1, source_target_pairs={{0,8},{4,12},{1,9},{5,13},{2,10},{6,14},{3,11},{7,15}} | collective-permute-start | bytes 1572872 | tf_op jit(solution)/shard_map/ppermute | solution.py:235
  160.5 28.2 %collective-permute-start.18 = (bf16[256,1024]{1,0:T(8,128)(2,1)S(1)}, bf16[256,1024]{1,0:T(8,128)(2,1)S(1)}, u32[]{:S(2)}, u32[]{:S(2)}) collective-permute-start(bf16[256,1024]{1,0:T(8,128)(2,1)S(1)} %convolution_convert_fusion.10), channel_id=1, source_target_pairs={{24,16},{28,20},{25,17},{29,21},{26,18},{30,22},{27,19},{31,23}} | collective-permute-start | bytes 1572872 | tf_op jit(solution)/shard_map/ppermute | solution.py:235
  161.2 20.2 %collective-permute-start.5 = (bf16[256,1024]{1,0:T(8,128)(2,1)S(1)}, bf16[256,1024]{1,0:T(8,128)(2,1)S(1)}, u32[]{:S(2)}, u32[]{:S(2)}) collective-permute-start(bf16[256,1024]{1,0:T(8,128)(2,1)S(1)} %convolution_convert_fusion.12), channel_id=1, source_target_pairs={{0,8},{4,12},{1,9},{5,13},{2,10},{6,14},{3,11},{7,15}} | collective-permute-start | bytes 1572872 | tf_op jit(solution)/shard_map/ppermute | solution.py:235
  162.5 18.9 %collective-permute-start.8 = (bf16[256,1024]{1,0:T(8,128)(2,1)S(1)}, bf16[256,1024]{1,0:T(8,128)(2,1)S(1)}, u32[]{:S(2)}, u32[]{:S(2)}) collective-permute-start(bf16[256,1024]{1,0:T(8,128)(2,1)S(1)} %convolution_convert_fusion.14), channel_id=1, source_target_pairs={{24,16},{28,20},{25,17},{29,21},{26,18},{30,22},{27,19},{31,23}} | collective-permute-start | bytes 1572872 | tf_op jit(solution)/shard_map/ppermute | solution.py:235
  165.9 1.9 copy-start.3
  169.6 1.9 copy-start.4
  181.7 16.8 %collective-permute-start.6 = (bf16[256,1024]{1,0:T(8,128)(2,1)S(1)}, bf16[256,1024]{1,0:T(8,128)(2,1)S(1)}, u32[]{:S(2)}, u32[]{:S(2)}) collective-permute-start(bf16[256,1024]{1,0:T(8,128)(2,1)S(1)} %get-tuple-element.60), channel_id=1, source_target_pairs={{0,8},{4,12},{8,16},{12,20},{1,9},{5,13},{9,17},{13,21},{2,10},{6,... | collective-permute-start | bytes 1572872 | tf_op jit(solution)/shard_map/ppermute | solution.py:235
  187.9 15.2 %collective-permute-start.9 = (bf16[256,1024]{1,0:T(8,128)(2,1)S(1)}, bf16[256,1024]{1,0:T(8,128)(2,1)S(1)}, u32[]{:S(2)}, u32[]{:S(2)}) collective-permute-start(bf16[256,1024]{1,0:T(8,128)(2,1)S(1)} %get-tuple-element.61), channel_id=1, source_target_pairs={{16,8},{20,12},{24,16},{28,20},{17,9},{21,13},{25,17},{29,21},{18,... | collective-permute-start | bytes 1572872 | tf_op jit(solution)/shard_map/ppermute | solution.py:235
  189.0 20.7 %collective-permute-start.16 = (bf16[256,1024]{1,0:T(8,128)(2,1)S(1)}, bf16[256,1024]{1,0:T(8,128)(2,1)S(1)}, u32[]{:S(2)}, u32[]{:S(2)}) collective-permute-start(bf16[256,1024]{1,0:T(8,128)(2,1)S(1)} %get-tuple-element.64), channel_id=1, source_target_pairs={{0,8},{4,12},{8,16},{12,20},{1,9},{5,13},{9,17},{13,21},{2,10},{6,... | collective-permute-start | bytes 1572872 | tf_op jit(solution)/shard_map/ppermute | solution.py:235
  193.8 20.6 %collective-permute-start.19 = (bf16[256,1024]{1,0:T(8,128)(2,1)S(1)}, bf16[256,1024]{1,0:T(8,128)(2,1)S(1)}, u32[]{:S(2)}, u32[]{:S(2)}) collective-permute-start(bf16[256,1024]{1,0:T(8,128)(2,1)S(1)} %get-tuple-element.65), channel_id=1, source_target_pairs={{16,8},{20,12},{24,16},{28,20},{17,9},{21,13},{25,17},{29,21},{18,... | collective-permute-start | bytes 1572872 | tf_op jit(solution)/shard_map/ppermute | solution.py:235
  198.7 24.3 %collective-permute-start.7 = (bf16[256,1024]{1,0:T(8,128)(2,1)S(1)}, bf16[256,1024]{1,0:T(8,128)(2,1)S(1)}, u32[]{:S(2)}, u32[]{:S(2)}) collective-permute-start(bf16[256,1024]{1,0:T(8,128)(2,1)S(1)} %add_convert_fusion.11), channel_id=1, source_target_pairs={{0,8},{4,12},{8,16},{12,20},{16,24},{20,28},{1,9},{5,13},{9,17},{1... | collective-permute-start | bytes 1572872 | tf_op jit(solution)/shard_map/ppermute | solution.py:235
  203.3 22.1 %collective-permute-start.10 = (bf16[256,1024]{1,0:T(8,128)(2,1)S(1)}, bf16[256,1024]{1,0:T(8,128)(2,1)S(1)}, u32[]{:S(2)}, u32[]{:S(2)}) collective-permute-start(bf16[256,1024]{1,0:T(8,128)(2,1)S(1)} %add_convert_fusion.10), channel_id=1, source_target_pairs={{8,0},{12,4},{16,8},{20,12},{24,16},{28,20},{9,1},{13,5},{17,9},{2... | collective-permute-start | bytes 1572872 | tf_op jit(solution)/shard_map/ppermute | solution.py:235
  209.9 22.3 %collective-permute-start.17 = (bf16[256,1024]{1,0:T(8,128)(2,1)S(1)}, bf16[256,1024]{1,0:T(8,128)(2,1)S(1)}, u32[]{:S(2)}, u32[]{:S(2)}) collective-permute-start(bf16[256,1024]{1,0:T(8,128)(2,1)S(1)} %add_convert_fusion.8), channel_id=1, source_target_pairs={{0,8},{4,12},{8,16},{12,20},{16,24},{20,28},{1,9},{5,13},{9,17},{1... | collective-permute-start | bytes 1572872 | tf_op jit(solution)/shard_map/ppermute | solution.py:235
  214.5 18.3 %collective-permute-start.20 = (bf16[256,1024]{1,0:T(8,128)(2,1)S(1)}, bf16[256,1024]{1,0:T(8,128)(2,1)S(1)}, u32[]{:S(2)}, u32[]{:S(2)}) collective-permute-start(bf16[256,1024]{1,0:T(8,128)(2,1)S(1)} %add_convert_fusion.7), channel_id=1, source_target_pairs={{8,0},{12,4},{16,8},{20,12},{24,16},{28,20},{9,1},{13,5},{17,9},{2... | collective-permute-start | bytes 1572872 | tf_op jit(solution)/shard_map/ppermute | solution.py:235
  216.6 26.8 %collective-permute-start.24 = (bf16[256,1024]{1,0:T(8,128)(2,1)S(1)}, bf16[256,1024]{1,0:T(8,128)(2,1)S(1)}, u32[]{:S(2)}, u32[]{:S(2)}) collective-permute-start(bf16[256,1024]{1,0:T(8,128)(2,1)S(1)} %convolution_convert_fusion.4), channel_id=1, source_target_pairs={{0,8},{4,12},{1,9},{5,13},{2,10},{6,14},{3,11},{7,15}} | collective-permute-start | bytes 1572872 | tf_op jit(solution)/shard_map/ppermute | solution.py:235
  223.0 28.1 %collective-permute-start.32 = (bf16[256,1024]{1,0:T(8,128)(2,1)S(1)}, bf16[256,1024]{1,0:T(8,128)(2,1)S(1)}, u32[]{:S(2)}, u32[]{:S(2)}) collective-permute-start(bf16[256,1024]{1,0:T(8,128)(2,1)S(1)} %convolution_convert_fusion), channel_id=1, source_target_pairs={{0,8},{4,12},{1,9},{5,13},{2,10},{6,14},{3,11},{7,15}} | collective-permute-start | bytes 1572872 | tf_op jit(solution)/shard_map/ppermute | solution.py:235
  225.4 18.0 %collective-permute-start.27 = (bf16[256,1024]{1,0:T(8,128)(2,1)S(1)}, bf16[256,1024]{1,0:T(8,128)(2,1)S(1)}, u32[]{:S(2)}, u32[]{:S(2)}) collective-permute-start(bf16[256,1024]{1,0:T(8,128)(2,1)S(1)} %convolution_convert_fusion.6), channel_id=1, source_target_pairs={{24,16},{28,20},{25,17},{29,21},{26,18},{30,22},{27,19},{31,23}} | collective-permute-start | bytes 1572872 | tf_op jit(solution)/shard_map/ppermute | solution.py:235
  232.2 18.9 %collective-permute-start.35 = (bf16[256,1024]{1,0:T(8,128)(2,1)S(1)}, bf16[256,1024]{1,0:T(8,128)(2,1)S(1)}, u32[]{:S(2)}, u32[]{:S(2)}) collective-permute-start(bf16[256,1024]{1,0:T(8,128)(2,1)S(1)} %convolution_convert_fusion.2), channel_id=1, source_target_pairs={{24,16},{28,20},{25,17},{29,21},{26,18},{30,22},{27,19},{31,23}} | collective-permute-start | bytes 1572872 | tf_op jit(solution)/shard_map/ppermute | solution.py:235
  243.8 36.2 %collective-permute-start.28 = (bf16[256,1024]{1,0:T(8,128)(2,1)S(1)}, bf16[256,1024]{1,0:T(8,128)(2,1)S(1)}, u32[]{:S(2)}, u32[]{:S(2)}) collective-permute-start(bf16[256,1024]{1,0:T(8,128)(2,1)S(1)} %get-tuple-element.59), channel_id=1, source_target_pairs={{16,8},{20,12},{24,16},{28,20},{17,9},{21,13},{25,17},{29,21},{18,... | collective-permute-start | bytes 1572872 | tf_op jit(solution)/shard_map/ppermute | solution.py:235
  246.7 20.8 %collective-permute-start.21 = (bf16[144,1024]{1,0:T(8,128)(2,1)S(1)}, bf16[144,1024]{1,0:T(8,128)(2,1)S(1)}, u32[]{:S(2)}, u32[]{:S(2)}) collective-permute-start(bf16[144,1024]{1,0:T(8,128)(2,1)S(1)} %pad_maximum_fusion.10), channel_id=1, source_target_pairs={{4,0},{8,4},{12,8},{16,12},{20,16},{24,20},{28,24},{5,1},{9,5},{13... | collective-permute-start | bytes 884744 | tf_op jit(solution)/shard_map/ppermute | solution.py:27
  248.0 26.4 %collective-permute-start.13 = (bf16[144,1024]{1,0:T(8,128)(2,1)S(1)}, bf16[144,1024]{1,0:T(8,128)(2,1)S(1)}, u32[]{:S(2)}, u32[]{:S(2)}) collective-permute-start(bf16[144,1024]{1,0:T(8,128)(2,1)S(1)} %pad_maximum_fusion.9), channel_id=1, source_target_pairs={{4,0},{8,4},{12,8},{16,12},{20,16},{24,20},{28,24},{5,1},{9,5},{13... | collective-permute-start | bytes 884744 | tf_op jit(solution)/shard_map/ppermute | solution.py:27
  252.2 28.5 %collective-permute-start.33 = (bf16[256,1024]{1,0:T(8,128)(2,1)}, bf16[256,1024]{1,0:T(8,128)(2,1)}, u32[]{:S(2)}, u32[]{:S(2)}) collective-permute-start(bf16[256,1024]{1,0:T(8,128)(2,1)} %get-tuple-element.62), channel_id=1, source_target_pairs={{0,8},{4,12},{8,16},{12,20},{1,9},{5,13},{9,17},{13,21},{2,10},{6,... | collective-permute-start | bytes 1572872 | tf_op jit(solution)/shard_map/ppermute | solution.py:235
  258.4 28.2 %collective-permute-start.25 = (bf16[256,1024]{1,0:T(8,128)(2,1)S(1)}, bf16[256,1024]{1,0:T(8,128)(2,1)S(1)}, u32[]{:S(2)}, u32[]{:S(2)}) collective-permute-start(bf16[256,1024]{1,0:T(8,128)(2,1)S(1)} %get-tuple-element.58), channel_id=1, source_target_pairs={{0,8},{4,12},{8,16},{12,20},{1,9},{5,13},{9,17},{13,21},{2,10},{6,... | collective-permute-start | bytes 1572872 | tf_op jit(solution)/shard_map/ppermute | solution.py:235
  267.5 16.5 %collective-permute-start.36 = (bf16[256,1024]{1,0:T(8,128)(2,1)S(1)}, bf16[256,1024]{1,0:T(8,128)(2,1)}, u32[]{:S(2)}, u32[]{:S(2)}) collective-permute-start(bf16[256,1024]{1,0:T(8,128)(2,1)S(1)} %get-tuple-element.63), channel_id=1, source_target_pairs={{16,8},{20,12},{24,16},{28,20},{17,9},{21,13},{25,17},{29,21},{18,... | collective-permute-start | bytes 1572872 | tf_op jit(solution)/shard_map/ppermute | solution.py:235
  274.4 41.3 %collective-permute-start.22 = (bf16[3,256,1024]{2,1,0:T(8,128)(2,1)S(1)}, bf16[3,256,1024]{2,1,0:T(8,128)(2,1)S(1)}, u32[]{:S(2)}, u32[]{:S(2)}) collective-permute-start(bf16[3,256,1024]{2,1,0:T(8,128)(2,1)S(1)} %shard_map.57), channel_id=1, source_target_pairs={{0,1},{1,0},{2,3},{3,2},{4,5},{5,4},{6,7},{7,6},{8,9},{9,8},{10,11... | collective-permute-start | bytes 4718600 | tf_op jit(solution)/shard_map/ppermute | solution.py:268
  279.9 35.8 %collective-permute-start.14 = (bf16[3,256,1024]{2,1,0:T(8,128)(2,1)S(1)}, bf16[3,256,1024]{2,1,0:T(8,128)(2,1)S(1)}, u32[]{:S(2)}, u32[]{:S(2)}) collective-permute-start(bf16[3,256,1024]{2,1,0:T(8,128)(2,1)S(1)} %shard_map.56), channel_id=1, source_target_pairs={{0,1},{1,0},{2,3},{3,2},{4,5},{5,4},{6,7},{7,6},{8,9},{9,8},{10,11... | collective-permute-start | bytes 4718600 | tf_op jit(solution)/shard_map/ppermute | solution.py:268
  280.7 16.8 %copy-start.10 = (bf16[256,512]{1,0:T(8,128)(2,1)S(1)}, bf16[256,512]{1,0:T(8,128)(2,1)}, u32[]{:S(2)}) copy-start(bf16[256,512]{1,0:T(8,128)(2,1)} %copy-done.9) | copy-start | bytes 786436
  280.7 16.8 %copy-start.12 = (bf16[256,512]{1,0:T(8,128)(2,1)S(1)}, bf16[256,512]{1,0:T(8,128)(2,1)}, u32[]{:S(2)}) copy-start(bf16[256,512]{1,0:T(8,128)(2,1)} %get-tuple-element.57) | copy-start | bytes 786436
  282.0 14.2 %collective-permute-start.34 = (bf16[256,1024]{1,0:T(8,128)(2,1)S(1)}, bf16[256,1024]{1,0:T(8,128)(2,1)S(1)}, u32[]{:S(2)}, u32[]{:S(2)}) collective-permute-start(bf16[256,1024]{1,0:T(8,128)(2,1)S(1)} %add_convert_fusion.2), channel_id=1, source_target_pairs={{0,8},{4,12},{8,16},{12,20},{16,24},{20,28},{1,9},{5,13},{9,17},{1... | collective-permute-start | bytes 1572872 | tf_op jit(solution)/shard_map/ppermute | solution.py:235
  285.2 17.6 %collective-permute-start.37 = (bf16[256,1024]{1,0:T(8,128)(2,1)S(1)}, bf16[256,1024]{1,0:T(8,128)(2,1)S(1)}, u32[]{:S(2)}, u32[]{:S(2)}) collective-permute-start(bf16[256,1024]{1,0:T(8,128)(2,1)S(1)} %add_convert_fusion.1), channel_id=1, source_target_pairs={{8,0},{12,4},{16,8},{20,12},{24,16},{28,20},{9,1},{13,5},{17,9},{2... | collective-permute-start | bytes 1572872 | tf_op jit(solution)/shard_map/ppermute | solution.py:235
  286.7 19.8 %collective-permute-start.26 = (bf16[256,1024]{1,0:T(8,128)(2,1)S(1)}, bf16[256,1024]{1,0:T(8,128)(2,1)S(1)}, u32[]{:S(2)}, u32[]{:S(2)}) collective-permute-start(bf16[256,1024]{1,0:T(8,128)(2,1)S(1)} %add_convert_fusion.5), channel_id=1, source_target_pairs={{0,8},{4,12},{8,16},{12,20},{16,24},{20,28},{1,9},{5,13},{9,17},{1... | collective-permute-start | bytes 1572872 | tf_op jit(solution)/shard_map/ppermute | solution.py:235
  296.2 19.2 %collective-permute-start.29 = (bf16[256,1024]{1,0:T(8,128)(2,1)S(1)}, bf16[256,1024]{1,0:T(8,128)(2,1)S(1)}, u32[]{:S(2)}, u32[]{:S(2)}) collective-permute-start(bf16[256,1024]{1,0:T(8,128)(2,1)S(1)} %add_convert_fusion.4), channel_id=1, source_target_pairs={{8,0},{12,4},{16,8},{20,12},{24,16},{28,20},{9,1},{13,5},{17,9},{2... | collective-permute-start | bytes 1572872 | tf_op jit(solution)/shard_map/ppermute | solution.py:235
  318.0 19.3 %collective-permute-start.38 = (bf16[144,1024]{1,0:T(8,128)(2,1)S(1)}, bf16[144,1024]{1,0:T(8,128)(2,1)S(1)}, u32[]{:S(2)}, u32[]{:S(2)}) collective-permute-start(bf16[144,1024]{1,0:T(8,128)(2,1)S(1)} %pad_maximum_fusion.12), channel_id=1, source_target_pairs={{4,0},{8,4},{12,8},{16,12},{20,16},{24,20},{28,24},{5,1},{9,5},{13... | collective-permute-start | bytes 884744 | tf_op jit(solution)/shard_map/ppermute | solution.py:27
  319.3 23.4 %collective-permute-start.30 = (bf16[144,1024]{1,0:T(8,128)(2,1)S(1)}, bf16[144,1024]{1,0:T(8,128)(2,1)S(1)}, u32[]{:S(2)}, u32[]{:S(2)}) collective-permute-start(bf16[144,1024]{1,0:T(8,128)(2,1)S(1)} %pad_maximum_fusion.11), channel_id=1, source_target_pairs={{4,0},{8,4},{12,8},{16,12},{20,16},{24,20},{28,24},{5,1},{9,5},{13... | collective-permute-start | bytes 884744 | tf_op jit(solution)/shard_map/ppermute | solution.py:27
  342.7 6.1 %collective-permute-start.39 = (bf16[3,256,1024]{2,1,0:T(8,128)(2,1)S(1)}, bf16[3,256,1024]{2,1,0:T(8,128)(2,1)S(1)}, u32[]{:S(2)}, u32[]{:S(2)}) collective-permute-start(bf16[3,256,1024]{2,1,0:T(8,128)(2,1)S(1)} %shard_map.59), channel_id=1, source_target_pairs={{0,1},{1,0},{2,3},{3,2},{4,5},{5,4},{6,7},{7,6},{8,9},{9,8},{10,11... | collective-permute-start | bytes 4718600 | tf_op jit(solution)/shard_map/ppermute | solution.py:268
  348.2 3.6 %collective-permute-start.31 = (bf16[3,256,1024]{2,1,0:T(8,128)(2,1)S(1)}, bf16[3,256,1024]{2,1,0:T(8,128)(2,1)S(1)}, u32[]{:S(2)}, u32[]{:S(2)}) collective-permute-start(bf16[3,256,1024]{2,1,0:T(8,128)(2,1)S(1)} %shard_map.58), channel_id=1, source_target_pairs={{0,1},{1,0},{2,3},{3,2},{4,5},{5,4},{6,7},{7,6},{8,9},{9,8},{10,11... | collective-permute-start | bytes 4718600 | tf_op jit(solution)/shard_map/ppermute | solution.py:268

commit v3 on v2

--- a/solution.py
+++ b/solution.py
@@ -149,9 +149,18 @@
         got = lax.ppermute(cotangent, "tp", [(i, (i + s) % tp_count) for i in range(tp_count)])
         full = lax.dynamic_update_slice(full, got, (0, (tp_place - s) % tp_count * share))
 
+    streams = jnp.transpose(feats, (1, 0, 2))
+    tail_f = streams[:, rows - reach - 2 :].astype(F32)
+    by_tap = taps[:, :, None]
+    tail_mix = by_tap[0] * tail_f[:, 2:] + by_tap[1] * tail_f[:, 1:-1] + by_tap[2] * tail_f[:, :-2]
+    prod_tail = (tail_mix[1] * tail_mix[2]).astype(BF16)
+    packed = jnp.concatenate([prod_tail] + [streams[i, rows - 2 :] for i in range(3)], axis=0)
+    arrived = ahead(packed, "ctx", 1)
+
     weights = []
     for w in range(waves):
         mine = weight[w * stretch : (w + 1) * stretch]
+        mine = after(mine, weights[-1][-1] if w else packed)
         held = [mine]
         for s in range(1, inner):
             route = [(zz * inner + xx, zz * inner + (xx + s) % inner) for zz, xx in cells]
@@ -173,15 +182,8 @@
             block = lax.ppermute(block, "ctx", route)
         tokens.append(block)
 
-    streams = jnp.transpose(feats, (1, 0, 2))
-    tail_f = streams[:, rows - reach - 2 :].astype(F32)
-    by_tap = taps[:, :, None]
-    tail_mix = by_tap[0] * tail_f[:, 2:] + by_tap[1] * tail_f[:, 1:-1] + by_tap[2] * tail_f[:, :-2]
-    prod_tail = (tail_mix[1] * tail_mix[2]).astype(BF16)
-    packed = jnp.concatenate([prod_tail] + [streams[i, rows - 2 :] for i in range(3)], axis=0)
-    packed = ahead(packed, "ctx", 1)
-    prod_halo = packed[:reach]
-    before = jnp.pad(packed[reach:].reshape(3, 2, channels).astype(F32), ((0, 0), (TAIL - 2, 0), (0, 0)))
+    prod_halo = arrived[:reach]
+    before = jnp.pad(arrived[reach:].reshape(3, 2, channels).astype(F32), ((0, 0), (TAIL - 2, 0), (0, 0)))
     behind = ahead(streams[:, :2], "ctx", -1)
     behind = jnp.pad(behind.astype(F32), ((0, 0), (0, TAIL - 2), (0, 0)))
     by_group = jnp.transpose(filters).astype(F32)
@@ -189,83 +191,100 @@
     backward_rows = jnp.concatenate([by_group, blank], axis=1)
     forward_rows = jnp.concatenate([by_group[:, ::-1], blank], axis=1)
     flops = 2 * groups * reach * 4 * reach * LANES
-    conv, mix = tiled(
-        forward_kernel,
-        [
-            (streams, False, 0),
-            (before, False, 0),
-            (behind, False, 0),
-            (taps, False, 0),
-            (forward_rows, True, 0),
-            (prod_halo, False, 0),
-        ],
-        [jax.ShapeDtypeStruct((rows, channels), F32), jax.ShapeDtypeStruct((3, rows + TAIL, channels), F32)],
-        channels,
-        width,
-        flops,
-    )
-
-    results = []
-    halos = []
-    gate_order = {}
-    per_wave = chunks // waves
-    for k in range(chunks):
-        lo, hi = k * piece, (k + 1) * piece
-        wave, at = k // per_wave, k % per_wave
+
+    def forward(wave, *others):
+        start = wave * stretch
+        return tiled(
+            forward_kernel,
+            [
+                (after(streams, *others), False, start),
+                (before, False, start),
+                (behind, False, start),
+                (taps, False, start),
+                (forward_rows, True, start),
+                (prod_halo, False, start),
+            ],
+            [
+                jax.ShapeDtypeStruct((rows, stretch), F32),
+                jax.ShapeDtypeStruct((3, rows + TAIL, stretch), F32),
+            ],
+            stretch,
+            width,
+            flops // waves,
+        )
+
+    def partials(wave, at):
         joined = jnp.concatenate([h[at * piece : (at + 1) * piece] for h in weights[wave]], axis=1)
-        partial = [
+        return [
             lax.optimization_barrier(
                 jnp.einsum("tn,cn->tc", block, joined, preferred_element_type=F32).astype(BF16)
             )
             for block in tokens
         ]
-        total = partial[0].astype(F32)
-        for sign in (1, -1):
-            got = None
-            for j in range(outer - 1):
-                send = partial[j + 1] if sign == 1 else partial[outer - 1 - j]
-                if got is not None:
-                    send = (send.astype(F32) + got.astype(F32)).astype(BF16)
-                    if wave and j == outer - 2:
-                        send = after(send, halos[k - per_wave])
-                elif wave:
-                    send = after(send, gate_order[wave - 1, at, sign])
-                sources = range(j + 1) if sign == 1 else range(outer - 1 - j, outer)
-                route = [(zz * inner + xx, (zz + sign) * inner + xx) for zz in sources for xx in range(inner)]
-                got = lax.ppermute(send, "ctx", route)
-                if j == outer - 3:
-                    gate_order[wave, at, sign] = got
-            total = total + got.astype(F32)
-        grad_y = total.astype(BF16)
-        if wave:
-            grad_y = after(grad_y, results[k - per_wave])
-        top = grad_y[: reach + 8].astype(F32)
-        halo = jnp.concatenate(
-            [
-                (top * mix[0, : reach + 8, lo:hi]).astype(BF16),
-                (top[:TAIL] * conv[:TAIL, lo:hi]).astype(BF16),
-            ],
-            axis=0,
-        )
-        halos.append(halo)
-        halo = ahead(halo, "ctx", -1)
-        (out,) = tiled(
-            backward_kernel,
-            [
-                (grad_y, False, 0),
-                (halo, False, 0),
-                (conv, False, lo),
-                (mix, False, lo),
-                (taps, False, lo),
-                (backward_rows, True, lo),
-            ],
-            [jax.ShapeDtypeStruct((3, rows, piece), BF16)],
-            piece,
-            width,
-            flops // chunks,
-        )
-        count = lax.axis_size("pp")
-        results.append(lax.ppermute(out, "pp", [(i, (i - 1) % count) for i in range(count)]))
+
+    results, halos = [], []
+    per_wave = chunks // waves
+    middle = [None] * per_wave
+    every = [[partials(wave, at) for at in range(per_wave)] for wave in range(waves)]
+    for wave in range(waves):
+        parts = every[wave]
+        conv, mix = forward(wave, *(middle[-1] if wave else parts[-1][1:]))
+        sums = []
+        for at in range(per_wave):
+            total = parts[at][0].astype(F32)
+            steps = []
+            for sign in (1, -1):
+                got = None
+                for j in range(outer - 1):
+                    send = parts[at][j + 1] if sign == 1 else parts[at][outer - 1 - j]
+                    if got is not None:
+                        send = (send.astype(F32) + got.astype(F32)).astype(BF16)
+                        if wave and j == outer - 2:
+                            send = after(send, halos[(wave - 1) * per_wave + at])
+                        if wave + 1 < waves and j == outer - 2:
+                            send = after(send, every[wave + 1][at][1], every[wave + 1][at][outer - 1])
+                    elif wave:
+                        send = after(send, middle[at][sign < 0])
+                    sources = range(j + 1) if sign == 1 else range(outer - 1 - j, outer)
+                    route = [(zz * inner + xx, (zz + sign) * inner + xx) for zz in sources for xx in range(inner)]
+                    got = lax.ppermute(send, "ctx", route)
+                    if j == max(0, outer - 3):
+                        steps.append(got)
+                total = total + got.astype(F32)
+            middle[at] = steps
+            sums.append(total.astype(BF16))
+        ready = results[-per_wave:]
+        for at in range(per_wave):
+            lo = wave * stretch + at * piece
+            here = slice(at * piece, (at + 1) * piece)
+            grad_y = after(sums[at], ready[at]) if wave else sums[at]
+            top = grad_y[: reach + 8].astype(F32)
+            halo = jnp.concatenate(
+                [
+                    (top * mix[0, : reach + 8, here]).astype(BF16),
+                    (top[:TAIL] * conv[:TAIL, here]).astype(BF16),
+                ],
+                axis=0,
+            )
+            halos.append(halo)
+            halo = ahead(halo, "ctx", -1)
+            (out,) = tiled(
+                backward_kernel,
+                [
+                    (grad_y, False, 0),
+                    (halo, False, 0),
+                    (conv, False, at * piece),
+                    (mix, False, at * piece),
+                    (taps, False, lo),
+                    (backward_rows, True, lo),
+                ],
+                [jax.ShapeDtypeStruct((3, rows, piece), BF16)],
+                piece,
+                width,
+                flops // chunks,
+            )
+            count = lax.axis_size("pp")
+            results.append(lax.ppermute(out, "pp", [(i, (i - 1) % count) for i in range(count)]))
     return jnp.transpose(jnp.concatenate(results, axis=2), (1, 0, 2))[None]
 
 

time: 358 us -> 307 us (0.86)
  waiting for transfers between devices: 160 us -> 112 us
  starting transfers between devices: 92.7 us -> 83.2 us
  other arithmetic: 20.5 us -> 26.7 us
    ppermute x6, waiting for transfers between devices: 104 us -> 13.9 us  [ahead(): lax.ppermute(block, axis, [(i - distance, i) for i in devices if i - dist...]
    ppermute x2, waiting for transfers between devices: 0.01 us -> 47.1 us  [local(): held.append(lax.ppermute(mine, 'ctx', route))]
    ppermute x24, starting transfers between devices: 67 us -> 58.8 us  [local(): got = lax.ppermute(send, 'ctx', route)]
    convert_element_type x12, other arithmetic: 5.75 us -> 13.2 us  [local(): send = (send.astype(F32) + got.astype(F32)).astype(BF16)]
    ppermute x24, waiting for transfers between devices: 50.5 us -> 45 us  [local(): got = lax.ppermute(send, 'ctx', route)]
    pallas_call x5 -> x6, Pallas kernels: 36.8 us -> 38.9 us  [tiled(): pl.pallas_call(functools.partial(kernel, group_width), grid=(channels //...]
    slice x5 -> x6, local copies, waits for them, and re-layouts: 7.71 us -> 7.23 us  [the longest x4 5.08 us: partials(): h[at * piece:(at + 1) * piece]]
  transfers between devices with their start and end apart: 40 -> 40, of which waited for: 14 -> 15; matrix products, arithmetic and copies ran while one was open for 16% -> 20% of each run, Pallas kernels for 10% -> 13%
where the time goes in v3:
time: 307 us; the launch traced here: 305 us
  waiting for transfers between devices  112 us (36%)
  starting transfers between devices  83.2 us (27%)
  Pallas kernels  38.9 us (13%)
  matrix products  28 us (9%)
  other arithmetic  26.7 us (9%)
  local copies, waits for them, and re-layouts  15.6 us (5%)
    ppermute x24, starting transfers between devices, local(): got = lax.ppermute(send, 'ctx', route)  58.8 us
    ppermute x2, waiting for transfers between devices, local(): held.append(lax.ppermute(mine, 'ctx', route))  47.1 us
    ppermute x24, waiting for transfers between devices, local(): got = lax.ppermute(send, 'ctx', route)  45 us
    pallas_call x6, Pallas kernels, tiled(): pl.pallas_call(functools.partial(kernel, group_width), grid=(channels //...  38.9 us
    dot_general x16, matrix products, partials(): jnp.einsum('tn,cn->tc', block, joined, preferred_element_type=F32)  28 us
    ppermute x6, waiting for transfers between devices, ahead(): lax.ppermute(block, axis, [(i - distance, i) for i in devices if i - dist...  13.9 us
    convert_element_type x12, other arithmetic, local(): send = (send.astype(F32) + got.astype(F32)).astype(BF16)  13.2 us
    ppermute x6, starting transfers between devices, ahead(): lax.ppermute(block, axis, [(i - distance, i) for i in devices if i - dist...  12.1 us
  transfers between devices with their start and end apart: 40, of which 15 were waited for; matrix products, arithmetic and copies ran while one was open for 20% of the time, Pallas kernels for 13%

profile of v3, /device:TPU:0, one launch (start us, length us, event | category | flops | bytes accessed | tf_op | source)
XLA Modules:
  0.0 305.2 jit_solution(2906960599993277050)
XLA Ops:
  2.3 3.0 collective-permute-start
  6.3 2.9 slice_convert_fusion
  9.3 1.9 fusion
  12.6 5.7 %collective-permute-start.12 = (bf16[134,4096]{1,0:T(8,128)(2,1)}, bf16[134,4096]{1,0:T(8,128)(2,1)}, u32[]{:S(2)}, u32[]{:S(2)}) collective-permute-start(bf16[134,4096]{1,0:T(8,128)(2,1)} %pad_maximum_fusion.4), channel_id=1, source_target_pairs={{0,4},{4,8},{8,12},{12,16},{16,20},{20,24},{24,28},{1,5},{5,9},{9,... | collective-permute-start | bytes 3293192 | tf_op jit(solution)/shard_map/ppermute | solution.py:27
  18.3 2.3 slice_bitcast_fusion.1
  20.5 1.4 collective-permute-start.1
  22.3 3.1 %fusion.20 = (bf16[1024,512]{1,0:T(8,128)(2,1)}, bf16[1024,512]{1,0:T(8,128)(2,1)}) fusion(bf16[2048,512]{1,0:T(8,128)(2,1)} %get-tuple-element.27), kind=kLoop, calls=%fused_computation.109 | loop fusion | bytes 4194304 | tf_op jit(solution)/shard_map/slice | solution.py:217
  26.2 2.5 collective-permute-done
  31.1 5.6 %collective-permute-start.2 = (bf16[256,1024]{1,0:T(8,128)(2,1)S(1)}, bf16[256,1024]{1,0:T(8,128)(2,1)}, u32[]{:S(2)}, u32[]{:S(2)}) collective-permute-start(bf16[256,1024]{1,0:T(8,128)(2,1)S(1)} %pad_maximum_fusion.6), channel_id=1, source_target_pairs={{0,24},{4,28},{8,0},{12,4},{16,8},{20,12},{24,16},{28,20},{1,25},{... | collective-permute-start | bytes 1572872 | tf_op jit(solution)/shard_map/ppermute | solution.py:182
  37.9 4.6 %collective-permute-done.12 = bf16[134,4096]{1,0:T(8,128)(2,1)} collective-permute-done((bf16[134,4096]{1,0:T(8,128)(2,1)}, bf16[134,4096]{1,0:T(8,128)(2,1)}, u32[]{:S(2)}, u32[]{:S(2)}) %collective-permute-start.12) | collective-permute-done | bytes 1097760 | tf_op jit(solution)/shard_map/ppermute | solution.py:27
  44.9 40.9 %collective-permute-done.1 = bf16[2048,512]{1,0:T(8,128)(2,1)} collective-permute-done((bf16[2048,512]{1,0:T(8,128)(2,1)}, bf16[2048,512]{1,0:T(8,128)(2,1)}, u32[]{:S(2)}, u32[]{:S(2)}) %collective-permute-start.1) | collective-permute-done | bytes 2097184 | tf_op jit(solution)/shard_map/ppermute | solution.py:167
  85.8 1.7 fusion.21
  87.5 1.8 convolution_convert_fusion.14
  89.3 1.9 convolution_convert_fusion.12
  91.2 1.8 convolution_convert_fusion.7
  92.9 1.9 convolution_convert_fusion.9
  94.9 6.3 %collective-permute-start.16 = (bf16[256,1024]{1,0:T(8,128)(2,1)S(1)}, bf16[256,1024]{1,0:T(8,128)(2,1)S(1)}, u32[]{:S(2)}, u32[]{:S(2)}) collective-permute-start(bf16[256,1024]{1,0:T(8,128)(2,1)S(1)} %convolution_convert_fusion.9), channel_id=1, source_target_pairs={{0,8},{4,12},{1,9},{5,13},{2,10},{6,14},{3,11},{7,15}} | collective-permute-start | bytes 1572872 | tf_op jit(solution)/shard_map/ppermute | solution.py:250
  101.8 2.2 collective-permute-start.5
  104.0 1.5 collective-permute-start.9
  105.5 2.6 convolution_convert_fusion.13
  108.1 1.8 convolution_convert_fusion.8
  110.9 1.6 convolution_convert_fusion.15
  114.5 5.2 %collective-permute-start.17 = (bf16[256,1024]{1,0:T(8,128)(2,1)}, bf16[256,1024]{1,0:T(8,128)(2,1)}, u32[]{:S(2)}, u32[]{:S(2)}) collective-permute-start(bf16[256,1024]{1,0:T(8,128)(2,1)} %get-tuple-element.84), channel_id=1, source_target_pairs={{0,8},{4,12},{8,16},{12,20},{1,9},{5,13},{9,17},{13,21},{2,10},{6,... | collective-permute-start | bytes 1572872 | tf_op jit(solution)/shard_map/ppermute | solution.py:250
  119.7 1.4 collective-permute-start.20
  121.2 1.6 convolution_convert_fusion.6
  122.8 8.8 %shard_map.55 = (f32[256,2048]{1,0:T(8,128)S(1)}, f32[3,264,2048]{2,1,0:T(8,128)}) custom-call(bf16[3,256,4096]{2,1,0:T(8,128)(2,1)} %bitcast.73, f32[3,8,4096]{2,1,0:T(8,128)S(1)} %pad_convert_fusion.1.before_ref, f32[3,8,4096]{2,1,0:T(8,128)S(1)} %pad_convert_fusion.after_ref, f32[3,3,4096]{2,1,0:T(4,128)S(1)} %bitcast.64, ...), custom_call_target="tpu_custom_call" | custom-call | flops 2147483648 | bytes 17121280 | tf_op jit(solution)/shard_map/pallas_call | solution.py:113
  131.6 1.5 fusion.3
  133.1 3.4 %collective-permute-start.6 = (bf16[256,1024]{1,0:T(8,128)(2,1)S(1)}, bf16[256,1024]{1,0:T(8,128)(2,1)S(1)}, u32[]{:S(2)}, u32[]{:S(2)}) collective-permute-start(bf16[256,1024]{1,0:T(8,128)(2,1)S(1)} %get-tuple-element.80), channel_id=1, source_target_pairs={{0,8},{4,12},{8,16},{12,20},{1,9},{5,13},{9,17},{13,21},{2,10},{6,... | collective-permute-start | bytes 1572872 | tf_op jit(solution)/shard_map/ppermute | solution.py:250
  139.8 6.4 %collective-permute-done.6 = bf16[256,1024]{1,0:T(8,128)(2,1)S(1)} collective-permute-done((bf16[256,1024]{1,0:T(8,128)(2,1)S(1)}, bf16[256,1024]{1,0:T(8,128)(2,1)S(1)}, u32[]{:S(2)}, u32[]{:S(2)}) %collective-permute-start.6) | collective-permute-done | bytes 524320 | tf_op jit(solution)/shard_map/ppermute | solution.py:250
  146.6 6.2 %collective-permute-done.7 = bf16[2048,512]{1,0:T(8,128)(2,1)S(1)} collective-permute-done((bf16[2048,512]{1,0:T(8,128)(2,1)S(1)}, bf16[2048,512]{1,0:T(8,128)(2,1)S(1)}, u32[]{:S(2)}, u32[]{:S(2)}) %collective-permute-start.7) | collective-permute-done | bytes 2097184 | tf_op jit(solution)/shard_map/ppermute | solution.py:167
  152.9 2.2 convolution_convert_fusion.10
  155.1 2.0 convolution_convert_fusion.11
  157.1 1.7 collective-permute-start.24
  159.5 1.8 convolution_convert_fusion.4
  161.3 2.0 convolution_convert_fusion.5
  163.3 2.0 convolution_convert_fusion
  165.3 1.3 collective-permute-start.32
  167.4 1.8 convolution_convert_fusion.2
  169.2 1.5 collective-permute-start.8
  171.2 4.4 %collective-permute-start.18 = (bf16[256,1024]{1,0:T(8,128)(2,1)S(1)}, bf16[256,1024]{1,0:T(8,128)(2,1)S(1)}, u32[]{:S(2)}, u32[]{:S(2)}) collective-permute-start(bf16[256,1024]{1,0:T(8,128)(2,1)S(1)} %add_convert_fusion.8), channel_id=1, source_target_pairs={{0,8},{4,12},{8,16},{12,20},{16,24},{20,28},{1,9},{5,13},{9,17},{1... | collective-permute-start | bytes 1572872 | tf_op jit(solution)/shard_map/ppermute | solution.py:250
  178.2 4.2 %collective-permute-done.32 = bf16[256,1024]{1,0:T(8,128)(2,1)S(1)} collective-permute-done((bf16[256,1024]{1,0:T(8,128)(2,1)S(1)}, bf16[256,1024]{1,0:T(8,128)(2,1)S(1)}, u32[]{:S(2)}, u32[]{:S(2)}) %collective-permute-start.32) | collective-permute-done | bytes 524320 | tf_op jit(solution)/shard_map/ppermute | solution.py:250
  183.7 1.5 collective-permute-start.28
  185.1 1.3 fusion.9
  186.5 16.1 %collective-permute-done.18 = bf16[256,1024]{1,0:T(8,128)(2,1)S(1)} collective-permute-done((bf16[256,1024]{1,0:T(8,128)(2,1)S(1)}, bf16[256,1024]{1,0:T(8,128)(2,1)S(1)}, u32[]{:S(2)}, u32[]{:S(2)}) %collective-permute-start.18) | collective-permute-done | bytes 524320 | tf_op jit(solution)/shard_map/ppermute | solution.py:250
  202.6 5.2 %collective-permute-start.33 = (bf16[256,1024]{1,0:T(8,128)(2,1)}, bf16[256,1024]{1,0:T(8,128)(2,1)}, u32[]{:S(2)}, u32[]{:S(2)}) collective-permute-start(bf16[256,1024]{1,0:T(8,128)(2,1)} %get-tuple-element.82), channel_id=1, source_target_pairs={{0,8},{4,12},{8,16},{12,20},{1,9},{5,13},{9,17},{13,21},{2,10},{6,... | collective-permute-start | bytes 1572872 | tf_op jit(solution)/shard_map/ppermute | solution.py:250
  208.4 1.4 fusion.15
  212.5 8.8 %shard_map.58 = (f32[256,2048]{1,0:T(8,128)S(1)}, f32[3,264,2048]{2,1,0:T(8,128)}) custom-call(bf16[3,256,4096]{2,1,0:T(8,128)(2,1)} %bitcast.74, f32[3,8,4096]{2,1,0:T(8,128)S(1)} %pad_convert_fusion.1.before_ref, f32[3,8,4096]{2,1,0:T(8,128)S(1)} %pad_convert_fusion.after_ref, f32[3,3,4096]{2,1,0:T(4,128)S(1)} %bitcast.65, ...), custom_call_target="tpu_custom_call" | custom-call | flops 2147483648 | bytes 17121280 | tf_op jit(solution)/shard_map/pallas_call | solution.py:113
  221.3 7.4 %collective-permute-start.25 = (bf16[256,1024]{1,0:T(8,128)(2,1)}, bf16[256,1024]{1,0:T(8,128)(2,1)}, u32[]{:S(2)}, u32[]{:S(2)}) collective-permute-start(bf16[256,1024]{1,0:T(8,128)(2,1)} %get-tuple-element.78), channel_id=1, source_target_pairs={{0,8},{4,12},{8,16},{12,20},{1,9},{5,13},{9,17},{13,21},{2,10},{6,... | collective-permute-start | bytes 1572872 | tf_op jit(solution)/shard_map/ppermute | solution.py:250
  228.7 1.5 collective-permute-start.36
  230.2 5.3 %shard_map.57 = bf16[3,256,1024]{2,1,0:T(8,128)(2,1)S(1)} custom-call(bf16[256,1024]{1,0:T(8,128)(2,1)S(1)} %add_convert_fusion.6.grad_ref, bf16[144,1024]{1,0:T(8,128)(2,1)S(1)} %collective-permute-done.22.halo_ref, f32[256,2048]{1,0:T(8,128)S(1)} %get-tuple-element.33.conv_ref, f32[3,264,2048]{2,1,0:T(8,128)} %get-tuple-element.32.mix_ref, ...), custom_call_target="tpu_custom_call" | custom-call | flops 1073741824 | bytes 12959744 | tf_op jit(solution)/shard_map/pallas_call | solution.py:113
  235.6 5.4 %shard_map.56 = bf16[3,256,1024]{2,1,0:T(8,128)(2,1)S(1)} custom-call(bf16[256,1024]{1,0:T(8,128)(2,1)S(1)} %add_convert_fusion.9.grad_ref, bf16[144,1024]{1,0:T(8,128)(2,1)S(1)} %collective-permute-done.14.halo_ref, f32[256,2048]{1,0:T(8,128)S(1)} %get-tuple-element.33.conv_ref, f32[3,264,2048]{2,1,0:T(8,128)} %get-tuple-element.32.mix_ref, ...), custom_call_target="tpu_custom_call" | custom-call | flops 1073741824 | bytes 12959744 | tf_op jit(solution)/shard_map/pallas_call | solution.py:113
  242.7 1.3 add_convert_fusion.2
  244.1 1.3 collective-permute-start.34
  249.2 5.2 %collective-permute-start.26 = (bf16[256,1024]{1,0:T(8,128)(2,1)S(1)}, bf16[256,1024]{1,0:T(8,128)(2,1)S(1)}, u32[]{:S(2)}, u32[]{:S(2)}) collective-permute-start(bf16[256,1024]{1,0:T(8,128)(2,1)S(1)} %add_convert_fusion.5), channel_id=1, source_target_pairs={{0,8},{4,12},{8,16},{12,20},{16,24},{20,28},{1,9},{5,13},{9,17},{1... | collective-permute-start | bytes 1572872 | tf_op jit(solution)/shard_map/ppermute | solution.py:250
  254.5 3.1 %collective-permute-done.34 = bf16[256,1024]{1,0:T(8,128)(2,1)S(1)} collective-permute-done((bf16[256,1024]{1,0:T(8,128)(2,1)S(1)}, bf16[256,1024]{1,0:T(8,128)(2,1)S(1)}, u32[]{:S(2)}, u32[]{:S(2)}) %collective-permute-start.34) | collective-permute-done | bytes 524320 | tf_op jit(solution)/shard_map/ppermute | solution.py:250
  260.4 3.4 %collective-permute-done.37 = bf16[256,1024]{1,0:T(8,128)(2,1)S(1)} collective-permute-done((bf16[256,1024]{1,0:T(8,128)(2,1)S(1)}, bf16[256,1024]{1,0:T(8,128)(2,1)S(1)}, u32[]{:S(2)}, u32[]{:S(2)}) %collective-permute-start.37) | collective-permute-done | bytes 524320 | tf_op jit(solution)/shard_map/ppermute | solution.py:250
  264.1 4.3 %collective-permute-done.26 = bf16[256,1024]{1,0:T(8,128)(2,1)S(1)} collective-permute-done((bf16[256,1024]{1,0:T(8,128)(2,1)S(1)}, bf16[256,1024]{1,0:T(8,128)(2,1)S(1)}, u32[]{:S(2)}, u32[]{:S(2)}) %collective-permute-start.26) | collective-permute-done | bytes 524320 | tf_op jit(solution)/shard_map/ppermute | solution.py:250
  268.4 5.9 %collective-permute-done.29 = bf16[256,1024]{1,0:T(8,128)(2,1)S(1)} collective-permute-done((bf16[256,1024]{1,0:T(8,128)(2,1)S(1)}, bf16[256,1024]{1,0:T(8,128)(2,1)S(1)}, u32[]{:S(2)}, u32[]{:S(2)}) %collective-permute-start.29) | collective-permute-done | bytes 524320 | tf_op jit(solution)/shard_map/ppermute | solution.py:250
  274.8 1.4 fusion.13
  278.8 9.2 %collective-permute-done.38.halo_ref = bf16[144,1024]{1,0:T(8,128)(2,1)S(1)} collective-permute-done((bf16[144,1024]{1,0:T(8,128)(2,1)S(1)}, bf16[144,1024]{1,0:T(8,128)(2,1)S(1)}, u32[]{:S(2)}, u32[]{:S(2)}) %collective-permute-start.38) | collective-permute-done | bytes 294944 | tf_op jit(solution)/shard_map/ppermute | solution.py:27
  288.0 5.3 %shard_map.60 = bf16[3,256,1024]{2,1,0:T(8,128)(2,1)S(1)} custom-call(bf16[256,1024]{1,0:T(8,128)(2,1)S(1)} %add_convert_fusion.grad_ref, bf16[144,1024]{1,0:T(8,128)(2,1)S(1)} %collective-permute-done.38.halo_ref, f32[256,2048]{1,0:T(8,128)S(1)} %get-tuple-element.43.conv_ref, f32[3,264,2048]{2,1,0:T(8,128)} %get-tuple-element.42.mix_ref, ...), custom_call_target="tpu_custom_call" | custom-call | flops 1073741824 | bytes 12959744 | tf_op jit(solution)/shard_map/pallas_call | solution.py:113
  293.4 5.3 %shard_map.59 = bf16[3,256,1024]{2,1,0:T(8,128)(2,1)S(1)} custom-call(bf16[256,1024]{1,0:T(8,128)(2,1)S(1)} %add_convert_fusion.3.grad_ref, bf16[144,1024]{1,0:T(8,128)(2,1)S(1)} %collective-permute-done.30.halo_ref, f32[256,2048]{1,0:T(8,128)S(1)} %get-tuple-element.43.conv_ref, f32[3,264,2048]{2,1,0:T(8,128)} %get-tuple-element.42.mix_ref, ...), custom_call_target="tpu_custom_call" | custom-call | flops 1073741824 | bytes 12959744 | tf_op jit(solution)/shard_map/pallas_call | solution.py:113
  299.2 3.0 collective-permute-done.31
  302.3 3.0 maximum_bitcast_fusion
  (147 shorter events, 40.1 us)
Async XLA Ops:
  1.0 25.2 %collective-permute-start.13 = (bf16[3,2,4096]{2,1,0:T(2,128)(2,1)S(1)}, bf16[3,2,4096]{2,1,0:T(2,128)(2,1)S(1)}, u32[]{:S(2)}, u32[]{:S(2)}) collective-permute-start(bf16[3,2,4096]{2,1,0:T(2,128)(2,1)S(1)} %slice.189), channel_id=1, source_target_pairs={{4,0},{8,4},{12,8},{16,12},{20,16},{24,20},{28,24},{5,1},{9,5},{13... | collective-permute-start | bytes 147464 | tf_op jit(solution)/shard_map/ppermute | solution.py:27
  2.3 26.5 %collective-permute-start = (bf16[256,2048]{1,0:T(8,128)(2,1)}, bf16[256,2048]{1,0:T(8,128)(2,1)}, u32[]{:S(2)}, u32[]{:S(2)}) collective-permute-start(bf16[256,2048]{1,0:T(8,128)(2,1)} %bitcast.75), channel_id=1, source_target_pairs={{0,2},{2,0},{1,3},{3,1},{4,6},{6,4},{5,7},{7,5},{8,10},{10,8},{9,1... | collective-permute-start | bytes 3145736 | tf_op jit(solution)/shard_map/ppermute | solution.py:149
  6.2 2.9 copy-start.9
  11.2 7.0 %copy-start.1 = (bf16[1,4096,512]{2,1,0:T(8,128)(2,1)S(1)}, bf16[1,4096,512]{2,1,0:T(8,128)(2,1)}, u32[]{:S(2)}) copy-start(bf16[1,4096,512]{2,1,0:T(8,128)(2,1)} %param.8) | copy-start | bytes 12582916
  12.6 30.0 %collective-permute-start.12 = (bf16[134,4096]{1,0:T(8,128)(2,1)}, bf16[134,4096]{1,0:T(8,128)(2,1)}, u32[]{:S(2)}, u32[]{:S(2)}) collective-permute-start(bf16[134,4096]{1,0:T(8,128)(2,1)} %pad_maximum_fusion.4), channel_id=1, source_target_pairs={{0,4},{4,8},{8,12},{12,16},{16,20},{20,24},{24,28},{1,5},{5,9},{9,... | collective-permute-start | bytes 3293192 | tf_op jit(solution)/shard_map/ppermute | solution.py:27
  20.5 1.7 copy-start.2
  20.5 65.2 %collective-permute-start.1 = (bf16[2048,512]{1,0:T(8,128)(2,1)}, bf16[2048,512]{1,0:T(8,128)(2,1)}, u32[]{:S(2)}, u32[]{:S(2)}) collective-permute-start(bf16[2048,512]{1,0:T(8,128)(2,1)} %get-tuple-element.27), channel_id=1, source_target_pairs={{0,4},{4,0},{8,12},{12,8},{16,20},{20,16},{24,28},{28,24},{1,5},{5... | collective-permute-start | bytes 6291464 | tf_op jit(solution)/shard_map/ppermute | solution.py:167
  22.3 3.1 %copy-start.23 = (bf16[1,128,256]{2,1,0:T(8,128)(2,1)S(1)}, bf16[1,128,256]{2,1,0:T(8,128)(2,1)}, u32[]{:S(2)}) copy-start(bf16[1,128,256]{2,1,0:T(8,128)(2,1)} %param.7) | copy-start | bytes 196612
  31.1 56.3 %collective-permute-start.2 = (bf16[256,1024]{1,0:T(8,128)(2,1)S(1)}, bf16[256,1024]{1,0:T(8,128)(2,1)}, u32[]{:S(2)}, u32[]{:S(2)}) collective-permute-start(bf16[256,1024]{1,0:T(8,128)(2,1)S(1)} %pad_maximum_fusion.6), channel_id=1, source_target_pairs={{0,24},{4,28},{8,0},{12,4},{16,8},{20,12},{24,16},{28,20},{1,25},{... | collective-permute-start | bytes 1572872 | tf_op jit(solution)/shard_map/ppermute | solution.py:182
  36.8 68.7 %collective-permute-start.3 = (bf16[256,1024]{1,0:T(8,128)(2,1)S(1)}, bf16[256,1024]{1,0:T(8,128)(2,1)}, u32[]{:S(2)}, u32[]{:S(2)}) collective-permute-start(bf16[256,1024]{1,0:T(8,128)(2,1)S(1)} %pad_maximum_fusion.7), channel_id=1, source_target_pairs={{0,16},{4,20},{8,24},{12,28},{16,0},{20,4},{24,8},{28,12},{1,17},{... | collective-permute-start | bytes 1572872 | tf_op jit(solution)/shard_map/ppermute | solution.py:182
  36.9 52.4 %collective-permute-start.4 = (bf16[256,1024]{1,0:T(8,128)(2,1)S(1)}, bf16[256,1024]{1,0:T(8,128)(2,1)}, u32[]{:S(2)}, u32[]{:S(2)}) collective-permute-start(bf16[256,1024]{1,0:T(8,128)(2,1)S(1)} %pad_maximum_fusion.8), channel_id=1, source_target_pairs={{0,8},{4,12},{8,16},{12,20},{16,24},{20,28},{24,0},{28,4},{1,9},{5... | collective-permute-start | bytes 1572872 | tf_op jit(solution)/shard_map/ppermute | solution.py:182
  44.9 42.6 %copy-start.4 = (bf16[1024,512]{1,0:T(8,128)(2,1)S(1)}, bf16[1024,512]{1,0:T(8,128)(2,1)}, u32[]{:S(2)}) copy-start(bf16[1024,512]{1,0:T(8,128)(2,1)} %get-tuple-element.62) | copy-start | bytes 3145732
  89.3 1.9 copy-start.3
  92.9 12.6 %copy-start = (bf16[2048,512]{1,0:T(8,128)(2,1)S(1)}, bf16[2048,512]{1,0:T(8,128)(2,1)}, u32[]{:S(2)}) copy-start(bf16[2048,512]{1,0:T(8,128)(2,1)} %get-tuple-element.28) | copy-start | bytes 6291460
  94.9 18.5 %collective-permute-start.16 = (bf16[256,1024]{1,0:T(8,128)(2,1)S(1)}, bf16[256,1024]{1,0:T(8,128)(2,1)S(1)}, u32[]{:S(2)}, u32[]{:S(2)}) collective-permute-start(bf16[256,1024]{1,0:T(8,128)(2,1)S(1)} %convolution_convert_fusion.9), channel_id=1, source_target_pairs={{0,8},{4,12},{1,9},{5,13},{2,10},{6,14},{3,11},{7,15}} | collective-permute-start | bytes 1572872 | tf_op jit(solution)/shard_map/ppermute | solution.py:250
  101.1 12.3 %collective-permute-start.19 = (bf16[256,1024]{1,0:T(8,128)(2,1)S(1)}, bf16[256,1024]{1,0:T(8,128)(2,1)S(1)}, u32[]{:S(2)}, u32[]{:S(2)}) collective-permute-start(bf16[256,1024]{1,0:T(8,128)(2,1)S(1)} %convolution_convert_fusion.7), channel_id=1, source_target_pairs={{24,16},{28,20},{25,17},{29,21},{26,18},{30,22},{27,19},{31,23}} | collective-permute-start | bytes 1572872 | tf_op jit(solution)/shard_map/ppermute | solution.py:250
  101.8 29.8 %collective-permute-start.5 = (bf16[256,1024]{1,0:T(8,128)(2,1)S(1)}, bf16[256,1024]{1,0:T(8,128)(2,1)}, u32[]{:S(2)}, u32[]{:S(2)}) collective-permute-start(bf16[256,1024]{1,0:T(8,128)(2,1)S(1)} %convolution_convert_fusion.12), channel_id=1, source_target_pairs={{0,8},{4,12},{1,9},{5,13},{2,10},{6,14},{3,11},{7,15}} | collective-permute-start | bytes 1572872 | tf_op jit(solution)/shard_map/ppermute | solution.py:250
  104.0 27.6 %collective-permute-start.9 = (bf16[256,1024]{1,0:T(8,128)(2,1)S(1)}, bf16[256,1024]{1,0:T(8,128)(2,1)}, u32[]{:S(2)}, u32[]{:S(2)}) collective-permute-start(bf16[256,1024]{1,0:T(8,128)(2,1)S(1)} %convolution_convert_fusion.14), channel_id=1, source_target_pairs={{24,16},{28,20},{25,17},{29,21},{26,18},{30,22},{27,19},{31,23}} | collective-permute-start | bytes 1572872 | tf_op jit(solution)/shard_map/ppermute | solution.py:250
  105.5 47.3 %collective-permute-start.7 = (bf16[2048,512]{1,0:T(8,128)(2,1)S(1)}, bf16[2048,512]{1,0:T(8,128)(2,1)S(1)}, u32[]{:S(2)}, u32[]{:S(2)}) collective-permute-start(bf16[2048,512]{1,0:T(8,128)(2,1)S(1)} %copy-done), channel_id=1, source_target_pairs={{0,4},{4,0},{8,12},{12,8},{16,20},{20,16},{24,28},{28,24},{1,5},{5... | collective-permute-start | bytes 6291464 | tf_op jit(solution)/shard_map/ppermute | solution.py:167
  109.9 1.0 copy-start.21
  114.5 22.8 %collective-permute-start.17 = (bf16[256,1024]{1,0:T(8,128)(2,1)}, bf16[256,1024]{1,0:T(8,128)(2,1)}, u32[]{:S(2)}, u32[]{:S(2)}) collective-permute-start(bf16[256,1024]{1,0:T(8,128)(2,1)} %get-tuple-element.84), channel_id=1, source_target_pairs={{0,8},{4,12},{8,16},{12,20},{1,9},{5,13},{9,17},{13,21},{2,10},{6,... | collective-permute-start | bytes 1572872 | tf_op jit(solution)/shard_map/ppermute | solution.py:250
  119.7 17.6 %collective-permute-start.20 = (bf16[256,1024]{1,0:T(8,128)(2,1)S(1)}, bf16[256,1024]{1,0:T(8,128)(2,1)}, u32[]{:S(2)}, u32[]{:S(2)}) collective-permute-start(bf16[256,1024]{1,0:T(8,128)(2,1)S(1)} %get-tuple-element.85), channel_id=1, source_target_pairs={{16,8},{20,12},{24,16},{28,20},{17,9},{21,13},{25,17},{29,21},{18,... | collective-permute-start | bytes 1572872 | tf_op jit(solution)/shard_map/ppermute | solution.py:250
  122.8 8.9 %copy-start.18 = (bf16[256,1024]{1,0:T(8,128)(2,1)S(1)}, bf16[256,1024]{1,0:T(8,128)(2,1)}, u32[]{:S(2)}) copy-start(bf16[256,1024]{1,0:T(8,128)(2,1)} %convolution_convert_fusion.13) | copy-start | bytes 1572868
  133.1 13.0 %collective-permute-start.6 = (bf16[256,1024]{1,0:T(8,128)(2,1)S(1)}, bf16[256,1024]{1,0:T(8,128)(2,1)S(1)}, u32[]{:S(2)}, u32[]{:S(2)}) collective-permute-start(bf16[256,1024]{1,0:T(8,128)(2,1)S(1)} %get-tuple-element.80), channel_id=1, source_target_pairs={{0,8},{4,12},{8,16},{12,20},{1,9},{5,13},{9,17},{13,21},{2,10},{6,... | collective-permute-start | bytes 1572872 | tf_op jit(solution)/shard_map/ppermute | solution.py:250
  136.6 9.8 %collective-permute-start.10 = (bf16[256,1024]{1,0:T(8,128)(2,1)S(1)}, bf16[256,1024]{1,0:T(8,128)(2,1)S(1)}, u32[]{:S(2)}, u32[]{:S(2)}) collective-permute-start(bf16[256,1024]{1,0:T(8,128)(2,1)S(1)} %get-tuple-element.81), channel_id=1, source_target_pairs={{16,8},{20,12},{24,16},{28,20},{17,9},{21,13},{25,17},{29,21},{18,... | collective-permute-start | bytes 1572872 | tf_op jit(solution)/shard_map/ppermute | solution.py:250
  152.9 10.4 %copy-start.7 = (bf16[1024,512]{1,0:T(8,128)(2,1)}, bf16[1024,512]{1,0:T(8,128)(2,1)S(1)}, u32[]{:S(2)}) copy-start(bf16[1024,512]{1,0:T(8,128)(2,1)S(1)} %get-tuple-element.69) | copy-start | bytes 3145732
  152.9 14.5 %copy-start.5 = (bf16[1024,512]{1,0:T(8,128)(2,1)}, bf16[1024,512]{1,0:T(8,128)(2,1)S(1)}, u32[]{:S(2)}) copy-start(bf16[1024,512]{1,0:T(8,128)(2,1)S(1)} %get-tuple-element.68) | copy-start | bytes 3145732
  155.1 3.7 %copy-start.10 = (bf16[256,1024]{1,0:T(8,128)(2,1)}, bf16[256,1024]{1,0:T(8,128)(2,1)S(1)}, u32[]{:S(2)}) copy-start(bf16[256,1024]{1,0:T(8,128)(2,1)S(1)} %convolution_convert_fusion.10) | copy-start | bytes 1572868
  157.1 4.2 %copy-start.14 = (bf16[256,1024]{1,0:T(8,128)(2,1)}, bf16[256,1024]{1,0:T(8,128)(2,1)S(1)}, u32[]{:S(2)}) copy-start(bf16[256,1024]{1,0:T(8,128)(2,1)S(1)} %convolution_convert_fusion.11) | copy-start | bytes 1572868
  157.1 14.0 %collective-permute-start.24 = (bf16[256,1024]{1,0:T(8,128)(2,1)S(1)}, bf16[256,1024]{1,0:T(8,128)(2,1)S(1)}, u32[]{:S(2)}, u32[]{:S(2)}) collective-permute-start(bf16[256,1024]{1,0:T(8,128)(2,1)S(1)} %convolution_convert_fusion.11), channel_id=1, source_target_pairs={{0,8},{4,12},{1,9},{5,13},{2,10},{6,14},{3,11},{7,15}} | collective-permute-start | bytes 1572872 | tf_op jit(solution)/shard_map/ppermute | solution.py:250
  158.8 16.7 %collective-permute-start.27 = (bf16[256,1024]{1,0:T(8,128)(2,1)S(1)}, bf16[256,1024]{1,0:T(8,128)(2,1)S(1)}, u32[]{:S(2)}, u32[]{:S(2)}) collective-permute-start(bf16[256,1024]{1,0:T(8,128)(2,1)S(1)} %convolution_convert_fusion.10), channel_id=1, source_target_pairs={{24,16},{28,20},{25,17},{29,21},{26,18},{30,22},{27,19},{31,23}} | collective-permute-start | bytes 1572872 | tf_op jit(solution)/shard_map/ppermute | solution.py:250
  161.3 5.3 %copy-start.16 = (bf16[256,1024]{1,0:T(8,128)(2,1)}, bf16[256,1024]{1,0:T(8,128)(2,1)S(1)}, u32[]{:S(2)}) copy-start(bf16[256,1024]{1,0:T(8,128)(2,1)S(1)} %convolution_convert_fusion.4) | copy-start | bytes 1572868
  163.3 2.0 copy-start.12
  165.3 17.1 %collective-permute-start.32 = (bf16[256,1024]{1,0:T(8,128)(2,1)S(1)}, bf16[256,1024]{1,0:T(8,128)(2,1)S(1)}, u32[]{:S(2)}, u32[]{:S(2)}) collective-permute-start(bf16[256,1024]{1,0:T(8,128)(2,1)S(1)} %convolution_convert_fusion.5), channel_id=1, source_target_pairs={{0,8},{4,12},{1,9},{5,13},{2,10},{6,14},{3,11},{7,15}} | collective-permute-start | bytes 1572872 | tf_op jit(solution)/shard_map/ppermute | solution.py:250
  166.7 17.0 %collective-permute-start.35 = (bf16[256,1024]{1,0:T(8,128)(2,1)S(1)}, bf16[256,1024]{1,0:T(8,128)(2,1)S(1)}, u32[]{:S(2)}, u32[]{:S(2)}) collective-permute-start(bf16[256,1024]{1,0:T(8,128)(2,1)S(1)} %convolution_convert_fusion.4), channel_id=1, source_target_pairs={{24,16},{28,20},{25,17},{29,21},{26,18},{30,22},{27,19},{31,23}} | collective-permute-start | bytes 1572872 | tf_op jit(solution)/shard_map/ppermute | solution.py:250
  169.2 38.6 %copy-start.20 = (bf16[256,1024]{1,0:T(8,128)(2,1)S(1)}, bf16[256,1024]{1,0:T(8,128)(2,1)}, u32[]{:S(2)}) copy-start(bf16[256,1024]{1,0:T(8,128)(2,1)} %convolution_convert_fusion.6) | copy-start | bytes 1572868
  169.2 38.9 %collective-permute-start.8 = (bf16[256,1024]{1,0:T(8,128)(2,1)S(1)}, bf16[256,1024]{1,0:T(8,128)(2,1)S(1)}, u32[]{:S(2)}, u32[]{:S(2)}) collective-permute-start(bf16[256,1024]{1,0:T(8,128)(2,1)S(1)} %add_convert_fusion.11), channel_id=1, source_target_pairs={{0,8},{4,12},{8,16},{12,20},{16,24},{20,28},{1,9},{5,13},{9,17},{1... | collective-permute-start | bytes 1572872 | tf_op jit(solution)/shard_map/ppermute | solution.py:250
  171.2 31.4 %collective-permute-start.18 = (bf16[256,1024]{1,0:T(8,128)(2,1)S(1)}, bf16[256,1024]{1,0:T(8,128)(2,1)S(1)}, u32[]{:S(2)}, u32[]{:S(2)}) collective-permute-start(bf16[256,1024]{1,0:T(8,128)(2,1)S(1)} %add_convert_fusion.8), channel_id=1, source_target_pairs={{0,8},{4,12},{8,16},{12,20},{16,24},{20,28},{1,9},{5,13},{9,17},{1... | collective-permute-start | bytes 1572872 | tf_op jit(solution)/shard_map/ppermute | solution.py:250
  175.6 32.2 %collective-permute-start.21 = (bf16[256,1024]{1,0:T(8,128)(2,1)S(1)}, bf16[256,1024]{1,0:T(8,128)(2,1)S(1)}, u32[]{:S(2)}, u32[]{:S(2)}) collective-permute-start(bf16[256,1024]{1,0:T(8,128)(2,1)S(1)} %add_convert_fusion.7), channel_id=1, source_target_pairs={{8,0},{12,4},{16,8},{20,12},{24,16},{28,20},{9,1},{13,5},{17,9},{2... | collective-permute-start | bytes 1572872 | tf_op jit(solution)/shard_map/ppermute | solution.py:250
  182.4 25.7 %collective-permute-start.11 = (bf16[256,1024]{1,0:T(8,128)(2,1)S(1)}, bf16[256,1024]{1,0:T(8,128)(2,1)S(1)}, u32[]{:S(2)}, u32[]{:S(2)}) collective-permute-start(bf16[256,1024]{1,0:T(8,128)(2,1)S(1)} %add_convert_fusion.10), channel_id=1, source_target_pairs={{8,0},{12,4},{16,8},{20,12},{24,16},{28,20},{9,1},{13,5},{17,9},{2... | collective-permute-start | bytes 1572872 | tf_op jit(solution)/shard_map/ppermute | solution.py:250
  183.7 57.3 %collective-permute-start.28 = (bf16[256,1024]{1,0:T(8,128)(2,1)}, bf16[256,1024]{1,0:T(8,128)(2,1)}, u32[]{:S(2)}, u32[]{:S(2)}) collective-permute-start(bf16[256,1024]{1,0:T(8,128)(2,1)} %get-tuple-element.79), channel_id=1, source_target_pairs={{16,8},{20,12},{24,16},{28,20},{17,9},{21,13},{25,17},{29,21},{18,... | collective-permute-start | bytes 1572872 | tf_op jit(solution)/shard_map/ppermute | solution.py:250
  186.5 21.6 %copy-start.19 = (bf16[256,1024]{1,0:T(8,128)(2,1)S(1)}, bf16[256,1024]{1,0:T(8,128)(2,1)}, u32[]{:S(2)}) copy-start(bf16[256,1024]{1,0:T(8,128)(2,1)} %convolution_convert_fusion.15) | copy-start | bytes 1572868
  202.6 40.1 %collective-permute-start.33 = (bf16[256,1024]{1,0:T(8,128)(2,1)}, bf16[256,1024]{1,0:T(8,128)(2,1)}, u32[]{:S(2)}, u32[]{:S(2)}) collective-permute-start(bf16[256,1024]{1,0:T(8,128)(2,1)} %get-tuple-element.82), channel_id=1, source_target_pairs={{0,8},{4,12},{8,16},{12,20},{1,9},{5,13},{9,17},{13,21},{2,10},{6,... | collective-permute-start | bytes 1572872 | tf_op jit(solution)/shard_map/ppermute | solution.py:250
  209.9 18.9 %collective-permute-start.22 = (bf16[144,1024]{1,0:T(8,128)(2,1)S(1)}, bf16[144,1024]{1,0:T(8,128)(2,1)S(1)}, u32[]{:S(2)}, u32[]{:S(2)}) collective-permute-start(bf16[144,1024]{1,0:T(8,128)(2,1)S(1)} %pad_maximum_fusion.10), channel_id=1, source_target_pairs={{4,0},{8,4},{12,8},{16,12},{20,16},{24,20},{28,24},{5,1},{9,5},{13... | collective-permute-start | bytes 884744 | tf_op jit(solution)/shard_map/ppermute | solution.py:27
  211.2 24.3 %collective-permute-start.14 = (bf16[144,1024]{1,0:T(8,128)(2,1)S(1)}, bf16[144,1024]{1,0:T(8,128)(2,1)S(1)}, u32[]{:S(2)}, u32[]{:S(2)}) collective-permute-start(bf16[144,1024]{1,0:T(8,128)(2,1)S(1)} %pad_maximum_fusion.9), channel_id=1, source_target_pairs={{4,0},{8,4},{12,8},{16,12},{20,16},{24,20},{28,24},{5,1},{9,5},{13... | collective-permute-start | bytes 884744 | tf_op jit(solution)/shard_map/ppermute | solution.py:27
  221.3 26.6 %collective-permute-start.25 = (bf16[256,1024]{1,0:T(8,128)(2,1)}, bf16[256,1024]{1,0:T(8,128)(2,1)}, u32[]{:S(2)}, u32[]{:S(2)}) collective-permute-start(bf16[256,1024]{1,0:T(8,128)(2,1)} %get-tuple-element.78), channel_id=1, source_target_pairs={{0,8},{4,12},{8,16},{12,20},{1,9},{5,13},{9,17},{13,21},{2,10},{6,... | collective-permute-start | bytes 1572872 | tf_op jit(solution)/shard_map/ppermute | solution.py:250
  228.7 16.7 %collective-permute-start.36 = (bf16[256,1024]{1,0:T(8,128)(2,1)}, bf16[256,1024]{1,0:T(8,128)(2,1)}, u32[]{:S(2)}, u32[]{:S(2)}) collective-permute-start(bf16[256,1024]{1,0:T(8,128)(2,1)} %get-tuple-element.83), channel_id=1, source_target_pairs={{16,8},{20,12},{24,16},{28,20},{17,9},{21,13},{25,17},{29,21},{18,... | collective-permute-start | bytes 1572872 | tf_op jit(solution)/shard_map/ppermute | solution.py:250
  235.5 6.0 %copy-start.15 = (bf16[256,1024]{1,0:T(8,128)(2,1)S(1)}, bf16[256,1024]{1,0:T(8,128)(2,1)}, u32[]{:S(2)}) copy-start(bf16[256,1024]{1,0:T(8,128)(2,1)} %copy-done.14) | copy-start | bytes 1572868
  235.5 7.2 %copy-start.17 = (bf16[256,1024]{1,0:T(8,128)(2,1)S(1)}, bf16[256,1024]{1,0:T(8,128)(2,1)}, u32[]{:S(2)}) copy-start(bf16[256,1024]{1,0:T(8,128)(2,1)} %copy-done.16) | copy-start | bytes 1572868
  235.5 39.1 %collective-permute-start.23 = (bf16[3,256,1024]{2,1,0:T(8,128)(2,1)S(1)}, bf16[3,256,1024]{2,1,0:T(8,128)(2,1)S(1)}, u32[]{:S(2)}, u32[]{:S(2)}) collective-permute-start(bf16[3,256,1024]{2,1,0:T(8,128)(2,1)S(1)} %shard_map.57), channel_id=1, source_target_pairs={{0,1},{1,0},{2,3},{3,2},{4,5},{5,4},{6,7},{7,6},{8,9},{9,8},{10,11... | collective-permute-start | bytes 4718600 | tf_op jit(solution)/shard_map/ppermute | solution.py:287
  241.0 4.4 %copy-start.13 = (bf16[256,1024]{1,0:T(8,128)(2,1)S(1)}, bf16[256,1024]{1,0:T(8,128)(2,1)}, u32[]{:S(2)}) copy-start(bf16[256,1024]{1,0:T(8,128)(2,1)} %copy-done.12) | copy-start | bytes 1572868
  241.0 7.0 %copy-start.11 = (bf16[256,1024]{1,0:T(8,128)(2,1)S(1)}, bf16[256,1024]{1,0:T(8,128)(2,1)}, u32[]{:S(2)}) copy-start(bf16[256,1024]{1,0:T(8,128)(2,1)} %copy-done.10) | copy-start | bytes 1572868
  241.0 33.7 %collective-permute-start.15 = (bf16[3,256,1024]{2,1,0:T(8,128)(2,1)S(1)}, bf16[3,256,1024]{2,1,0:T(8,128)(2,1)S(1)}, u32[]{:S(2)}, u32[]{:S(2)}) collective-permute-start(bf16[3,256,1024]{2,1,0:T(8,128)(2,1)S(1)} %shard_map.56), channel_id=1, source_target_pairs={{0,1},{1,0},{2,3},{3,2},{4,5},{5,4},{6,7},{7,6},{8,9},{9,8},{10,11... | collective-permute-start | bytes 4718600 | tf_op jit(solution)/shard_map/ppermute | solution.py:287
  242.7 16.2 %copy-start.8 = (bf16[1024,512]{1,0:T(8,128)(2,1)S(1)}, bf16[1024,512]{1,0:T(8,128)(2,1)}, u32[]{:S(2)}) copy-start(bf16[1024,512]{1,0:T(8,128)(2,1)} %copy-done.7) | copy-start | bytes 3145732
  242.7 16.2 %copy-start.22 = (bf16[256,512]{1,0:T(8,128)(2,1)S(1)}, bf16[256,512]{1,0:T(8,128)(2,1)}, u32[]{:S(2)}) copy-start(bf16[256,512]{1,0:T(8,128)(2,1)} %get-tuple-element.77) | copy-start | bytes 786436
  244.1 13.5 %collective-permute-start.34 = (bf16[256,1024]{1,0:T(8,128)(2,1)S(1)}, bf16[256,1024]{1,0:T(8,128)(2,1)S(1)}, u32[]{:S(2)}, u32[]{:S(2)}) collective-permute-start(bf16[256,1024]{1,0:T(8,128)(2,1)S(1)} %add_convert_fusion.2), channel_id=1, source_target_pairs={{0,8},{4,12},{8,16},{12,20},{16,24},{20,28},{1,9},{5,13},{9,17},{1... | collective-permute-start | bytes 1572872 | tf_op jit(solution)/shard_map/ppermute | solution.py:250
  246.7 17.2 %collective-permute-start.37 = (bf16[256,1024]{1,0:T(8,128)(2,1)S(1)}, bf16[256,1024]{1,0:T(8,128)(2,1)S(1)}, u32[]{:S(2)}, u32[]{:S(2)}) collective-permute-start(bf16[256,1024]{1,0:T(8,128)(2,1)S(1)} %add_convert_fusion.1), channel_id=1, source_target_pairs={{8,0},{12,4},{16,8},{20,12},{24,16},{28,20},{9,1},{13,5},{17,9},{2... | collective-permute-start | bytes 1572872 | tf_op jit(solution)/shard_map/ppermute | solution.py:250
  249.2 10.4 %copy-start.6 = (bf16[1024,512]{1,0:T(8,128)(2,1)S(1)}, bf16[1024,512]{1,0:T(8,128)(2,1)}, u32[]{:S(2)}) copy-start(bf16[1024,512]{1,0:T(8,128)(2,1)} %copy-done.5) | copy-start | bytes 3145732
  249.2 19.2 %collective-permute-start.26 = (bf16[256,1024]{1,0:T(8,128)(2,1)S(1)}, bf16[256,1024]{1,0:T(8,128)(2,1)S(1)}, u32[]{:S(2)}, u32[]{:S(2)}) collective-permute-start(bf16[256,1024]{1,0:T(8,128)(2,1)S(1)} %add_convert_fusion.5), channel_id=1, source_target_pairs={{0,8},{4,12},{8,16},{12,20},{16,24},{20,28},{1,9},{5,13},{9,17},{1... | collective-permute-start | bytes 1572872 | tf_op jit(solution)/shard_map/ppermute | solution.py:250
  257.6 16.8 %collective-permute-start.29 = (bf16[256,1024]{1,0:T(8,128)(2,1)S(1)}, bf16[256,1024]{1,0:T(8,128)(2,1)S(1)}, u32[]{:S(2)}, u32[]{:S(2)}) collective-permute-start(bf16[256,1024]{1,0:T(8,128)(2,1)S(1)} %add_convert_fusion.4), channel_id=1, source_target_pairs={{8,0},{12,4},{16,8},{20,12},{24,16},{28,20},{9,1},{13,5},{17,9},{2... | collective-permute-start | bytes 1572872 | tf_op jit(solution)/shard_map/ppermute | solution.py:250
  276.2 11.8 %collective-permute-start.38 = (bf16[144,1024]{1,0:T(8,128)(2,1)S(1)}, bf16[144,1024]{1,0:T(8,128)(2,1)S(1)}, u32[]{:S(2)}, u32[]{:S(2)}) collective-permute-start(bf16[144,1024]{1,0:T(8,128)(2,1)S(1)} %pad_maximum_fusion.12), channel_id=1, source_target_pairs={{4,0},{8,4},{12,8},{16,12},{20,16},{24,20},{28,24},{5,1},{9,5},{13... | collective-permute-start | bytes 884744 | tf_op jit(solution)/shard_map/ppermute | solution.py:27
  277.5 15.9 %collective-permute-start.30 = (bf16[144,1024]{1,0:T(8,128)(2,1)S(1)}, bf16[144,1024]{1,0:T(8,128)(2,1)S(1)}, u32[]{:S(2)}, u32[]{:S(2)}) collective-permute-start(bf16[144,1024]{1,0:T(8,128)(2,1)S(1)} %pad_maximum_fusion.11), channel_id=1, source_target_pairs={{4,0},{8,4},{12,8},{16,12},{20,16},{24,20},{28,24},{5,1},{9,5},{13... | collective-permute-start | bytes 884744 | tf_op jit(solution)/shard_map/ppermute | solution.py:27
  293.3 5.9 %collective-permute-start.39 = (bf16[3,256,1024]{2,1,0:T(8,128)(2,1)S(1)}, bf16[3,256,1024]{2,1,0:T(8,128)(2,1)S(1)}, u32[]{:S(2)}, u32[]{:S(2)}) collective-permute-start(bf16[3,256,1024]{2,1,0:T(8,128)(2,1)S(1)} %shard_map.60), channel_id=1, source_target_pairs={{0,1},{1,0},{2,3},{3,2},{4,5},{5,4},{6,7},{7,6},{8,9},{9,8},{10,11... | collective-permute-start | bytes 4718600 | tf_op jit(solution)/shard_map/ppermute | solution.py:287
  298.7 3.6 %collective-permute-start.31 = (bf16[3,256,1024]{2,1,0:T(8,128)(2,1)S(1)}, bf16[3,256,1024]{2,1,0:T(8,128)(2,1)S(1)}, u32[]{:S(2)}, u32[]{:S(2)}) collective-permute-start(bf16[3,256,1024]{2,1,0:T(8,128)(2,1)S(1)} %shard_map.59), channel_id=1, source_target_pairs={{0,1},{1,0},{2,3},{3,2},{4,5},{5,4},{6,7},{7,6},{8,9},{9,8},{10,11... | collective-permute-start | bytes 4718600 | tf_op jit(solution)/shard_map/ppermute | solution.py:287

commit v4 on v3

--- a/solution.py
+++ b/solution.py
@@ -149,23 +149,26 @@
         got = lax.ppermute(cotangent, "tp", [(i, (i + s) % tp_count) for i in range(tp_count)])
         full = lax.dynamic_update_slice(full, got, (0, (tp_place - s) % tp_count * share))
 
+    def spread(mine):
+        held = [mine]
+        for s in range(1, inner):
+            route = [(zz * inner + xx, zz * inner + (xx + s) % inner) for zz, xx in cells]
+            held.append(lax.ppermute(mine, "ctx", route))
+        return held
+
+    first = weight[:stretch]
+    weights = [spread(first)]
+
     streams = jnp.transpose(feats, (1, 0, 2))
-    tail_f = streams[:, rows - reach - 2 :].astype(F32)
+    tail_f = after(streams[:, rows - reach - 2 :], first).astype(F32)
     by_tap = taps[:, :, None]
     tail_mix = by_tap[0] * tail_f[:, 2:] + by_tap[1] * tail_f[:, 1:-1] + by_tap[2] * tail_f[:, :-2]
     prod_tail = (tail_mix[1] * tail_mix[2]).astype(BF16)
     packed = jnp.concatenate([prod_tail] + [streams[i, rows - 2 :] for i in range(3)], axis=0)
     arrived = ahead(packed, "ctx", 1)
-
-    weights = []
-    for w in range(waves):
+    for w in range(1, waves):
         mine = weight[w * stretch : (w + 1) * stretch]
-        mine = after(mine, weights[-1][-1] if w else packed)
-        held = [mine]
-        for s in range(1, inner):
-            route = [(zz * inner + xx, zz * inner + (xx + s) % inner) for zz, xx in cells]
-            held.append(lax.ppermute(mine, "ctx", route))
-        weights.append(held)
+        weights.append(spread(after(mine, weights[-1][-1] if w > 1 else arrived)))
 
     tokens = []
     for s in range(outer):
@@ -258,6 +261,8 @@
             lo = wave * stretch + at * piece
             here = slice(at * piece, (at + 1) * piece)
             grad_y = after(sums[at], ready[at]) if wave else sums[at]
+            if at:
+                grad_y = after(grad_y, halos[-1])
             top = grad_y[: reach + 8].astype(F32)
             halo = jnp.concatenate(
                 [

time: 307 us -> 344 us (1.12)
  starting transfers between devices: 83.2 us -> 126 us
  waiting for transfers between devices: 112 us -> 101 us
  local copies, waits for them, and re-layouts: 15.6 us -> 19.7 us
    ppermute x2, waiting for transfers between devices: 47.1 us -> 0.01 us  [spread(): held.append(lax.ppermute(mine, 'ctx', route))]
    ppermute x6, waiting for transfers between devices: 13.9 us -> 45.4 us  [ahead(): lax.ppermute(block, axis, [(i - distance, i) for i in devices if i - dist...]
    ppermute x3, waiting for transfers between devices: 0.01 us -> 24.4 us  [local(): block = lax.ppermute(block, 'ctx', route)]
    ppermute x3, starting transfers between devices: 6.71 us -> 30.5 us  [local(): block = lax.ppermute(block, 'ctx', route)]
    ppermute x24, starting transfers between devices: 58.8 us -> 79.9 us  [local(): got = lax.ppermute(send, 'ctx', route)]
    ppermute x24, waiting for transfers between devices: 45 us -> 27.9 us  [local(): got = lax.ppermute(send, 'ctx', route)]
  transfers between devices with their start and end apart: 40 -> 40, of which waited for: 15 -> 9; matrix products, arithmetic and copies ran while one was open for 20% -> 18% of each run, Pallas kernels for 13% -> 11%
where the time goes in v4:
time: 344 us; the launch traced here: 340 us
  starting transfers between devices  126 us (37%)
  waiting for transfers between devices  101 us (29%)
  Pallas kernels  38.7 us (11%)
  other arithmetic  27.5 us (8%)
  matrix products  26.1 us (8%)
  local copies, waits for them, and re-layouts  19.7 us (6%)
    ppermute x24, starting transfers between devices, local(): got = lax.ppermute(send, 'ctx', route)  79.9 us
    ppermute x6, waiting for transfers between devices, ahead(): lax.ppermute(block, axis, [(i - distance, i) for i in devices if i - dist...  45.4 us
    pallas_call x6, Pallas kernels, tiled(): pl.pallas_call(functools.partial(kernel, group_width), grid=(channels //...  38.7 us
    ppermute x3, starting transfers between devices, local(): block = lax.ppermute(block, 'ctx', route)  30.5 us
    ppermute x24, waiting for transfers between devices, local(): got = lax.ppermute(send, 'ctx', route)  27.9 us
    dot_general x16, matrix products, partials(): jnp.einsum('tn,cn->tc', block, joined, preferred_element_type=F32)  26.1 us
    ppermute x3, waiting for transfers between devices, local(): block = lax.ppermute(block, 'ctx', route)  24.4 us
    convert_element_type x12, other arithmetic, local(): send = (send.astype(F32) + got.astype(F32)).astype(BF16)  12 us
  transfers between devices with their start and end apart: 40, of which 9 were waited for; matrix products, arithmetic and copies ran while one was open for 18% of the time, Pallas kernels for 11%

profile of v4, /device:TPU:0, one launch (start us, length us, event | category | flops | bytes accessed | tf_op | source)
XLA Modules:
  0.0 340.3 jit_solution(10895031128818710105)
XLA Ops:
  0.0 3.0 collective-permute-start
  3.0 4.5 %slice_bitcast_fusion.1 = (bf16[2048,512]{1,0:T(8,128)(2,1)}, bf16[2048,512]{1,0:T(8,128)(2,1)}) fusion(bf16[1,4096,512]{2,1,0:T(8,128)(2,1)} %param.8), kind=kLoop, calls=%fused_computation.13 | loop fusion | bytes 8388608 | tf_op jit(solution)/shard_map/slice | solution.py:159
  7.5 1.8 collective-permute-start.1
  11.2 1.9 fusion
  14.5 3.2 collective-permute-start.7
  20.0 3.1 slice_bitcast_fusion.3
  23.6 32.5 %collective-permute-done.13 = bf16[3,2,4096]{2,1,0:T(2,128)(2,1)S(1)} collective-permute-done((bf16[3,2,4096]{2,1,0:T(2,128)(2,1)S(1)}, bf16[3,2,4096]{2,1,0:T(2,128)(2,1)S(1)}, u32[]{:S(2)}, u32[]{:S(2)}) %collective-permute-start.13) | collective-permute-done | bytes 49184 | tf_op jit(solution)/shard_map/ppermute | solution.py:27
  56.2 1.3 constant_dynamic-update-slice_fusion
  59.4 26.7 %collective-permute-start.3 = (bf16[256,1024]{1,0:T(8,128)(2,1)}, bf16[256,1024]{1,0:T(8,128)(2,1)}, u32[]{:S(2)}, u32[]{:S(2)}) collective-permute-start(bf16[256,1024]{1,0:T(8,128)(2,1)} %pad_maximum_fusion.7), channel_id=1, source_target_pairs={{0,16},{4,20},{8,24},{12,28},{16,0},{20,4},{24,8},{28,12},{1,17},{... | collective-permute-start | bytes 1572872 | tf_op jit(solution)/shard_map/ppermute | solution.py:185
  87.0 1.6 collective-permute-start.4
  89.4 2.2 collective-permute-start.2
  93.2 1.3 slice.200.halo_ref
  94.8 2.1 fusion.22
  96.8 24.4 %collective-permute-done.3 = bf16[256,1024]{1,0:T(8,128)(2,1)} collective-permute-done((bf16[256,1024]{1,0:T(8,128)(2,1)}, bf16[256,1024]{1,0:T(8,128)(2,1)}, u32[]{:S(2)}, u32[]{:S(2)}) %collective-permute-start.3) | collective-permute-done | bytes 524320 | tf_op jit(solution)/shard_map/ppermute | solution.py:185
  121.3 1.8 convolution_convert_fusion.8
  123.1 1.8 convolution_convert_fusion.9
  124.9 11.0 %collective-permute-start.16 = (bf16[256,1024]{1,0:T(8,128)(2,1)S(1)}, bf16[256,1024]{1,0:T(8,128)(2,1)S(1)}, u32[]{:S(2)}, u32[]{:S(2)}) collective-permute-start(bf16[256,1024]{1,0:T(8,128)(2,1)S(1)} %convolution_convert_fusion.9), channel_id=1, source_target_pairs={{0,8},{4,12},{1,9},{5,13},{2,10},{6,14},{3,11},{7,15}} | collective-permute-start | bytes 1572872 | tf_op jit(solution)/shard_map/ppermute | solution.py:253
  135.9 1.8 convolution_convert_fusion.7
  138.4 1.8 convolution_convert_fusion.12
  140.2 1.5 collective-permute-start.5
  141.7 1.8 convolution_convert_fusion.14
  143.5 1.5 collective-permute-start.10
  145.0 1.5 convolution_convert_fusion.6
  146.5 1.8 convolution_convert_fusion.13
  148.7 4.2 %collective-permute-start.17 = (bf16[256,1024]{1,0:T(8,128)(2,1)S(1)}, bf16[256,1024]{1,0:T(8,128)(2,1)S(1)}, u32[]{:S(2)}, u32[]{:S(2)}) collective-permute-start(bf16[256,1024]{1,0:T(8,128)(2,1)S(1)} %get-tuple-element.80), channel_id=1, source_target_pairs={{0,8},{4,12},{8,16},{12,20},{1,9},{5,13},{9,17},{13,21},{2,10},{6,... | collective-permute-start | bytes 1572872 | tf_op jit(solution)/shard_map/ppermute | solution.py:253
  153.8 1.6 convolution_convert_fusion.15
  155.3 8.8 %shard_map.55 = (f32[256,2048]{1,0:T(8,128)S(1)}, f32[3,264,2048]{2,1,0:T(8,128)}) custom-call(bf16[3,256,4096]{2,1,0:T(8,128)(2,1)} %bitcast.74, f32[3,8,4096]{2,1,0:T(8,128)S(1)} %pad_convert_fusion.1.before_ref, f32[3,8,4096]{2,1,0:T(8,128)S(1)} %pad_convert_fusion.after_ref, f32[3,3,4096]{2,1,0:T(4,128)S(1)} %bitcast.68, ...), custom_call_target="tpu_custom_call" | custom-call | flops 2147483648 | bytes 17121280 | tf_op jit(solution)/shard_map/pallas_call | solution.py:113
  164.1 2.2 fusion.3
  166.3 1.5 collective-permute-start.11
  167.7 7.5 %collective-permute-start.6 = (bf16[256,1024]{1,0:T(8,128)(2,1)S(1)}, bf16[256,1024]{1,0:T(8,128)(2,1)S(1)}, u32[]{:S(2)}, u32[]{:S(2)}) collective-permute-start(bf16[256,1024]{1,0:T(8,128)(2,1)S(1)} %get-tuple-element.78), channel_id=1, source_target_pairs={{0,8},{4,12},{8,16},{12,20},{1,9},{5,13},{9,17},{13,21},{2,10},{6,... | collective-permute-start | bytes 1572872 | tf_op jit(solution)/shard_map/ppermute | solution.py:253
  175.2 8.8 %shard_map.58 = (f32[256,2048]{1,0:T(8,128)S(1)}, f32[3,264,2048]{2,1,0:T(8,128)}) custom-call(bf16[3,256,4096]{2,1,0:T(8,128)(2,1)} %bitcast.75, f32[3,8,4096]{2,1,0:T(8,128)S(1)} %pad_convert_fusion.1.before_ref, f32[3,8,4096]{2,1,0:T(8,128)S(1)} %pad_convert_fusion.after_ref, f32[3,3,4096]{2,1,0:T(4,128)S(1)} %bitcast.69, ...), custom_call_target="tpu_custom_call" | custom-call | flops 2147483648 | bytes 17121280 | tf_op jit(solution)/shard_map/pallas_call | solution.py:113
  186.6 1.7 fusion.21
  188.2 1.8 convolution_convert_fusion.11
  190.0 2.0 convolution_convert_fusion.10
  193.3 5.8 %collective-permute-start.9 = (bf16[256,1024]{1,0:T(8,128)(2,1)S(1)}, bf16[256,1024]{1,0:T(8,128)(2,1)S(1)}, u32[]{:S(2)}, u32[]{:S(2)}) collective-permute-start(bf16[256,1024]{1,0:T(8,128)(2,1)S(1)} %add_convert_fusion.11), channel_id=1, source_target_pairs={{0,8},{4,12},{8,16},{12,20},{16,24},{20,28},{1,9},{5,13},{9,17},{1... | collective-permute-start | bytes 1572872 | tf_op jit(solution)/shard_map/ppermute | solution.py:253
  199.1 1.8 convolution_convert_fusion
  200.9 1.8 convolution_convert_fusion.5
  202.7 4.0 %collective-permute-start.32 = (bf16[256,1024]{1,0:T(8,128)(2,1)S(1)}, bf16[256,1024]{1,0:T(8,128)(2,1)S(1)}, u32[]{:S(2)}, u32[]{:S(2)}) collective-permute-start(bf16[256,1024]{1,0:T(8,128)(2,1)S(1)} %convolution_convert_fusion.5), channel_id=1, source_target_pairs={{0,8},{4,12},{1,9},{5,13},{2,10},{6,14},{3,11},{7,15}} | collective-permute-start | bytes 1572872 | tf_op jit(solution)/shard_map/ppermute | solution.py:253
  206.8 1.8 convolution_convert_fusion.4
  210.8 4.6 %collective-permute-start.18 = (bf16[256,1024]{1,0:T(8,128)(2,1)S(1)}, bf16[256,1024]{1,0:T(8,128)(2,1)S(1)}, u32[]{:S(2)}, u32[]{:S(2)}) collective-permute-start(bf16[256,1024]{1,0:T(8,128)(2,1)S(1)} %add_convert_fusion.8), channel_id=1, source_target_pairs={{0,8},{4,12},{8,16},{12,20},{16,24},{20,28},{1,9},{5,13},{9,17},{1... | collective-permute-start | bytes 1572872 | tf_op jit(solution)/shard_map/ppermute | solution.py:253
  215.4 1.9 collective-permute-start.24
  218.8 2.9 collective-permute-done.21
  222.4 11.5 %collective-permute-done.18 = bf16[256,1024]{1,0:T(8,128)(2,1)S(1)} collective-permute-done((bf16[256,1024]{1,0:T(8,128)(2,1)S(1)}, bf16[256,1024]{1,0:T(8,128)(2,1)S(1)}, u32[]{:S(2)}, u32[]{:S(2)}) %collective-permute-start.18) | collective-permute-done | bytes 524320 | tf_op jit(solution)/shard_map/ppermute | solution.py:253
  236.6 1.5 collective-permute-start.36
  239.4 1.8 convolution_convert_fusion.2
  242.5 7.4 %collective-permute-start.33 = (bf16[256,1024]{1,0:T(8,128)(2,1)}, bf16[256,1024]{1,0:T(8,128)(2,1)}, u32[]{:S(2)}, u32[]{:S(2)}) collective-permute-start(bf16[256,1024]{1,0:T(8,128)(2,1)} %get-tuple-element.76), channel_id=1, source_target_pairs={{0,8},{4,12},{8,16},{12,20},{1,9},{5,13},{9,17},{13,21},{2,10},{6,... | collective-permute-start | bytes 1572872 | tf_op jit(solution)/shard_map/ppermute | solution.py:253
  249.9 1.3 fusion.7
  251.2 1.5 collective-permute-start.28
  252.7 4.1 %collective-permute-start.25 = (bf16[256,1024]{1,0:T(8,128)(2,1)}, bf16[256,1024]{1,0:T(8,128)(2,1)}, u32[]{:S(2)}, u32[]{:S(2)}) collective-permute-start(bf16[256,1024]{1,0:T(8,128)(2,1)} %get-tuple-element.74), channel_id=1, source_target_pairs={{0,8},{4,12},{8,16},{12,20},{1,9},{5,13},{9,17},{13,21},{2,10},{6,... | collective-permute-start | bytes 1572872 | tf_op jit(solution)/shard_map/ppermute | solution.py:253
  256.8 5.3 %shard_map.57 = bf16[3,256,1024]{2,1,0:T(8,128)(2,1)S(1)} custom-call(bf16[256,1024]{1,0:T(8,128)(2,1)S(1)} %add_convert_fusion.6.grad_ref, bf16[144,1024]{1,0:T(8,128)(2,1)S(1)} %collective-permute-done.22.halo_ref, f32[256,2048]{1,0:T(8,128)S(1)} %get-tuple-element.35.conv_ref, f32[3,264,2048]{2,1,0:T(8,128)} %get-tuple-element.34.mix_ref, ...), custom_call_target="tpu_custom_call" | custom-call | flops 1073741824 | bytes 12959744 | tf_op jit(solution)/shard_map/pallas_call | solution.py:113
  262.2 5.3 %shard_map.56 = bf16[3,256,1024]{2,1,0:T(8,128)(2,1)S(1)} custom-call(bf16[256,1024]{1,0:T(8,128)(2,1)S(1)} %add_convert_fusion.9.grad_ref, bf16[144,1024]{1,0:T(8,128)(2,1)S(1)} %collective-permute-done.14.halo_ref, f32[256,2048]{1,0:T(8,128)S(1)} %get-tuple-element.35.conv_ref, f32[3,264,2048]{2,1,0:T(8,128)} %get-tuple-element.34.mix_ref, ...), custom_call_target="tpu_custom_call" | custom-call | flops 1073741824 | bytes 12959744 | tf_op jit(solution)/shard_map/pallas_call | solution.py:113
  268.0 1.4 add_convert_fusion.1
  269.4 1.4 collective-permute-start.37
  270.9 1.4 add_convert_fusion.2
  272.3 9.6 %collective-permute-start.34 = (bf16[256,1024]{1,0:T(8,128)(2,1)S(1)}, bf16[256,1024]{1,0:T(8,128)(2,1)S(1)}, u32[]{:S(2)}, u32[]{:S(2)}) collective-permute-start(bf16[256,1024]{1,0:T(8,128)(2,1)S(1)} %add_convert_fusion.2), channel_id=1, source_target_pairs={{0,8},{4,12},{8,16},{12,20},{16,24},{20,28},{1,9},{5,13},{9,17},{1... | collective-permute-start | bytes 1572872 | tf_op jit(solution)/shard_map/ppermute | solution.py:253
  285.7 5.5 %collective-permute-done.37 = bf16[256,1024]{1,0:T(8,128)(2,1)S(1)} collective-permute-done((bf16[256,1024]{1,0:T(8,128)(2,1)S(1)}, bf16[256,1024]{1,0:T(8,128)(2,1)S(1)}, u32[]{:S(2)}, u32[]{:S(2)}) %collective-permute-start.37) | collective-permute-done | bytes 524320 | tf_op jit(solution)/shard_map/ppermute | solution.py:253
  291.2 4.0 %collective-permute-start.26 = (bf16[256,1024]{1,0:T(8,128)(2,1)S(1)}, bf16[256,1024]{1,0:T(8,128)(2,1)S(1)}, u32[]{:S(2)}, u32[]{:S(2)}) collective-permute-start(bf16[256,1024]{1,0:T(8,128)(2,1)S(1)} %add_convert_fusion.5), channel_id=1, source_target_pairs={{0,8},{4,12},{8,16},{12,20},{16,24},{20,28},{1,9},{5,13},{9,17},{1... | collective-permute-start | bytes 1572872 | tf_op jit(solution)/shard_map/ppermute | solution.py:253
  297.0 4.9 %collective-permute-done.29 = bf16[256,1024]{1,0:T(8,128)(2,1)S(1)} collective-permute-done((bf16[256,1024]{1,0:T(8,128)(2,1)S(1)}, bf16[256,1024]{1,0:T(8,128)(2,1)S(1)}, u32[]{:S(2)}, u32[]{:S(2)}) %collective-permute-start.29) | collective-permute-done | bytes 524320 | tf_op jit(solution)/shard_map/ppermute | solution.py:253
  301.9 3.0 collective-permute-done.26
  310.2 12.9 %collective-permute-done.38.halo_ref = bf16[144,1024]{1,0:T(8,128)(2,1)S(1)} collective-permute-done((bf16[144,1024]{1,0:T(8,128)(2,1)S(1)}, bf16[144,1024]{1,0:T(8,128)(2,1)S(1)}, u32[]{:S(2)}, u32[]{:S(2)}) %collective-permute-start.38) | collective-permute-done | bytes 294944 | tf_op jit(solution)/shard_map/ppermute | solution.py:27
  323.1 5.3 %shard_map.60 = bf16[3,256,1024]{2,1,0:T(8,128)(2,1)S(1)} custom-call(bf16[256,1024]{1,0:T(8,128)(2,1)S(1)} %add_convert_fusion.grad_ref, bf16[144,1024]{1,0:T(8,128)(2,1)S(1)} %collective-permute-done.38.halo_ref, f32[256,2048]{1,0:T(8,128)S(1)} %get-tuple-element.46.conv_ref, f32[3,264,2048]{2,1,0:T(8,128)} %get-tuple-element.45.mix_ref, ...), custom_call_target="tpu_custom_call" | custom-call | flops 1073741824 | bytes 12959744 | tf_op jit(solution)/shard_map/pallas_call | solution.py:113
  328.4 5.3 %shard_map.59 = bf16[3,256,1024]{2,1,0:T(8,128)(2,1)S(1)} custom-call(bf16[256,1024]{1,0:T(8,128)(2,1)S(1)} %add_convert_fusion.3.grad_ref, bf16[144,1024]{1,0:T(8,128)(2,1)S(1)} %collective-permute-done.30.halo_ref, f32[256,2048]{1,0:T(8,128)S(1)} %get-tuple-element.46.conv_ref, f32[3,264,2048]{2,1,0:T(8,128)} %get-tuple-element.45.mix_ref, ...), custom_call_target="tpu_custom_call" | custom-call | flops 1073741824 | bytes 12959744 | tf_op jit(solution)/shard_map/pallas_call | solution.py:113
  334.3 3.0 collective-permute-done.31
  337.3 3.0 maximum_bitcast_fusion
  (152 shorter events, 38.3 us)
Async XLA Ops:
  0.0 9.3 %copy-start = (bf16[1,256,3,4096]{3,1,2,0:T(8,128)(2,1)S(1)}, bf16[1,256,3,4096]{3,1,2,0:T(8,128)(2,1)}, u32[]{:S(2)}) copy-start(bf16[1,256,3,4096]{3,1,2,0:T(8,128)(2,1)} %param.5) | copy-start | bytes 18874372
  0.0 56.2 %collective-permute-start = (bf16[256,2048]{1,0:T(8,128)(2,1)}, bf16[256,2048]{1,0:T(8,128)(2,1)}, u32[]{:S(2)}, u32[]{:S(2)}) collective-permute-start(bf16[256,2048]{1,0:T(8,128)(2,1)} %bitcast.79), channel_id=1, source_target_pairs={{0,2},{2,0},{1,3},{3,1},{4,6},{6,4},{5,7},{7,5},{8,10},{10,8},{9,1... | collective-permute-start | bytes 3145736 | tf_op jit(solution)/shard_map/ppermute | solution.py:149
  7.5 87.2 %collective-permute-start.1 = (bf16[2048,512]{1,0:T(8,128)(2,1)}, bf16[2048,512]{1,0:T(8,128)(2,1)}, u32[]{:S(2)}, u32[]{:S(2)}) collective-permute-start(bf16[2048,512]{1,0:T(8,128)(2,1)} %get-tuple-element.58), channel_id=1, source_target_pairs={{0,4},{4,0},{8,12},{12,8},{16,20},{20,16},{24,28},{28,24},{1,5},{5... | collective-permute-start | bytes 6291464 | tf_op jit(solution)/shard_map/ppermute | solution.py:156
  10.2 0.9 copy-start.7
  13.3 5.9 %copy-start.2 = (bf16[1,256,2048]{2,1,0:T(8,128)(2,1)S(1)}, bf16[1,256,2048]{2,1,0:T(8,128)(2,1)}, u32[]{:S(2)}) copy-start(bf16[1,256,2048]{2,1,0:T(8,128)(2,1)} %param.9) | copy-start | bytes 3145732
  14.5 77.2 %collective-permute-start.7 = (bf16[134,4096]{1,0:T(8,128)(2,1)}, bf16[134,4096]{1,0:T(8,128)(2,1)}, u32[]{:S(2)}, u32[]{:S(2)}) collective-permute-start(bf16[134,4096]{1,0:T(8,128)(2,1)} %pad_maximum_fusion.4), channel_id=1, source_target_pairs={{0,4},{4,8},{8,12},{12,16},{16,20},{20,24},{24,28},{1,5},{5,9},{9,... | collective-permute-start | bytes 3293192 | tf_op jit(solution)/shard_map/ppermute | solution.py:27
  17.7 38.5 %collective-permute-start.13 = (bf16[3,2,4096]{2,1,0:T(2,128)(2,1)S(1)}, bf16[3,2,4096]{2,1,0:T(2,128)(2,1)S(1)}, u32[]{:S(2)}, u32[]{:S(2)}) collective-permute-start(bf16[3,2,4096]{2,1,0:T(2,128)(2,1)S(1)} %slice.199), channel_id=1, source_target_pairs={{4,0},{8,4},{12,8},{16,12},{20,16},{24,20},{28,24},{5,1},{9,5},{13... | collective-permute-start | bytes 147464 | tf_op jit(solution)/shard_map/ppermute | solution.py:27
  19.0 0.8 copy-start.23
  58.5 33.2 %copy-start.1 = (bf16[2048,512]{1,0:T(8,128)(2,1)S(1)}, bf16[2048,512]{1,0:T(8,128)(2,1)}, u32[]{:S(2)}) copy-start(bf16[2048,512]{1,0:T(8,128)(2,1)} %get-tuple-element.30) | copy-start | bytes 6291460
  59.4 61.9 %collective-permute-start.3 = (bf16[256,1024]{1,0:T(8,128)(2,1)}, bf16[256,1024]{1,0:T(8,128)(2,1)}, u32[]{:S(2)}, u32[]{:S(2)}) collective-permute-start(bf16[256,1024]{1,0:T(8,128)(2,1)} %pad_maximum_fusion.7), channel_id=1, source_target_pairs={{0,16},{4,20},{8,24},{12,28},{16,0},{20,4},{24,8},{28,12},{1,17},{... | collective-permute-start | bytes 1572872 | tf_op jit(solution)/shard_map/ppermute | solution.py:185
  87.0 36.1 %collective-permute-start.4 = (bf16[256,1024]{1,0:T(8,128)(2,1)}, bf16[256,1024]{1,0:T(8,128)(2,1)}, u32[]{:S(2)}, u32[]{:S(2)}) collective-permute-start(bf16[256,1024]{1,0:T(8,128)(2,1)} %pad_maximum_fusion.8), channel_id=1, source_target_pairs={{0,8},{4,12},{8,16},{12,20},{16,24},{20,28},{24,0},{28,4},{1,9},{5... | collective-permute-start | bytes 1572872 | tf_op jit(solution)/shard_map/ppermute | solution.py:185
  89.4 46.5 %collective-permute-start.2 = (bf16[256,1024]{1,0:T(8,128)(2,1)}, bf16[256,1024]{1,0:T(8,128)(2,1)}, u32[]{:S(2)}, u32[]{:S(2)}) collective-permute-start(bf16[256,1024]{1,0:T(8,128)(2,1)} %pad_maximum_fusion.6), channel_id=1, source_target_pairs={{0,24},{4,28},{8,0},{12,4},{16,8},{20,12},{24,16},{28,20},{1,25},{... | collective-permute-start | bytes 1572872 | tf_op jit(solution)/shard_map/ppermute | solution.py:185
  91.7 94.9 %collective-permute-start.8 = (bf16[2048,512]{1,0:T(8,128)(2,1)S(1)}, bf16[2048,512]{1,0:T(8,128)(2,1)}, u32[]{:S(2)}, u32[]{:S(2)}) collective-permute-start(bf16[2048,512]{1,0:T(8,128)(2,1)S(1)} %copy-done.1), channel_id=1, source_target_pairs={{0,4},{4,0},{8,12},{12,8},{16,20},{20,16},{24,28},{28,24},{1,5},{5... | collective-permute-start | bytes 6291464 | tf_op jit(solution)/shard_map/ppermute | solution.py:156
  93.2 1.3 copy-start.22
  94.7 112.1 %copy-start.5 = (bf16[1024,512]{1,0:T(8,128)(2,1)}, bf16[1024,512]{1,0:T(8,128)(2,1)S(1)}, u32[]{:S(2)}) copy-start(bf16[1024,512]{1,0:T(8,128)(2,1)S(1)} %get-tuple-element.61) | copy-start | bytes 3145732
  94.7 26.5 %copy-start.4 = (bf16[1024,512]{1,0:T(8,128)(2,1)S(1)}, bf16[1024,512]{1,0:T(8,128)(2,1)}, u32[]{:S(2)}) copy-start(bf16[1024,512]{1,0:T(8,128)(2,1)} %get-tuple-element.57) | copy-start | bytes 3145732
  124.9 13.5 %copy-start.3 = (bf16[1024,512]{1,0:T(8,128)(2,1)S(1)}, bf16[1024,512]{1,0:T(8,128)(2,1)}, u32[]{:S(2)}) copy-start(bf16[1024,512]{1,0:T(8,128)(2,1)} %get-tuple-element.56) | copy-start | bytes 3145732
  124.9 23.4 %collective-permute-start.16 = (bf16[256,1024]{1,0:T(8,128)(2,1)S(1)}, bf16[256,1024]{1,0:T(8,128)(2,1)S(1)}, u32[]{:S(2)}, u32[]{:S(2)}) collective-permute-start(bf16[256,1024]{1,0:T(8,128)(2,1)S(1)} %convolution_convert_fusion.9), channel_id=1, source_target_pairs={{0,8},{4,12},{1,9},{5,13},{2,10},{6,14},{3,11},{7,15}} | collective-permute-start | bytes 1572872 | tf_op jit(solution)/shard_map/ppermute | solution.py:253
  137.7 2.5 copy-start.14
  137.7 10.6 %collective-permute-start.19 = (bf16[256,1024]{1,0:T(8,128)(2,1)S(1)}, bf16[256,1024]{1,0:T(8,128)(2,1)S(1)}, u32[]{:S(2)}, u32[]{:S(2)}) collective-permute-start(bf16[256,1024]{1,0:T(8,128)(2,1)S(1)} %convolution_convert_fusion.7), channel_id=1, source_target_pairs={{24,16},{28,20},{25,17},{29,21},{26,18},{30,22},{27,19},{31,23}} | collective-permute-start | bytes 1572872 | tf_op jit(solution)/shard_map/ppermute | solution.py:253
  140.2 3.3 copy-start.16
  140.2 4.8 %copy-start.20 = (bf16[256,512]{1,0:T(8,128)(2,1)S(1)}, bf16[256,512]{1,0:T(8,128)(2,1)}, u32[]{:S(2)}) copy-start(bf16[256,512]{1,0:T(8,128)(2,1)} %get-tuple-element.73) | copy-start | bytes 786436
  140.2 23.9 %collective-permute-start.5 = (bf16[256,1024]{1,0:T(8,128)(2,1)S(1)}, bf16[256,1024]{1,0:T(8,128)(2,1)S(1)}, u32[]{:S(2)}, u32[]{:S(2)}) collective-permute-start(bf16[256,1024]{1,0:T(8,128)(2,1)S(1)} %convolution_convert_fusion.12), channel_id=1, source_target_pairs={{0,8},{4,12},{1,9},{5,13},{2,10},{6,14},{3,11},{7,15}} | collective-permute-start | bytes 1572872 | tf_op jit(solution)/shard_map/ppermute | solution.py:253
  143.5 3.1 copy-start.12
  143.5 20.6 %collective-permute-start.10 = (bf16[256,1024]{1,0:T(8,128)(2,1)S(1)}, bf16[256,1024]{1,0:T(8,128)(2,1)}, u32[]{:S(2)}, u32[]{:S(2)}) collective-permute-start(bf16[256,1024]{1,0:T(8,128)(2,1)S(1)} %convolution_convert_fusion.14), channel_id=1, source_target_pairs={{24,16},{28,20},{25,17},{29,21},{26,18},{30,22},{27,19},{31,23}} | collective-permute-start | bytes 1572872 | tf_op jit(solution)/shard_map/ppermute | solution.py:253
  148.7 26.5 %collective-permute-start.17 = (bf16[256,1024]{1,0:T(8,128)(2,1)S(1)}, bf16[256,1024]{1,0:T(8,128)(2,1)S(1)}, u32[]{:S(2)}, u32[]{:S(2)}) collective-permute-start(bf16[256,1024]{1,0:T(8,128)(2,1)S(1)} %get-tuple-element.80), channel_id=1, source_target_pairs={{0,8},{4,12},{8,16},{12,20},{1,9},{5,13},{9,17},{13,21},{2,10},{6,... | collective-permute-start | bytes 1572872 | tf_op jit(solution)/shard_map/ppermute | solution.py:253
  152.9 22.3 %collective-permute-start.20 = (bf16[256,1024]{1,0:T(8,128)(2,1)S(1)}, bf16[256,1024]{1,0:T(8,128)(2,1)S(1)}, u32[]{:S(2)}, u32[]{:S(2)}) collective-permute-start(bf16[256,1024]{1,0:T(8,128)(2,1)S(1)} %get-tuple-element.81), channel_id=1, source_target_pairs={{16,8},{20,12},{24,16},{28,20},{17,9},{21,13},{25,17},{29,21},{18,... | collective-permute-start | bytes 1572872 | tf_op jit(solution)/shard_map/ppermute | solution.py:253
  166.3 18.2 %collective-permute-start.11 = (bf16[256,1024]{1,0:T(8,128)(2,1)}, bf16[256,1024]{1,0:T(8,128)(2,1)}, u32[]{:S(2)}, u32[]{:S(2)}) collective-permute-start(bf16[256,1024]{1,0:T(8,128)(2,1)} %get-tuple-element.79), channel_id=1, source_target_pairs={{16,8},{20,12},{24,16},{28,20},{17,9},{21,13},{25,17},{29,21},{18,... | collective-permute-start | bytes 1572872 | tf_op jit(solution)/shard_map/ppermute | solution.py:253
  167.7 16.5 %copy-start.15 = (bf16[256,1024]{1,0:T(8,128)(2,1)S(1)}, bf16[256,1024]{1,0:T(8,128)(2,1)}, u32[]{:S(2)}) copy-start(bf16[256,1024]{1,0:T(8,128)(2,1)} %copy-done.14) | copy-start | bytes 1572868
  167.7 18.6 %collective-permute-start.6 = (bf16[256,1024]{1,0:T(8,128)(2,1)S(1)}, bf16[256,1024]{1,0:T(8,128)(2,1)S(1)}, u32[]{:S(2)}, u32[]{:S(2)}) collective-permute-start(bf16[256,1024]{1,0:T(8,128)(2,1)S(1)} %get-tuple-element.78), channel_id=1, source_target_pairs={{0,8},{4,12},{8,16},{12,20},{1,9},{5,13},{9,17},{13,21},{2,10},{6,... | collective-permute-start | bytes 1572872 | tf_op jit(solution)/shard_map/ppermute | solution.py:253
  184.1 1.0 copy-start.17
  184.1 2.3 copy-start.13
  190.0 25.3 %copy-start.8 = (bf16[256,1024]{1,0:T(8,128)(2,1)}, bf16[256,1024]{1,0:T(8,128)(2,1)S(1)}, u32[]{:S(2)}) copy-start(bf16[256,1024]{1,0:T(8,128)(2,1)S(1)} %convolution_convert_fusion.11) | copy-start | bytes 1572868
  192.0 18.7 %collective-permute-start.12 = (bf16[256,1024]{1,0:T(8,128)(2,1)S(1)}, bf16[256,1024]{1,0:T(8,128)(2,1)S(1)}, u32[]{:S(2)}, u32[]{:S(2)}) collective-permute-start(bf16[256,1024]{1,0:T(8,128)(2,1)S(1)} %add_convert_fusion.10), channel_id=1, source_target_pairs={{8,0},{12,4},{16,8},{20,12},{24,16},{28,20},{9,1},{13,5},{17,9},{2... | collective-permute-start | bytes 1572872 | tf_op jit(solution)/shard_map/ppermute | solution.py:253
  193.3 22.0 %collective-permute-start.9 = (bf16[256,1024]{1,0:T(8,128)(2,1)S(1)}, bf16[256,1024]{1,0:T(8,128)(2,1)S(1)}, u32[]{:S(2)}, u32[]{:S(2)}) collective-permute-start(bf16[256,1024]{1,0:T(8,128)(2,1)S(1)} %add_convert_fusion.11), channel_id=1, source_target_pairs={{0,8},{4,12},{8,16},{12,20},{16,24},{20,28},{1,9},{5,13},{9,17},{1... | collective-permute-start | bytes 1572872 | tf_op jit(solution)/shard_map/ppermute | solution.py:253
  202.7 31.6 %copy-start.11 = (bf16[256,1024]{1,0:T(8,128)(2,1)}, bf16[256,1024]{1,0:T(8,128)(2,1)S(1)}, u32[]{:S(2)}) copy-start(bf16[256,1024]{1,0:T(8,128)(2,1)S(1)} %convolution_convert_fusion.5) | copy-start | bytes 1572868
  202.7 14.6 %copy-start.19 = (bf16[256,1024]{1,0:T(8,128)(2,1)S(1)}, bf16[256,1024]{1,0:T(8,128)(2,1)}, u32[]{:S(2)}) copy-start(bf16[256,1024]{1,0:T(8,128)(2,1)} %convolution_convert_fusion.15) | copy-start | bytes 1572868
  202.7 32.7 %collective-permute-start.32 = (bf16[256,1024]{1,0:T(8,128)(2,1)S(1)}, bf16[256,1024]{1,0:T(8,128)(2,1)S(1)}, u32[]{:S(2)}, u32[]{:S(2)}) collective-permute-start(bf16[256,1024]{1,0:T(8,128)(2,1)S(1)} %convolution_convert_fusion.5), channel_id=1, source_target_pairs={{0,8},{4,12},{1,9},{5,13},{2,10},{6,14},{3,11},{7,15}} | collective-permute-start | bytes 1572872 | tf_op jit(solution)/shard_map/ppermute | solution.py:253
  208.6 32.6 %copy-start.10 = (bf16[256,1024]{1,0:T(8,128)(2,1)}, bf16[256,1024]{1,0:T(8,128)(2,1)S(1)}, u32[]{:S(2)}) copy-start(bf16[256,1024]{1,0:T(8,128)(2,1)S(1)} %convolution_convert_fusion.4) | copy-start | bytes 1572868
  208.6 25.3 %copy-start.18 = (bf16[256,1024]{1,0:T(8,128)(2,1)S(1)}, bf16[256,1024]{1,0:T(8,128)(2,1)}, u32[]{:S(2)}) copy-start(bf16[256,1024]{1,0:T(8,128)(2,1)} %convolution_convert_fusion.6) | copy-start | bytes 1572868
  208.6 26.8 %collective-permute-start.35 = (bf16[256,1024]{1,0:T(8,128)(2,1)S(1)}, bf16[256,1024]{1,0:T(8,128)(2,1)S(1)}, u32[]{:S(2)}, u32[]{:S(2)}) collective-permute-start(bf16[256,1024]{1,0:T(8,128)(2,1)S(1)} %convolution_convert_fusion.4), channel_id=1, source_target_pairs={{24,16},{28,20},{25,17},{29,21},{26,18},{30,22},{27,19},{31,23}} | collective-permute-start | bytes 1572872 | tf_op jit(solution)/shard_map/ppermute | solution.py:253
  209.4 12.3 %collective-permute-start.21 = (bf16[256,1024]{1,0:T(8,128)(2,1)S(1)}, bf16[256,1024]{1,0:T(8,128)(2,1)S(1)}, u32[]{:S(2)}, u32[]{:S(2)}) collective-permute-start(bf16[256,1024]{1,0:T(8,128)(2,1)S(1)} %add_convert_fusion.7), channel_id=1, source_target_pairs={{8,0},{12,4},{16,8},{20,12},{24,16},{28,20},{9,1},{13,5},{17,9},{2... | collective-permute-start | bytes 1572872 | tf_op jit(solution)/shard_map/ppermute | solution.py:253
  210.8 23.2 %collective-permute-start.18 = (bf16[256,1024]{1,0:T(8,128)(2,1)S(1)}, bf16[256,1024]{1,0:T(8,128)(2,1)S(1)}, u32[]{:S(2)}, u32[]{:S(2)}) collective-permute-start(bf16[256,1024]{1,0:T(8,128)(2,1)S(1)} %add_convert_fusion.8), channel_id=1, source_target_pairs={{0,8},{4,12},{8,16},{12,20},{16,24},{20,28},{1,9},{5,13},{9,17},{1... | collective-permute-start | bytes 1572872 | tf_op jit(solution)/shard_map/ppermute | solution.py:253
  215.4 27.1 %collective-permute-start.24 = (bf16[256,1024]{1,0:T(8,128)(2,1)S(1)}, bf16[256,1024]{1,0:T(8,128)(2,1)S(1)}, u32[]{:S(2)}, u32[]{:S(2)}) collective-permute-start(bf16[256,1024]{1,0:T(8,128)(2,1)S(1)} %convolution_convert_fusion.11), channel_id=1, source_target_pairs={{0,8},{4,12},{1,9},{5,13},{2,10},{6,14},{3,11},{7,15}} | collective-permute-start | bytes 1572872 | tf_op jit(solution)/shard_map/ppermute | solution.py:253
  221.7 28.2 %collective-permute-start.27 = (bf16[256,1024]{1,0:T(8,128)(2,1)S(1)}, bf16[256,1024]{1,0:T(8,128)(2,1)S(1)}, u32[]{:S(2)}, u32[]{:S(2)}) collective-permute-start(bf16[256,1024]{1,0:T(8,128)(2,1)S(1)} %convolution_convert_fusion.10), channel_id=1, source_target_pairs={{24,16},{28,20},{25,17},{29,21},{26,18},{30,22},{27,19},{31,23}} | collective-permute-start | bytes 1572872 | tf_op jit(solution)/shard_map/ppermute | solution.py:253
  236.6 30.9 %collective-permute-start.36 = (bf16[256,1024]{1,0:T(8,128)(2,1)S(1)}, bf16[256,1024]{1,0:T(8,128)(2,1)}, u32[]{:S(2)}, u32[]{:S(2)}) collective-permute-start(bf16[256,1024]{1,0:T(8,128)(2,1)S(1)} %get-tuple-element.77), channel_id=1, source_target_pairs={{16,8},{20,12},{24,16},{28,20},{17,9},{21,13},{25,17},{29,21},{18,... | collective-permute-start | bytes 1572872 | tf_op jit(solution)/shard_map/ppermute | solution.py:253
  238.1 14.6 %collective-permute-start.22 = (bf16[144,1024]{1,0:T(8,128)(2,1)S(1)}, bf16[144,1024]{1,0:T(8,128)(2,1)S(1)}, u32[]{:S(2)}, u32[]{:S(2)}) collective-permute-start(bf16[144,1024]{1,0:T(8,128)(2,1)S(1)} %pad_maximum_fusion.10), channel_id=1, source_target_pairs={{4,0},{8,4},{12,8},{16,12},{20,16},{24,20},{28,24},{5,1},{9,5},{13... | collective-permute-start | bytes 884744 | tf_op jit(solution)/shard_map/ppermute | solution.py:27
  241.2 20.9 %collective-permute-start.14 = (bf16[144,1024]{1,0:T(8,128)(2,1)S(1)}, bf16[144,1024]{1,0:T(8,128)(2,1)S(1)}, u32[]{:S(2)}, u32[]{:S(2)}) collective-permute-start(bf16[144,1024]{1,0:T(8,128)(2,1)S(1)} %pad_maximum_fusion.9), channel_id=1, source_target_pairs={{4,0},{8,4},{12,8},{16,12},{20,16},{24,20},{28,24},{5,1},{9,5},{13... | collective-permute-start | bytes 884744 | tf_op jit(solution)/shard_map/ppermute | solution.py:27
  242.5 26.9 %collective-permute-start.33 = (bf16[256,1024]{1,0:T(8,128)(2,1)}, bf16[256,1024]{1,0:T(8,128)(2,1)}, u32[]{:S(2)}, u32[]{:S(2)}) collective-permute-start(bf16[256,1024]{1,0:T(8,128)(2,1)} %get-tuple-element.76), channel_id=1, source_target_pairs={{0,8},{4,12},{8,16},{12,20},{1,9},{5,13},{9,17},{13,21},{2,10},{6,... | collective-permute-start | bytes 1572872 | tf_op jit(solution)/shard_map/ppermute | solution.py:253
  251.2 21.0 %collective-permute-start.28 = (bf16[256,1024]{1,0:T(8,128)(2,1)}, bf16[256,1024]{1,0:T(8,128)(2,1)}, u32[]{:S(2)}, u32[]{:S(2)}) collective-permute-start(bf16[256,1024]{1,0:T(8,128)(2,1)} %get-tuple-element.75), channel_id=1, source_target_pairs={{16,8},{20,12},{24,16},{28,20},{17,9},{21,13},{25,17},{29,21},{18,... | collective-permute-start | bytes 1572872 | tf_op jit(solution)/shard_map/ppermute | solution.py:253
  252.7 30.4 %collective-permute-start.25 = (bf16[256,1024]{1,0:T(8,128)(2,1)}, bf16[256,1024]{1,0:T(8,128)(2,1)}, u32[]{:S(2)}, u32[]{:S(2)}) collective-permute-start(bf16[256,1024]{1,0:T(8,128)(2,1)} %get-tuple-element.74), channel_id=1, source_target_pairs={{0,8},{4,12},{8,16},{12,20},{1,9},{5,13},{9,17},{13,21},{2,10},{6,... | collective-permute-start | bytes 1572872 | tf_op jit(solution)/shard_map/ppermute | solution.py:253
  262.1 43.0 %collective-permute-start.23 = (bf16[3,256,1024]{2,1,0:T(8,128)(2,1)S(1)}, bf16[3,256,1024]{2,1,0:T(8,128)(2,1)S(1)}, u32[]{:S(2)}, u32[]{:S(2)}) collective-permute-start(bf16[3,256,1024]{2,1,0:T(8,128)(2,1)S(1)} %shard_map.57), channel_id=1, source_target_pairs={{0,1},{1,0},{2,3},{3,2},{4,5},{5,4},{6,7},{7,6},{8,9},{9,8},{10,11... | collective-permute-start | bytes 4718600 | tf_op jit(solution)/shard_map/ppermute | solution.py:292
  267.4 14.4 %copy-start.9 = (bf16[256,1024]{1,0:T(8,128)(2,1)S(1)}, bf16[256,1024]{1,0:T(8,128)(2,1)}, u32[]{:S(2)}) copy-start(bf16[256,1024]{1,0:T(8,128)(2,1)} %copy-done.8) | copy-start | bytes 1572868
  267.5 37.7 %collective-permute-start.15 = (bf16[3,256,1024]{2,1,0:T(8,128)(2,1)S(1)}, bf16[3,256,1024]{2,1,0:T(8,128)(2,1)S(1)}, u32[]{:S(2)}, u32[]{:S(2)}) collective-permute-start(bf16[3,256,1024]{2,1,0:T(8,128)(2,1)S(1)} %shard_map.56), channel_id=1, source_target_pairs={{0,1},{1,0},{2,3},{3,2},{4,5},{5,4},{6,7},{7,6},{8,9},{9,8},{10,11... | collective-permute-start | bytes 4718600 | tf_op jit(solution)/shard_map/ppermute | solution.py:292
  269.4 25.8 %copy-start.6 = (bf16[1024,512]{1,0:T(8,128)(2,1)S(1)}, bf16[1024,512]{1,0:T(8,128)(2,1)}, u32[]{:S(2)}) copy-start(bf16[1024,512]{1,0:T(8,128)(2,1)} %copy-done.5) | copy-start | bytes 3145732
  269.4 25.8 %copy-start.21 = (bf16[256,512]{1,0:T(8,128)(2,1)S(1)}, bf16[256,512]{1,0:T(8,128)(2,1)}, u32[]{:S(2)}) copy-start(bf16[256,512]{1,0:T(8,128)(2,1)} %get-tuple-element.73) | copy-start | bytes 786436
  269.4 21.8 %collective-permute-start.37 = (bf16[256,1024]{1,0:T(8,128)(2,1)S(1)}, bf16[256,1024]{1,0:T(8,128)(2,1)S(1)}, u32[]{:S(2)}, u32[]{:S(2)}) collective-permute-start(bf16[256,1024]{1,0:T(8,128)(2,1)S(1)} %add_convert_fusion.1), channel_id=1, source_target_pairs={{8,0},{12,4},{16,8},{20,12},{24,16},{28,20},{9,1},{13,5},{17,9},{2... | collective-permute-start | bytes 1572872 | tf_op jit(solution)/shard_map/ppermute | solution.py:253
  272.3 24.4 %collective-permute-start.34 = (bf16[256,1024]{1,0:T(8,128)(2,1)S(1)}, bf16[256,1024]{1,0:T(8,128)(2,1)S(1)}, u32[]{:S(2)}, u32[]{:S(2)}) collective-permute-start(bf16[256,1024]{1,0:T(8,128)(2,1)S(1)} %add_convert_fusion.2), channel_id=1, source_target_pairs={{0,8},{4,12},{8,16},{12,20},{16,24},{20,28},{1,9},{5,13},{9,17},{1... | collective-permute-start | bytes 1572872 | tf_op jit(solution)/shard_map/ppermute | solution.py:253
  283.1 18.8 %collective-permute-start.29 = (bf16[256,1024]{1,0:T(8,128)(2,1)S(1)}, bf16[256,1024]{1,0:T(8,128)(2,1)S(1)}, u32[]{:S(2)}, u32[]{:S(2)}) collective-permute-start(bf16[256,1024]{1,0:T(8,128)(2,1)S(1)} %add_convert_fusion.4), channel_id=1, source_target_pairs={{8,0},{12,4},{16,8},{20,12},{24,16},{28,20},{9,1},{13,5},{17,9},{2... | collective-permute-start | bytes 1572872 | tf_op jit(solution)/shard_map/ppermute | solution.py:253
  291.2 13.6 %collective-permute-start.26 = (bf16[256,1024]{1,0:T(8,128)(2,1)S(1)}, bf16[256,1024]{1,0:T(8,128)(2,1)S(1)}, u32[]{:S(2)}, u32[]{:S(2)}) collective-permute-start(bf16[256,1024]{1,0:T(8,128)(2,1)S(1)} %add_convert_fusion.5), channel_id=1, source_target_pairs={{0,8},{4,12},{8,16},{12,20},{16,24},{20,28},{1,9},{5,13},{9,17},{1... | collective-permute-start | bytes 1572872 | tf_op jit(solution)/shard_map/ppermute | solution.py:253
  307.6 15.5 %collective-permute-start.38 = (bf16[144,1024]{1,0:T(8,128)(2,1)S(1)}, bf16[144,1024]{1,0:T(8,128)(2,1)S(1)}, u32[]{:S(2)}, u32[]{:S(2)}) collective-permute-start(bf16[144,1024]{1,0:T(8,128)(2,1)S(1)} %pad_maximum_fusion.12), channel_id=1, source_target_pairs={{4,0},{8,4},{12,8},{16,12},{20,16},{24,20},{28,24},{5,1},{9,5},{13... | collective-permute-start | bytes 884744 | tf_op jit(solution)/shard_map/ppermute | solution.py:27
  308.9 19.5 %collective-permute-start.30 = (bf16[144,1024]{1,0:T(8,128)(2,1)S(1)}, bf16[144,1024]{1,0:T(8,128)(2,1)S(1)}, u32[]{:S(2)}, u32[]{:S(2)}) collective-permute-start(bf16[144,1024]{1,0:T(8,128)(2,1)S(1)} %pad_maximum_fusion.11), channel_id=1, source_target_pairs={{4,0},{8,4},{12,8},{16,12},{20,16},{24,20},{28,24},{5,1},{9,5},{13... | collective-permute-start | bytes 884744 | tf_op jit(solution)/shard_map/ppermute | solution.py:27
  328.3 5.9 %collective-permute-start.39 = (bf16[3,256,1024]{2,1,0:T(8,128)(2,1)S(1)}, bf16[3,256,1024]{2,1,0:T(8,128)(2,1)S(1)}, u32[]{:S(2)}, u32[]{:S(2)}) collective-permute-start(bf16[3,256,1024]{2,1,0:T(8,128)(2,1)S(1)} %shard_map.60), channel_id=1, source_target_pairs={{0,1},{1,0},{2,3},{3,2},{4,5},{5,4},{6,7},{7,6},{8,9},{9,8},{10,11... | collective-permute-start | bytes 4718600 | tf_op jit(solution)/shard_map/ppermute | solution.py:292
  333.7 3.6 %collective-permute-start.31 = (bf16[3,256,1024]{2,1,0:T(8,128)(2,1)S(1)}, bf16[3,256,1024]{2,1,0:T(8,128)(2,1)S(1)}, u32[]{:S(2)}, u32[]{:S(2)}) collective-permute-start(bf16[3,256,1024]{2,1,0:T(8,128)(2,1)S(1)} %shard_map.59), channel_id=1, source_target_pairs={{0,1},{1,0},{2,3},{3,2},{4,5},{5,4},{6,7},{7,6},{8,9},{9,8},{10,11... | collective-permute-start | bytes 4718600 | tf_op jit(solution)/shard_map/ppermute | solution.py:292

commit v5 on v3

--- a/solution.py
+++ b/solution.py
@@ -150,6 +150,8 @@
         full = lax.dynamic_update_slice(full, got, (0, (tp_place - s) % tp_count * share))
 
     streams = jnp.transpose(feats, (1, 0, 2))
+    opening = streams[:, :2]
+    behind = ahead(opening, "ctx", -1)
     tail_f = streams[:, rows - reach - 2 :].astype(F32)
     by_tap = taps[:, :, None]
     tail_mix = by_tap[0] * tail_f[:, 2:] + by_tap[1] * tail_f[:, 1:-1] + by_tap[2] * tail_f[:, :-2]
@@ -157,15 +159,17 @@
     packed = jnp.concatenate([prod_tail] + [streams[i, rows - 2 :] for i in range(3)], axis=0)
     arrived = ahead(packed, "ctx", 1)
 
-    weights = []
-    for w in range(waves):
-        mine = weight[w * stretch : (w + 1) * stretch]
-        mine = after(mine, weights[-1][-1] if w else packed)
+    def spread(mine):
         held = [mine]
         for s in range(1, inner):
             route = [(zz * inner + xx, zz * inner + (xx + s) % inner) for zz, xx in cells]
             held.append(lax.ppermute(mine, "ctx", route))
-        weights.append(held)
+        return held
+
+    weights = []
+    for w in range(waves):
+        mine = weight[w * stretch : (w + 1) * stretch]
+        weights.append(spread(after(mine, weights[-1][-1]) if w else after(mine, opening, packed)))
 
     tokens = []
     for s in range(outer):
@@ -182,10 +186,6 @@
             block = lax.ppermute(block, "ctx", route)
         tokens.append(block)
 
-    prod_halo = arrived[:reach]
-    before = jnp.pad(arrived[reach:].reshape(3, 2, channels).astype(F32), ((0, 0), (TAIL - 2, 0), (0, 0)))
-    behind = ahead(streams[:, :2], "ctx", -1)
-    behind = jnp.pad(behind.astype(F32), ((0, 0), (0, TAIL - 2), (0, 0)))
     by_group = jnp.transpose(filters).astype(F32)
     blank = jnp.zeros((groups, reach), F32)
     backward_rows = jnp.concatenate([by_group, blank], axis=1)
@@ -194,12 +194,17 @@
 
     def forward(wave, *others):
         start = wave * stretch
+        body, past, coming = lax.optimization_barrier((streams, arrived, behind) + others)[:3]
+        prod_halo = past[:reach]
+        before = past[reach:].reshape(3, 2, channels).astype(F32)
+        before = jnp.pad(before, ((0, 0), (TAIL - 2, 0), (0, 0)))
+        coming = jnp.pad(coming.astype(F32), ((0, 0), (0, TAIL - 2), (0, 0)))
         return tiled(
             forward_kernel,
             [
-                (after(streams, *others), False, start),
+                (body, False, start),
                 (before, False, start),
-                (behind, False, start),
+                (coming, False, start),
                 (taps, False, start),
                 (forward_rows, True, start),
                 (prod_halo, False, start),
@@ -213,8 +218,8 @@
             flops // waves,
         )
 
-    def partials(wave, at):
-        joined = jnp.concatenate([h[at * piece : (at + 1) * piece] for h in weights[wave]], axis=1)
+    def partials(wave):
+        joined = jnp.concatenate(weights[wave], axis=1)
         return [
             lax.optimization_barrier(
                 jnp.einsum("tn,cn->tc", block, joined, preferred_element_type=F32).astype(BF16)
@@ -222,42 +227,60 @@
             for block in tokens
         ]
 
+    def hop(block, sign, far, sources):
+        route = [(zz * inner + xx, (zz + sign * far) * inner + xx) for zz in sources for xx in range(inner)]
+        return lax.ppermute(block, "ctx", route)
+
+    def added(one, other):
+        return (one.astype(F32) + other.astype(F32)).astype(BF16)
+
+    def summed(part, sign, previous, held, steps):
+        toward = part if sign == -1 else part[:1] + part[:0:-1]
+        start = (lambda block: block) if previous is None else (lambda block: after(block, previous[sign < 0]))
+        if outer == 4:
+            end = 0 if sign == 1 else outer - 1
+            far = hop(start(toward[3]), sign, 1, [end])
+            near = hop(start(toward[1]), sign, 1, [zz for zz in range(outer) if 0 <= zz + sign < outer])
+            both = added(toward[2], far)
+            if held:
+                both = after(both, *held)
+            steps.append(near)
+            return [near, hop(both, sign, 2, [zz for zz in range(outer) if 0 <= zz + 2 * sign < outer])]
+        got = None
+        for j in range(outer - 1):
+            send = toward[outer - 1 - j]
+            send = start(send) if got is None else added(send, got)
+            if held and j == outer - 2:
+                send = after(send, *held)
+            got = hop(send, sign, 1, range(j + 1) if sign == 1 else range(outer - 1 - j, outer))
+            if j == max(0, outer - 3):
+                steps.append(got)
+        return [got]
+
     results, halos = [], []
     per_wave = chunks // waves
-    middle = [None] * per_wave
-    every = [[partials(wave, at) for at in range(per_wave)] for wave in range(waves)]
+    parts = [partials(wave) for wave in range(waves)]
+    middle = None
     for wave in range(waves):
-        parts = every[wave]
-        conv, mix = forward(wave, *(middle[-1] if wave else parts[-1][1:]))
-        sums = []
-        for at in range(per_wave):
-            total = parts[at][0].astype(F32)
-            steps = []
-            for sign in (1, -1):
-                got = None
-                for j in range(outer - 1):
-                    send = parts[at][j + 1] if sign == 1 else parts[at][outer - 1 - j]
-                    if got is not None:
-                        send = (send.astype(F32) + got.astype(F32)).astype(BF16)
-                        if wave and j == outer - 2:
-                            send = after(send, halos[(wave - 1) * per_wave + at])
-                        if wave + 1 < waves and j == outer - 2:
-                            send = after(send, every[wave + 1][at][1], every[wave + 1][at][outer - 1])
-                    elif wave:
-                        send = after(send, middle[at][sign < 0])
-                    sources = range(j + 1) if sign == 1 else range(outer - 1 - j, outer)
-                    route = [(zz * inner + xx, (zz + sign) * inner + xx) for zz in sources for xx in range(inner)]
-                    got = lax.ppermute(send, "ctx", route)
-                    if j == max(0, outer - 3):
-                        steps.append(got)
+        conv, mix = forward(wave, *(middle or parts[wave][1:]))
+        total = parts[wave][0].astype(F32)
+        held = halos[-per_wave:] if wave else []
+        if wave + 1 < waves:
+            held = held + [parts[wave + 1][1], parts[wave + 1][outer - 1]]
+        steps = []
+        for sign in (1, -1):
+            for got in summed(parts[wave], sign, middle, held, steps):
                 total = total + got.astype(F32)
-            middle[at] = steps
-            sums.append(total.astype(BF16))
+        middle = steps
+        total = total.astype(BF16)
         ready = results[-per_wave:]
         for at in range(per_wave):
             lo = wave * stretch + at * piece
             here = slice(at * piece, (at + 1) * piece)
-            grad_y = after(sums[at], ready[at]) if wave else sums[at]
+            grad_y = total[:, here]
+            grad_y = after(grad_y, ready[at]) if wave else grad_y
+            if at:
+                grad_y = after(grad_y, halos[-1])
             top = grad_y[: reach + 8].astype(F32)
             halo = jnp.concatenate(
                 [

time: 307 us -> 303 us (0.987)
  matrix products: 28 us -> 21 us
  starting transfers between devices: 83.2 us -> 89 us
  waiting for transfers between devices: 112 us -> 107 us
    ppermute x26 -> x14, waiting for transfers between devices: 92.1 us -> 68 us  [the longest x12 46 us: hop(): return lax.ppermute(block, 'ctx', route)]
    ppermute x3, starting transfers between devices: 6.71 us -> 28.5 us  [local(): block = lax.ppermute(block, 'ctx', route)]
    ppermute x1, waiting for transfers between devices: 2.53 us -> 15.3 us  [local(): lax.ppermute(cotangent, 'tp', [(i, (i + s) % tp_count) for i in range(tp_...]
    ppermute x26 -> x14, starting transfers between devices: 60.3 us -> 47.6 us  [the longest x12 44.6 us: hop(): return lax.ppermute(block, 'ctx', route)]
    ppermute x3, waiting for transfers between devices: 0.01 us -> 8.2 us  [local(): block = lax.ppermute(block, 'ctx', route)]
    dot_general x16 -> x8, matrix products: 28 us -> 21 us  [partials(): jnp.einsum('tn,cn->tc', block, joined, preferred_element_type=F32)]
    concatenate x0 -> x2, local copies, waits for them, and re-layouts: none -> 3.81 us  [partials(): joined = jnp.concatenate(weights[wave], axis=1)]
    convert_element_type x16 -> x4, other arithmetic: 14.2 us -> 11.6 us  [the longest x2 5.9 us: local(): total = total.astype(BF16)]
  transfers between devices with their start and end apart: 40 -> 28, of which waited for: 15 -> 10; matrix products, arithmetic and copies ran while one was open for 20% -> 16% of each run, Pallas kernels for 13% -> 13%
where the time goes in v5:
time: 303 us; the launch traced here: 301 us
  waiting for transfers between devices  107 us (35%)
  starting transfers between devices  89 us (29%)
  Pallas kernels  38.9 us (13%)
  other arithmetic  25.9 us (9%)
  matrix products  21 us (7%)
  local copies, waits for them, and re-layouts  18.4 us (6%)
    ppermute x12, waiting for transfers between devices, hop(): return lax.ppermute(block, 'ctx', route)  46 us
    ppermute x12, starting transfers between devices, hop(): return lax.ppermute(block, 'ctx', route)  44.6 us
    pallas_call x6, Pallas kernels, tiled(): pl.pallas_call(functools.partial(kernel, group_width), grid=(channels //...  38.9 us
    ppermute x3, starting transfers between devices, local(): block = lax.ppermute(block, 'ctx', route)  28.5 us
    ppermute x2, waiting for transfers between devices, spread(): held.append(lax.ppermute(mine, 'ctx', route))  22 us
    dot_general x8, matrix products, partials(): jnp.einsum('tn,cn->tc', block, joined, preferred_element_type=F32)  21 us
    ppermute x1, waiting for transfers between devices, local(): lax.ppermute(cotangent, 'tp', [(i, (i + s) % tp_count) for i in range(tp_...  15.3 us
    ppermute x6, waiting for transfers between devices, ahead(): lax.ppermute(block, axis, [(i - distance, i) for i in devices if i - dist...  12.6 us
  transfers between devices with their start and end apart: 28, of which 10 were waited for; matrix products, arithmetic and copies ran while one was open for 16% of the time, Pallas kernels for 13%

profile of v5, /device:TPU:0, one launch (start us, length us, event | category | flops | bytes accessed | tf_op | source)
XLA Modules:
  0.0 301.4 jit_solution(916341404367467434)
XLA Ops:
  1.9 3.0 %slice_convert_fusion = f32[3,130,4096]{2,1,0:T(8,128)S(1)} fusion(bf16[3,256,4096]{2,1,0:T(8,128)(2,1)} %bitcast.74), kind=kLoop, calls=%fused_computation.6 | loop fusion | flops 1597440 | bytes 9584640 | tf_op jit(solution)/shard_map/convert_element_type | solution.py:155
  5.1 2.3 slice_bitcast_fusion.1
  7.5 1.9 fusion
  9.7 1.1 pad_maximum_fusion
  10.8 2.9 collective-permute-start.1
  13.8 1.5 collective-permute-start
  15.3 3.5 %collective-permute-start.12 = (bf16[134,4096]{1,0:T(8,128)(2,1)}, bf16[134,4096]{1,0:T(8,128)(2,1)}, u32[]{:S(2)}, u32[]{:S(2)}) collective-permute-start(bf16[134,4096]{1,0:T(8,128)(2,1)} %pad_maximum_fusion), channel_id=1, source_target_pairs={{0,4},{4,8},{8,12},{12,16},{16,20},{20,24},{24,28},{1,5},{5,9},{9,... | collective-permute-start | bytes 3293192 | tf_op jit(solution)/shard_map/ppermute | solution.py:27
  18.7 1.3 collective-permute-start.13
  20.7 1.9 constant_dynamic-update-slice_fusion.1
  23.0 15.3 %collective-permute-done = bf16[256,2048]{1,0:T(8,128)(2,1)S(1)} collective-permute-done((bf16[256,2048]{1,0:T(8,128)(2,1)S(1)}, bf16[256,2048]{1,0:T(8,128)(2,1)S(1)}, u32[]{:S(2)}, u32[]{:S(2)}) %collective-permute-start) | collective-permute-done | bytes 1048608 | tf_op jit(solution)/shard_map/ppermute | solution.py:149
  38.8 3.7 %collective-permute-start.2 = (bf16[256,1024]{1,0:T(8,128)(2,1)S(1)}, bf16[256,1024]{1,0:T(8,128)(2,1)S(1)}, u32[]{:S(2)}, u32[]{:S(2)}) collective-permute-start(bf16[256,1024]{1,0:T(8,128)(2,1)S(1)} %pad_maximum_fusion.2), channel_id=1, source_target_pairs={{0,24},{4,28},{8,0},{12,4},{16,8},{20,12},{24,16},{28,20},{1,25},{... | collective-permute-start | bytes 1572872 | tf_op jit(solution)/shard_map/ppermute | solution.py:186
  42.7 18.5 %collective-permute-done.1 = bf16[2048,512]{1,0:T(8,128)(2,1)} collective-permute-done((bf16[2048,512]{1,0:T(8,128)(2,1)}, bf16[2048,512]{1,0:T(8,128)(2,1)}, u32[]{:S(2)}, u32[]{:S(2)}) %collective-permute-start.1) | collective-permute-done | bytes 2097184 | tf_op jit(solution)/shard_map/ppermute | solution.py:166
  61.2 24.8 %collective-permute-start.5 = (bf16[256,1024]{1,0:T(8,128)(2,1)S(1)}, bf16[256,1024]{1,0:T(8,128)(2,1)S(1)}, u32[]{:S(2)}, u32[]{:S(2)}) collective-permute-start(bf16[256,1024]{1,0:T(8,128)(2,1)S(1)} %pad_maximum_fusion.4), channel_id=1, source_target_pairs={{0,8},{4,12},{8,16},{12,20},{16,24},{20,28},{24,0},{28,4},{1,9},{5... | collective-permute-start | bytes 1572872 | tf_op jit(solution)/shard_map/ppermute | solution.py:186
  85.9 1.9 constant_dynamic-update-slice_fusion
  87.9 2.3 convolution_convert_fusion.6
  90.3 8.2 %collective-permute-done.5 = bf16[256,1024]{1,0:T(8,128)(2,1)S(1)} collective-permute-done((bf16[256,1024]{1,0:T(8,128)(2,1)S(1)}, bf16[256,1024]{1,0:T(8,128)(2,1)S(1)}, u32[]{:S(2)}, u32[]{:S(2)}) %collective-permute-start.5) | collective-permute-done | bytes 524320 | tf_op jit(solution)/shard_map/ppermute | solution.py:186
  98.5 2.3 convolution_convert_fusion.4
  100.8 2.6 collective-permute-start.6
  103.4 1.6 collective-permute-start.10
  105.0 2.3 convolution_convert_fusion.5
  107.3 2.3 convolution_convert_fusion.7
  109.5 1.5 constant_dynamic-update-slice_fusion.3
  111.0 2.3 collective-permute-start.3
  113.3 1.5 collective-permute-start.9
  115.6 2.3 slice.147.halo_ref
  118.0 8.3 %collective-permute-done.6 = bf16[256,2048]{1,0:T(8,128)(2,1)} collective-permute-done((bf16[256,2048]{1,0:T(8,128)(2,1)}, bf16[256,2048]{1,0:T(8,128)(2,1)}, u32[]{:S(2)}, u32[]{:S(2)}) %collective-permute-start.6) | collective-permute-done | bytes 1048608 | tf_op jit(solution)/shard_map/ppermute | solution.py:232
  126.3 3.9 %fusion.2 = (bf16[256,2048]{1,0:T(8,128)(2,1)}, bf16[256,2048]{1,0:T(8,128)(2,1)}) fusion(bf16[256,2048]{1,0:T(8,128)(2,1)} %convolution_convert_fusion.5, bf16[256,2048]{1,0:T(8,128)(2,1)} %collective-permute-done.6, bf16[256,2048]{1,0:T(8,128)(2,1)} %collective-permute-done.10), kind=kLoop, calls=%fused_computation.19 | loop fusion | flops 3670016 | bytes 5242880 | tf_op jit(solution)/shard_map/convert_element_type | solution.py:235
  130.2 3.5 %collective-permute-done.7 = bf16[2048,512]{1,0:T(8,128)(2,1)} collective-permute-done((bf16[2048,512]{1,0:T(8,128)(2,1)S(1)}, bf16[2048,512]{1,0:T(8,128)(2,1)}, u32[]{:S(2)}, u32[]{:S(2)}) %collective-permute-start.7) | collective-permute-done | bytes 2097184 | tf_op jit(solution)/shard_map/ppermute | solution.py:166
  133.7 1.9 constant_dynamic-update-slice_fusion.2
  135.7 2.4 convolution_convert_fusion.3
  138.1 2.3 convolution_convert_fusion.2
  140.3 1.3 collective-permute-start.11
  141.6 7.4 %collective-permute-start.8 = (bf16[256,2048]{1,0:T(8,128)(2,1)}, bf16[256,2048]{1,0:T(8,128)(2,1)}, u32[]{:S(2)}, u32[]{:S(2)}) collective-permute-start(bf16[256,2048]{1,0:T(8,128)(2,1)} %get-tuple-element.31), channel_id=1, source_target_pairs={{0,16},{4,20},{8,24},{12,28},{1,17},{5,21},{9,25},{13,29},{2,18},{... | collective-permute-start | bytes 3145736 | tf_op jit(solution)/shard_map/ppermute | solution.py:232
  149.0 8.9 %shard_map.55 = (f32[256,2048]{1,0:T(8,128)S(1)}, f32[3,264,2048]{2,1,0:T(8,128)}) custom-call(bf16[3,256,4096]{2,1,0:T(8,128)(2,1)} %bitcast.75, f32[3,8,4096]{2,1,0:T(8,128)S(1)} %pad_convert_fusion.3.before_ref, f32[3,8,4096]{2,1,0:T(8,128)S(1)} %pad_convert_fusion.2.after_ref, f32[3,3,4096]{2,1,0:T(4,128)S(1)} %bitcast.66, ...), custom_call_target="tpu_custom_call" | custom-call | flops 2147483648 | bytes 17121280 | tf_op jit(solution)/shard_map/pallas_call | solution.py:113
  158.9 3.8 %convolution_convert_fusion = bf16[256,2048]{1,0:T(8,128)(2,1)S(1)} fusion(bf16[256,1024]{1,0:T(8,128)(2,1)} %copy-done.10, bf16[2048,1024]{1,0:T(8,128)(2,1)} %copy-done.5), kind=kOutput, calls=%fused_computation.11 | convolution fusion | flops 1074266112 | bytes 5767168 | tf_op jit(solution)/shard_map/tn,cn->tc/dot_general | solution.py:225
  162.7 3.5 %collective-permute-start.19 = (bf16[256,2048]{1,0:T(8,128)(2,1)S(1)}, bf16[256,2048]{1,0:T(8,128)(2,1)S(1)}, u32[]{:S(2)}, u32[]{:S(2)}) collective-permute-start(bf16[256,2048]{1,0:T(8,128)(2,1)S(1)} %copy-done.9), channel_id=1, source_target_pairs={{0,8},{4,12},{1,9},{5,13},{2,10},{6,14},{3,11},{7,15}} | collective-permute-start | bytes 3145736 | tf_op jit(solution)/shard_map/ppermute | solution.py:232
  167.0 1.3 collective-permute-start.21
  168.3 23.5 %collective-permute-done.11 = bf16[256,2048]{1,0:T(8,128)(2,1)} collective-permute-done((bf16[256,2048]{1,0:T(8,128)(2,1)}, bf16[256,2048]{1,0:T(8,128)(2,1)}, u32[]{:S(2)}, u32[]{:S(2)}) %collective-permute-start.11) | collective-permute-done | bytes 1048608 | tf_op jit(solution)/shard_map/ppermute | solution.py:232
  191.8 2.3 collective-permute-start.18
  194.1 3.1 %add_convert_fusion.1 = bf16[256,2048]{1,0:T(8,128)(2,1)S(1)} fusion(bf16[256,2048]{1,0:T(8,128)(2,1)} %collective-permute-done.11, bf16[256,2048]{1,0:T(8,128)(2,1)} %collective-permute-done.9, bf16[256,2048]{1,0:T(8,128)(2,1)} %collective-permute-done.8, bf16[256,2048]{1,0:T(8,128)(2,1)} %collective-permute-done.3, bf16[256,2048]{1,0:T(8,128)(2,1)S(1)} %copy-done.6), kind=kLoop, calls=%fused_computation.26 | loop fusion | flops 5242880 | bytes 6291456 | tf_op jit(solution)/shard_map/convert_element_type | solution.py:275
  197.4 1.1 fusion.11
  198.5 1.3 collective-permute-start.14
  200.0 1.1 fusion.10
  201.1 1.3 collective-permute-start.16
  202.4 1.7 fusion.4
  204.2 1.3 collective-permute-start.23
  205.5 4.9 %collective-permute-done.16.halo_ref = bf16[144,1024]{1,0:T(8,128)(2,1)S(1)} collective-permute-done((bf16[144,1024]{1,0:T(8,128)(2,1)S(1)}, bf16[144,1024]{1,0:T(8,128)(2,1)S(1)}, u32[]{:S(2)}, u32[]{:S(2)}) %collective-permute-start.16) | collective-permute-done | bytes 294944 | tf_op jit(solution)/shard_map/ppermute | solution.py:27
  210.4 18.8 %collective-permute-start.20 = (bf16[256,2048]{1,0:T(8,128)(2,1)S(1)}, bf16[256,2048]{1,0:T(8,128)(2,1)}, u32[]{:S(2)}, u32[]{:S(2)}) collective-permute-start(bf16[256,2048]{1,0:T(8,128)(2,1)S(1)} %get-tuple-element.41), channel_id=1, source_target_pairs={{0,16},{4,20},{8,24},{12,28},{1,17},{5,21},{9,25},{13,29},{2,18},{... | collective-permute-start | bytes 3145736 | tf_op jit(solution)/shard_map/ppermute | solution.py:232
  229.2 5.3 %shard_map.57 = bf16[3,256,1024]{2,1,0:T(8,128)(2,1)S(1)} custom-call(bf16[256,1024]{1,0:T(8,128)(2,1)S(1)} %get-tuple-element.38.grad_ref, bf16[144,1024]{1,0:T(8,128)(2,1)S(1)} %collective-permute-done.16.halo_ref, f32[256,2048]{1,0:T(8,128)S(1)} %get-tuple-element.37.conv_ref, f32[3,264,2048]{2,1,0:T(8,128)} %get-tuple-element.36.mix_ref, ...), custom_call_target="tpu_custom_call" | custom-call | flops 1073741824 | bytes 12959744 | tf_op jit(solution)/shard_map/pallas_call | solution.py:113
  234.5 5.3 %shard_map.56 = bf16[3,256,1024]{2,1,0:T(8,128)(2,1)S(1)} custom-call(bf16[256,1024]{1,0:T(8,128)(2,1)S(1)} %get-tuple-element.66.grad_ref, bf16[144,1024]{1,0:T(8,128)(2,1)S(1)} %collective-permute-done.14.halo_ref, f32[256,2048]{1,0:T(8,128)S(1)} %get-tuple-element.37.conv_ref, f32[3,264,2048]{2,1,0:T(8,128)} %get-tuple-element.36.mix_ref, ...), custom_call_target="tpu_custom_call" | custom-call | flops 1073741824 | bytes 12959744 | tf_op jit(solution)/shard_map/pallas_call | solution.py:113
  240.4 1.3 slice.159.halo_ref
  241.7 8.9 %shard_map.58 = (f32[256,2048]{1,0:T(8,128)S(1)}, f32[3,264,2048]{2,1,0:T(8,128)}) custom-call(bf16[3,256,4096]{2,1,0:T(8,128)(2,1)} %bitcast.76, f32[3,8,4096]{2,1,0:T(8,128)S(1)} %pad_convert_fusion.1.before_ref, f32[3,8,4096]{2,1,0:T(8,128)S(1)} %pad_convert_fusion.after_ref, f32[3,3,4096]{2,1,0:T(4,128)S(1)} %bitcast.69, ...), custom_call_target="tpu_custom_call" | custom-call | flops 2147483648 | bytes 17121280 | tf_op jit(solution)/shard_map/pallas_call | solution.py:113
  250.6 3.5 %convolution_convert_fusion.1 = bf16[256,2048]{1,0:T(8,128)(2,1)S(1)} fusion(bf16[2048,1024]{1,0:T(8,128)(2,1)} %copy-done.5, bf16[256,512]{1,0:T(8,128)(2,1)S(1)} %get-tuple-element.65, bf16[256,512]{1,0:T(8,128)(2,1)S(1)} %get-tuple-element.58), kind=kOutput, calls=%fused_computation.12 | convolution fusion | flops 1075314688 | bytes 5767168 | tf_op jit(solution)/shard_map/tn,cn->tc/dot_general | solution.py:225
  254.1 14.2 %collective-permute-done.23 = bf16[256,2048]{1,0:T(8,128)(2,1)} collective-permute-done((bf16[256,2048]{1,0:T(8,128)(2,1)}, bf16[256,2048]{1,0:T(8,128)(2,1)}, u32[]{:S(2)}, u32[]{:S(2)}) %collective-permute-start.23) | collective-permute-done | bytes 1048608 | tf_op jit(solution)/shard_map/ppermute | solution.py:232
  268.3 2.8 add_convert_fusion
  271.2 1.1 fusion.9
  272.4 1.1 fusion.8
  273.6 1.3 collective-permute-start.26
  274.9 1.6 collective-permute-start.24
  276.5 7.7 %collective-permute-done.26.halo_ref = bf16[144,1024]{1,0:T(8,128)(2,1)S(1)} collective-permute-done((bf16[144,1024]{1,0:T(8,128)(2,1)S(1)}, bf16[144,1024]{1,0:T(8,128)(2,1)S(1)}, u32[]{:S(2)}, u32[]{:S(2)}) %collective-permute-start.26) | collective-permute-done | bytes 294944 | tf_op jit(solution)/shard_map/ppermute | solution.py:27
  284.1 5.3 %shard_map.60 = bf16[3,256,1024]{2,1,0:T(8,128)(2,1)S(1)} custom-call(bf16[256,1024]{1,0:T(8,128)(2,1)S(1)} %get-tuple-element.52.grad_ref, bf16[144,1024]{1,0:T(8,128)(2,1)S(1)} %collective-permute-done.26.halo_ref, f32[256,2048]{1,0:T(8,128)S(1)} %get-tuple-element.50.conv_ref, f32[3,264,2048]{2,1,0:T(8,128)} %get-tuple-element.49.mix_ref, ...), custom_call_target="tpu_custom_call" | custom-call | flops 1073741824 | bytes 12959744 | tf_op jit(solution)/shard_map/pallas_call | solution.py:113
  289.5 5.3 %shard_map.59 = bf16[3,256,1024]{2,1,0:T(8,128)(2,1)S(1)} custom-call(bf16[256,1024]{1,0:T(8,128)(2,1)S(1)} %get-tuple-element.45.grad_ref, bf16[144,1024]{1,0:T(8,128)(2,1)S(1)} %collective-permute-done.24.halo_ref, f32[256,2048]{1,0:T(8,128)S(1)} %get-tuple-element.50.conv_ref, f32[3,264,2048]{2,1,0:T(8,128)} %get-tuple-element.49.mix_ref, ...), custom_call_target="tpu_custom_call" | custom-call | flops 1073741824 | bytes 12959744 | tf_op jit(solution)/shard_map/pallas_call | solution.py:113
  295.3 3.0 %collective-permute-done.25 = bf16[3,256,1024]{2,1,0:T(8,128)(2,1)S(1)} collective-permute-done((bf16[3,256,1024]{2,1,0:T(8,128)(2,1)S(1)}, bf16[3,256,1024]{2,1,0:T(8,128)(2,1)S(1)}, u32[]{:S(2)}, u32[]{:S(2)}) %collective-permute-start.25) | collective-permute-done | bytes 1572896 | tf_op jit(solution)/shard_map/ppermute | solution.py:310
  298.4 3.0 maximum_bitcast_fusion
  (96 shorter events, 8.4 us)
Async XLA Ops:
  1.9 3.2 %copy-start.2 = (bf16[1,4096,512]{2,1,0:T(8,128)(2,1)S(1)}, bf16[1,4096,512]{2,1,0:T(8,128)(2,1)}, u32[]{:S(2)}) copy-start(bf16[1,4096,512]{2,1,0:T(8,128)(2,1)} %param.8) | copy-start | bytes 12582916
  5.1 2.3 copy-start.7
  9.4 4.3 %copy-start.3 = (bf16[1,256,2048]{2,1,0:T(8,128)(2,1)S(1)}, bf16[1,256,2048]{2,1,0:T(8,128)(2,1)}, u32[]{:S(2)}) copy-start(bf16[1,256,2048]{2,1,0:T(8,128)(2,1)} %param.9) | copy-start | bytes 3145732
  9.7 10.6 %copy-start.8 = (bf16[1,128,256]{2,1,0:T(8,128)(2,1)S(1)}, bf16[1,128,256]{2,1,0:T(8,128)(2,1)}, u32[]{:S(2)}) copy-start(bf16[1,128,256]{2,1,0:T(8,128)(2,1)} %param.7) | copy-start | bytes 196612
  10.8 50.3 %collective-permute-start.1 = (bf16[2048,512]{1,0:T(8,128)(2,1)}, bf16[2048,512]{1,0:T(8,128)(2,1)}, u32[]{:S(2)}, u32[]{:S(2)}) collective-permute-start(bf16[2048,512]{1,0:T(8,128)(2,1)} %get-tuple-element.29), channel_id=1, source_target_pairs={{0,4},{4,0},{8,12},{12,8},{16,20},{20,16},{24,28},{28,24},{1,5},{5... | collective-permute-start | bytes 6291464 | tf_op jit(solution)/shard_map/ppermute | solution.py:166
  13.8 24.6 %collective-permute-start = (bf16[256,2048]{1,0:T(8,128)(2,1)S(1)}, bf16[256,2048]{1,0:T(8,128)(2,1)S(1)}, u32[]{:S(2)}, u32[]{:S(2)}) collective-permute-start(bf16[256,2048]{1,0:T(8,128)(2,1)S(1)} %bitcast.77), channel_id=1, source_target_pairs={{0,2},{2,0},{1,3},{3,1},{4,6},{6,4},{5,7},{7,5},{8,10},{10,8},{9,1... | collective-permute-start | bytes 3145736 | tf_op jit(solution)/shard_map/ppermute | solution.py:149
  15.3 98.0 %collective-permute-start.12 = (bf16[134,4096]{1,0:T(8,128)(2,1)}, bf16[134,4096]{1,0:T(8,128)(2,1)}, u32[]{:S(2)}, u32[]{:S(2)}) collective-permute-start(bf16[134,4096]{1,0:T(8,128)(2,1)} %pad_maximum_fusion), channel_id=1, source_target_pairs={{0,4},{4,8},{8,12},{12,16},{16,20},{20,24},{24,28},{1,5},{5,9},{9,... | collective-permute-start | bytes 3293192 | tf_op jit(solution)/shard_map/ppermute | solution.py:27
  18.7 92.3 %collective-permute-start.13 = (bf16[3,2,4096]{2,1,0:T(2,128)(2,1)S(1)}, bf16[3,2,4096]{2,1,0:T(2,128)(2,1)S(1)}, u32[]{:S(2)}, u32[]{:S(2)}) collective-permute-start(bf16[3,2,4096]{2,1,0:T(2,128)(2,1)S(1)} %slice.168), channel_id=1, source_target_pairs={{4,0},{8,4},{12,8},{16,12},{20,16},{24,20},{28,24},{5,1},{9,5},{13... | collective-permute-start | bytes 147464 | tf_op jit(solution)/shard_map/ppermute | solution.py:27
  38.8 49.0 %collective-permute-start.2 = (bf16[256,1024]{1,0:T(8,128)(2,1)S(1)}, bf16[256,1024]{1,0:T(8,128)(2,1)S(1)}, u32[]{:S(2)}, u32[]{:S(2)}) collective-permute-start(bf16[256,1024]{1,0:T(8,128)(2,1)S(1)} %pad_maximum_fusion.2), channel_id=1, source_target_pairs={{0,24},{4,28},{8,0},{12,4},{16,8},{20,12},{24,16},{28,20},{1,25},{... | collective-permute-start | bytes 1572872 | tf_op jit(solution)/shard_map/ppermute | solution.py:186
  42.5 60.8 %collective-permute-start.4 = (bf16[256,1024]{1,0:T(8,128)(2,1)S(1)}, bf16[256,1024]{1,0:T(8,128)(2,1)S(1)}, u32[]{:S(2)}, u32[]{:S(2)}) collective-permute-start(bf16[256,1024]{1,0:T(8,128)(2,1)S(1)} %pad_maximum_fusion.3), channel_id=1, source_target_pairs={{0,16},{4,20},{8,24},{12,28},{16,0},{20,4},{24,8},{28,12},{1,17},{... | collective-permute-start | bytes 1572872 | tf_op jit(solution)/shard_map/ppermute | solution.py:186
  42.7 45.2 %copy-start.1 = (bf16[2048,512]{1,0:T(8,128)(2,1)S(1)}, bf16[2048,512]{1,0:T(8,128)(2,1)}, u32[]{:S(2)}) copy-start(bf16[2048,512]{1,0:T(8,128)(2,1)} %get-tuple-element.30) | copy-start | bytes 6291460
  61.2 37.3 %collective-permute-start.5 = (bf16[256,1024]{1,0:T(8,128)(2,1)S(1)}, bf16[256,1024]{1,0:T(8,128)(2,1)S(1)}, u32[]{:S(2)}, u32[]{:S(2)}) collective-permute-start(bf16[256,1024]{1,0:T(8,128)(2,1)S(1)} %pad_maximum_fusion.4), channel_id=1, source_target_pairs={{0,8},{4,12},{8,16},{12,20},{16,24},{20,28},{24,0},{28,4},{1,9},{5... | collective-permute-start | bytes 1572872 | tf_op jit(solution)/shard_map/ppermute | solution.py:186
  87.9 2.4 copy-start.11
  87.9 45.9 %collective-permute-start.7 = (bf16[2048,512]{1,0:T(8,128)(2,1)S(1)}, bf16[2048,512]{1,0:T(8,128)(2,1)}, u32[]{:S(2)}, u32[]{:S(2)}) collective-permute-start(bf16[2048,512]{1,0:T(8,128)(2,1)S(1)} %copy-done.1), channel_id=1, source_target_pairs={{0,4},{4,0},{8,12},{12,8},{16,20},{20,16},{24,28},{28,24},{1,5},{5... | collective-permute-start | bytes 6291464 | tf_op jit(solution)/shard_map/ppermute | solution.py:166
  98.5 2.3 copy-start.13
  100.8 25.5 %collective-permute-start.6 = (bf16[256,2048]{1,0:T(8,128)(2,1)}, bf16[256,2048]{1,0:T(8,128)(2,1)}, u32[]{:S(2)}, u32[]{:S(2)}) collective-permute-start(bf16[256,2048]{1,0:T(8,128)(2,1)} %convolution_convert_fusion.4), channel_id=1, source_target_pairs={{0,8},{4,12},{1,9},{5,13},{2,10},{6,14},{3,11},{7,15}} | collective-permute-start | bytes 3145736 | tf_op jit(solution)/shard_map/ppermute | solution.py:232
  103.4 6.2 %copy-start.10 = (bf16[256,1024]{1,0:T(8,128)(2,1)}, bf16[256,1024]{1,0:T(8,128)(2,1)S(1)}, u32[]{:S(2)}) copy-start(bf16[256,1024]{1,0:T(8,128)(2,1)S(1)} %collective-permute-done.4) | copy-start | bytes 1572868
  103.4 22.9 %collective-permute-start.10 = (bf16[256,2048]{1,0:T(8,128)(2,1)}, bf16[256,2048]{1,0:T(8,128)(2,1)}, u32[]{:S(2)}, u32[]{:S(2)}) collective-permute-start(bf16[256,2048]{1,0:T(8,128)(2,1)} %convolution_convert_fusion.6), channel_id=1, source_target_pairs={{24,16},{28,20},{25,17},{29,21},{26,18},{30,22},{27,19},{31,23}} | collective-permute-start | bytes 3145736 | tf_op jit(solution)/shard_map/ppermute | solution.py:232
  111.0 46.9 %collective-permute-start.3 = (bf16[256,2048]{1,0:T(8,128)(2,1)}, bf16[256,2048]{1,0:T(8,128)(2,1)}, u32[]{:S(2)}, u32[]{:S(2)}) collective-permute-start(bf16[256,2048]{1,0:T(8,128)(2,1)} %convolution_convert_fusion.6), channel_id=1, source_target_pairs={{0,8},{4,12},{8,16},{12,20},{16,24},{20,28},{1,9},{5,13},{9,17},{1... | collective-permute-start | bytes 3145736 | tf_op jit(solution)/shard_map/ppermute | solution.py:232
  113.3 44.7 %collective-permute-start.9 = (bf16[256,2048]{1,0:T(8,128)(2,1)}, bf16[256,2048]{1,0:T(8,128)(2,1)}, u32[]{:S(2)}, u32[]{:S(2)}) collective-permute-start(bf16[256,2048]{1,0:T(8,128)(2,1)} %convolution_convert_fusion.4), channel_id=1, source_target_pairs={{8,0},{12,4},{16,8},{20,12},{24,16},{28,20},{9,1},{13,5},{17,9},{2... | collective-permute-start | bytes 3145736 | tf_op jit(solution)/shard_map/ppermute | solution.py:232
  118.0 15.7 %copy-start.4 = (bf16[2048,1024]{1,0:T(8,128)(2,1)S(1)}, bf16[2048,1024]{1,0:T(8,128)(2,1)}, u32[]{:S(2)}) copy-start(bf16[2048,1024]{1,0:T(8,128)(2,1)} %constant_dynamic-update-slice_fusion.3) | copy-start | bytes 12582916
  130.2 5.4 %copy-start.14 = (bf16[256,1024]{1,0:T(8,128)(2,1)S(1)}, bf16[256,1024]{1,0:T(8,128)(2,1)}, u32[]{:S(2)}) copy-start(bf16[256,1024]{1,0:T(8,128)(2,1)} %copy-done.13) | copy-start | bytes 1572868
  135.7 4.7 %copy-start.5 = (bf16[2048,1024]{1,0:T(8,128)(2,1)}, bf16[2048,1024]{1,0:T(8,128)(2,1)S(1)}, u32[]{:S(2)}) copy-start(bf16[2048,1024]{1,0:T(8,128)(2,1)S(1)} %constant_dynamic-update-slice_fusion.2) | copy-start | bytes 12582916
  135.7 2.4 copy-start.12
  138.1 11.0 %copy-start = (bf16[128,4096]{1,0:T(8,128)(2,1)S(1)}, bf16[128,4096]{1,0:T(8,128)(2,1)}, u32[]{:S(2)}) copy-start(bf16[128,4096]{1,0:T(8,128)(2,1)} %slice.147.halo_ref) | copy-start | bytes 3145732
  140.3 51.5 %collective-permute-start.11 = (bf16[256,2048]{1,0:T(8,128)(2,1)}, bf16[256,2048]{1,0:T(8,128)(2,1)}, u32[]{:S(2)}, u32[]{:S(2)}) collective-permute-start(bf16[256,2048]{1,0:T(8,128)(2,1)} %get-tuple-element.32), channel_id=1, source_target_pairs={{16,0},{20,4},{24,8},{28,12},{17,1},{21,5},{25,9},{29,13},{18,2},{... | collective-permute-start | bytes 3145736 | tf_op jit(solution)/shard_map/ppermute | solution.py:232
  141.6 52.5 %collective-permute-start.8 = (bf16[256,2048]{1,0:T(8,128)(2,1)}, bf16[256,2048]{1,0:T(8,128)(2,1)}, u32[]{:S(2)}, u32[]{:S(2)}) collective-permute-start(bf16[256,2048]{1,0:T(8,128)(2,1)} %get-tuple-element.31), channel_id=1, source_target_pairs={{0,16},{4,20},{8,24},{12,28},{1,17},{5,21},{9,25},{13,29},{2,18},{... | collective-permute-start | bytes 3145736 | tf_op jit(solution)/shard_map/ppermute | solution.py:232
  158.9 3.8 %copy-start.9 = (bf16[256,2048]{1,0:T(8,128)(2,1)S(1)}, bf16[256,2048]{1,0:T(8,128)(2,1)}, u32[]{:S(2)}) copy-start(bf16[256,2048]{1,0:T(8,128)(2,1)} %convolution_convert_fusion.3) | copy-start | bytes 3145732
  158.9 35.3 %copy-start.6 = (bf16[256,2048]{1,0:T(8,128)(2,1)S(1)}, bf16[256,2048]{1,0:T(8,128)(2,1)}, u32[]{:S(2)}) copy-start(bf16[256,2048]{1,0:T(8,128)(2,1)} %convolution_convert_fusion.7) | copy-start | bytes 3145732
  162.7 38.4 %collective-permute-start.19 = (bf16[256,2048]{1,0:T(8,128)(2,1)S(1)}, bf16[256,2048]{1,0:T(8,128)(2,1)S(1)}, u32[]{:S(2)}, u32[]{:S(2)}) collective-permute-start(bf16[256,2048]{1,0:T(8,128)(2,1)S(1)} %copy-done.9), channel_id=1, source_target_pairs={{0,8},{4,12},{1,9},{5,13},{2,10},{6,14},{3,11},{7,15}} | collective-permute-start | bytes 3145736 | tf_op jit(solution)/shard_map/ppermute | solution.py:232
  166.2 36.2 %collective-permute-start.22 = (bf16[256,2048]{1,0:T(8,128)(2,1)}, bf16[256,2048]{1,0:T(8,128)(2,1)S(1)}, u32[]{:S(2)}, u32[]{:S(2)}) collective-permute-start(bf16[256,2048]{1,0:T(8,128)(2,1)} %convolution_convert_fusion.2), channel_id=1, source_target_pairs={{24,16},{28,20},{25,17},{29,21},{26,18},{30,22},{27,19},{31,23}} | collective-permute-start | bytes 3145736 | tf_op jit(solution)/shard_map/ppermute | solution.py:232
  167.0 72.8 %collective-permute-start.21 = (bf16[256,2048]{1,0:T(8,128)(2,1)S(1)}, bf16[256,2048]{1,0:T(8,128)(2,1)S(1)}, u32[]{:S(2)}, u32[]{:S(2)}) collective-permute-start(bf16[256,2048]{1,0:T(8,128)(2,1)S(1)} %copy-done.9), channel_id=1, source_target_pairs={{8,0},{12,4},{16,8},{20,12},{24,16},{28,20},{9,1},{13,5},{17,9},{2... | collective-permute-start | bytes 3145736 | tf_op jit(solution)/shard_map/ppermute | solution.py:232
  191.8 62.3 %collective-permute-start.18 = (bf16[256,2048]{1,0:T(8,128)(2,1)}, bf16[256,2048]{1,0:T(8,128)(2,1)}, u32[]{:S(2)}, u32[]{:S(2)}) collective-permute-start(bf16[256,2048]{1,0:T(8,128)(2,1)} %convolution_convert_fusion.2), channel_id=1, source_target_pairs={{0,8},{4,12},{8,16},{12,20},{16,24},{20,28},{1,9},{5,13},{9,17},{1... | collective-permute-start | bytes 3145736 | tf_op jit(solution)/shard_map/ppermute | solution.py:232
  198.5 35.9 %collective-permute-start.14 = (bf16[144,1024]{1,0:T(8,128)(2,1)S(1)}, bf16[144,1024]{1,0:T(8,128)(2,1)S(1)}, u32[]{:S(2)}, u32[]{:S(2)}) collective-permute-start(bf16[144,1024]{1,0:T(8,128)(2,1)S(1)} %pad_maximum_fusion.7), channel_id=1, source_target_pairs={{4,0},{8,4},{12,8},{16,12},{20,16},{24,20},{28,24},{5,1},{9,5},{13... | collective-permute-start | bytes 884744 | tf_op jit(solution)/shard_map/ppermute | solution.py:27
  201.1 9.2 %collective-permute-start.16 = (bf16[144,1024]{1,0:T(8,128)(2,1)S(1)}, bf16[144,1024]{1,0:T(8,128)(2,1)S(1)}, u32[]{:S(2)}, u32[]{:S(2)}) collective-permute-start(bf16[144,1024]{1,0:T(8,128)(2,1)S(1)} %pad_maximum_fusion.8), channel_id=1, source_target_pairs={{4,0},{8,4},{12,8},{16,12},{20,16},{24,20},{28,24},{5,1},{9,5},{13... | collective-permute-start | bytes 884744 | tf_op jit(solution)/shard_map/ppermute | solution.py:27
  204.2 64.1 %collective-permute-start.23 = (bf16[256,2048]{1,0:T(8,128)(2,1)}, bf16[256,2048]{1,0:T(8,128)(2,1)}, u32[]{:S(2)}, u32[]{:S(2)}) collective-permute-start(bf16[256,2048]{1,0:T(8,128)(2,1)} %get-tuple-element.44), channel_id=1, source_target_pairs={{16,0},{20,4},{24,8},{28,12},{17,1},{21,5},{25,9},{29,13},{18,2},{... | collective-permute-start | bytes 3145736 | tf_op jit(solution)/shard_map/ppermute | solution.py:232
  210.4 57.9 %collective-permute-start.20 = (bf16[256,2048]{1,0:T(8,128)(2,1)S(1)}, bf16[256,2048]{1,0:T(8,128)(2,1)}, u32[]{:S(2)}, u32[]{:S(2)}) collective-permute-start(bf16[256,2048]{1,0:T(8,128)(2,1)S(1)} %get-tuple-element.41), channel_id=1, source_target_pairs={{0,16},{4,20},{8,24},{12,28},{1,17},{5,21},{9,25},{13,29},{2,18},{... | collective-permute-start | bytes 3145736 | tf_op jit(solution)/shard_map/ppermute | solution.py:232
  234.4 36.7 %collective-permute-start.17 = (bf16[3,256,1024]{2,1,0:T(8,128)(2,1)S(1)}, bf16[3,256,1024]{2,1,0:T(8,128)(2,1)S(1)}, u32[]{:S(2)}, u32[]{:S(2)}) collective-permute-start(bf16[3,256,1024]{2,1,0:T(8,128)(2,1)S(1)} %shard_map.57), channel_id=1, source_target_pairs={{0,1},{1,0},{2,3},{3,2},{4,5},{5,4},{6,7},{7,6},{8,9},{9,8},{10,11... | collective-permute-start | bytes 4718600 | tf_op jit(solution)/shard_map/ppermute | solution.py:310
  239.8 31.4 %collective-permute-start.15 = (bf16[3,256,1024]{2,1,0:T(8,128)(2,1)S(1)}, bf16[3,256,1024]{2,1,0:T(8,128)(2,1)S(1)}, u32[]{:S(2)}, u32[]{:S(2)}) collective-permute-start(bf16[3,256,1024]{2,1,0:T(8,128)(2,1)S(1)} %shard_map.56), channel_id=1, source_target_pairs={{0,1},{1,0},{2,3},{3,2},{4,5},{5,4},{6,7},{7,6},{8,9},{9,8},{10,11... | collective-permute-start | bytes 4718600 | tf_op jit(solution)/shard_map/ppermute | solution.py:310
  273.6 10.5 %collective-permute-start.26 = (bf16[144,1024]{1,0:T(8,128)(2,1)S(1)}, bf16[144,1024]{1,0:T(8,128)(2,1)S(1)}, u32[]{:S(2)}, u32[]{:S(2)}) collective-permute-start(bf16[144,1024]{1,0:T(8,128)(2,1)S(1)} %pad_maximum_fusion.10), channel_id=1, source_target_pairs={{4,0},{8,4},{12,8},{16,12},{20,16},{24,20},{28,24},{5,1},{9,5},{13... | collective-permute-start | bytes 884744 | tf_op jit(solution)/shard_map/ppermute | solution.py:27
  274.9 14.6 %collective-permute-start.24 = (bf16[144,1024]{1,0:T(8,128)(2,1)S(1)}, bf16[144,1024]{1,0:T(8,128)(2,1)S(1)}, u32[]{:S(2)}, u32[]{:S(2)}) collective-permute-start(bf16[144,1024]{1,0:T(8,128)(2,1)S(1)} %pad_maximum_fusion.9), channel_id=1, source_target_pairs={{4,0},{8,4},{12,8},{16,12},{20,16},{24,20},{28,24},{5,1},{9,5},{13... | collective-permute-start | bytes 884744 | tf_op jit(solution)/shard_map/ppermute | solution.py:27
  289.4 5.9 %collective-permute-start.27 = (bf16[3,256,1024]{2,1,0:T(8,128)(2,1)S(1)}, bf16[3,256,1024]{2,1,0:T(8,128)(2,1)S(1)}, u32[]{:S(2)}, u32[]{:S(2)}) collective-permute-start(bf16[3,256,1024]{2,1,0:T(8,128)(2,1)S(1)} %shard_map.60), channel_id=1, source_target_pairs={{0,1},{1,0},{2,3},{3,2},{4,5},{5,4},{6,7},{7,6},{8,9},{9,8},{10,11... | collective-permute-start | bytes 4718600 | tf_op jit(solution)/shard_map/ppermute | solution.py:310
  294.8 3.6 %collective-permute-start.25 = (bf16[3,256,1024]{2,1,0:T(8,128)(2,1)S(1)}, bf16[3,256,1024]{2,1,0:T(8,128)(2,1)S(1)}, u32[]{:S(2)}, u32[]{:S(2)}) collective-permute-start(bf16[3,256,1024]{2,1,0:T(8,128)(2,1)S(1)} %shard_map.59), channel_id=1, source_target_pairs={{0,1},{1,0},{2,3},{3,2},{4,5},{5,4},{6,7},{7,6},{8,9},{9,8},{10,11... | collective-permute-start | bytes 4718600 | tf_op jit(solution)/shard_map/ppermute | solution.py:310
